TPU v7x, 32 devices: a whole 2x2x4 slice. The times are simulated.
32 devices in a mesh: pp: 4 (over y, core), node: 2 (over x), local: 4 (over z).
Axes of the slice: x: 2, y: 2, z: 4, core: 2. Of those that a mesh axis runs over, the one named last changes fastest.
Arguments:
- act_fwd: bfloat16 [4, 1024, 4096], P('pp', ('node', 'local')), may hold values from -6 to 6
- routes_fwd: int32 [4, 1024, 1], P('pp', ('node', 'local')), may hold values from 0 to 1; in each aligned block of 128 rows (0 to 127, 128 to 255, ..., all dimensions but the last counted through in order) at most 80 rows name the same one
- weight_fwd: float32 [4, 1024], P('pp', ('node', 'local')), may hold values from 0.25 to 1
- grad_bwd: bfloat16 [4, 1024, 4096], P('pp', ('node', 'local')), may hold values from -6 to 6
- routes_bwd: int32 [4, 1024, 1], P('pp', ('node', 'local')), may hold values from 0 to 1; in each aligned block of 128 rows (0 to 127, 128 to 255, ..., all dimensions but the last counted through in order) at most 80 rows name the same one
- weight_bwd: float32 [4, 1024], P('pp', ('node', 'local')), may hold values from 0.25 to 1
- saved_bwd: bfloat16 [4, 1024, 2048], P('pp', ('node', 'local')), may hold values from -8 to 8
- w_gate_up: bfloat16 [4, 2, 4096, 2048], P('pp', 'node', 'local'), may hold values from -0.09375 to 0.09375
- w_down: bfloat16 [4, 2, 1024, 4096], P('pp', 'node', None, 'local'), may hold values from -0.1875 to 0.1875
Outputs:
- next_input: bfloat16 [4, 1024, 4096], P('pp', ('node', 'local'))
- prev_grad: bfloat16 [4, 1024, 4096], P('pp', ('node', 'local'))
Inputs may be any that keep to these rules, and one draw needn't show every extreme that they name: `routes_fwd`: within each device's 128 tokens (aligned blocks of rows), no expert is named more than 80 times, a bound that some block reaches. `routes_bwd`: within each device's 128 tokens (aligned blocks of rows), no expert is named more than 80 times, a bound that some block reaches.
All inputs are finite; a program needn't handle non-finite values.
Results may differ from a plain program's by a relative error of at most 0.017.
Values may be sent and summed in bfloat16 or wider, within the bound.
No kernel may reach another device: no remote copies, remote signals or barrier semaphores. Data moves between devices by JAX's collectives and lax.ppermute only.
A program may use at most 128 MiB of HBM per device.

v0:
```python
import jax
import jax.numpy as jnp
from jax import lax
from jax.experimental import pallas as pl
from jax.experimental.pallas import tpu as pltpu
from jax.sharding import PartitionSpec as P

F32 = jnp.float32
BF16 = jnp.bfloat16
AXES = ("pp", "node", "local")


def move(value, by_pp=0, by_node=0, by_local=0, wrap=True, first=0, last=None):
    pps, nodes, locs = (lax.axis_size(a) for a in AXES)
    last = locs - 1 if last is None else last
    pairs = []
    for s in range(pps):
        for n in range(nodes):
            for l in range(locs):
                to = l + by_local
                if not wrap and not (first <= l <= last and 0 <= to < locs):
                    continue
                source = (s * nodes + n) * locs + l
                target = (((s + by_pp) % pps) * nodes + (n ^ by_node)) * locs + to % locs
                pairs.append((source, target))
    return lax.ppermute(value, AXES, pairs)


def sorted_places(route):
    ones = route.astype(F32)
    count = route.shape[0]
    earlier = (jnp.arange(count)[None, :] < jnp.arange(count)[:, None]).astype(F32)
    ones_before = jnp.dot(earlier, ones[:, None], preferred_element_type=F32)[:, 0]
    zeros = count - jnp.sum(ones)
    index = jnp.arange(count, dtype=F32)
    place = jnp.where(route == 0, index - ones_before, zeros + ones_before)
    return place.astype(jnp.int32)


def sorter(route):
    place = sorted_places(route)
    rows = jnp.arange(route.shape[0], dtype=jnp.int32)
    return (rows[:, None] == place[None, :]).astype(BF16)


def one_hot(row, count):
    return (row[:, None] == jnp.arange(count, dtype=jnp.int32)[None, :]).astype(BF16)


def dot_t(left, right):
    return lax.dot_general(left, right, (((1,), (1,)), ((), ())), preferred_element_type=F32)


def windows(blocks, node, capacity):
    tokens = blocks.shape[-2]
    start = tokens - capacity
    low = lax.slice_in_dim(blocks, 0, capacity, axis=-2 + blocks.ndim)
    high = lax.slice_in_dim(blocks, start, tokens, axis=-2 + blocks.ndim)
    own = jnp.where(node == 0, low, high)
    other = jnp.where(node == 0, high, low)
    return own, other


def join(*values):
    return lax.optimization_barrier(values)


def after(values, *others):
    return list(join(*values, *others)[: len(values)])


def cut(tokens, placer, local):
    column = tokens.shape[1] // 4
    blocks = []
    for m in range(4):
        block = lax.dynamic_slice_in_dim(tokens, ((local - m) % 4) * column, column, axis=1)
        blocks.append(jnp.dot(placer, block, preferred_element_type=F32).astype(BF16))
    return blocks


def sums(partial):
    right, left = partial(3), partial(1)
    for step in (1, 2, 3):
        right, left = right.astype(BF16), left.astype(BF16)
        got_r, got_l = yield (
            (right, dict(by_local=1, wrap=False, last=step - 1)),
            (left, dict(by_local=-1, wrap=False, first=4 - step)),
        )
        right = partial(3 - step).astype(F32) + got_r.astype(F32)
        if step < 3:
            left = partial(step + 1).astype(F32) + got_l.astype(F32)
    yield right + got_l.astype(F32)


def gathers(rows, local):
    from_left, from_right = [rows], [rows]
    for step in (1, 2, 3):
        got_r, got_l = yield (
            (from_left[-1], dict(by_local=1, wrap=False, first=step - 1)),
            (from_right[-1], dict(by_local=-1, wrap=False, last=4 - step)),
        )
        from_left.append(got_r)
        from_right.append(got_l)
    slots = [rows]
    for m in (1, 2, 3):
        slots.append(jnp.where(local + m < 4, from_right[m], from_left[4 - m]))
    yield jnp.stack(slots)


def send(pieces):
    return [move(value, **how) for value, how in pieces]


def operands(pieces):
    return [value for value, _ in pieces]


def valid(zeros, node, tokens, capacity):
    row = jnp.arange(capacity, dtype=F32)[None, :]
    return jnp.where(node == 0, row < zeros[:, None], row + (tokens - capacity) >= zeros[:, None])


def merge(own, other, node, tokens):
    slots, capacity, column = own.shape
    low = jnp.where(node == 0, own, other)
    high = jnp.where(node == 0, other, own)
    rest = jnp.zeros((slots, tokens - capacity, column), own.dtype)
    return jnp.concatenate([low, rest], axis=1) + jnp.concatenate([rest, high], axis=1)


def homeward(merged, by_pp):
    return [(merged[m], dict(by_pp=by_pp, by_local=m)) for m in (2, 1, 3, 0)]


def column_of(row_ref):
    n = row_ref.shape[1]
    row = lax.broadcasted_iota(jnp.int32, (n, n), 0)
    col = lax.broadcasted_iota(jnp.int32, (n, n), 1)
    return jnp.sum(jnp.where(row == col, row_ref[...], 0.0), axis=1, keepdims=True)


def cut_kernel(at_ref, route_ref, weight_ref, values_ref, *blocks):
    tokens = route_ref.shape[1]
    column = blocks[0].shape[1]
    row = lax.broadcasted_iota(jnp.int32, (tokens, tokens), 0)
    col = lax.broadcasted_iota(jnp.int32, (tokens, tokens), 1)
    ones = route_ref[...].astype(F32)
    before = jnp.dot(
        jnp.broadcast_to(ones, (8, tokens)).astype(BF16),
        (row < col).astype(BF16),
        preferred_element_type=F32,
    )[0:1]
    zeros = tokens - jnp.sum(ones, axis=1, keepdims=True)
    index = col[0:1].astype(F32)
    place = jnp.where(ones == 0.0, index - before, zeros + before).astype(jnp.int32)
    picker = (row == place).astype(BF16)
    weight = column_of(weight_ref)
    for i, block_ref in enumerate(blocks):
        cols = pl.ds(pl.multiple_of(at_ref[i] * column, column), column)
        block = (weight * values_ref[:, cols].astype(F32)).astype(BF16)
        block_ref[...] = jnp.dot(picker, block, preferred_element_type=F32).astype(BF16)


def scaled_cut(tokens, weight, route, local):
    rows, features = tokens.shape
    vmem = pl.BlockSpec(memory_space=pltpu.VMEM)
    at = jnp.stack([(local - m) % 4 for m in range(4)]).astype(jnp.int32)
    return list(
        pl.pallas_call(
            cut_kernel,
            out_shape=[jax.ShapeDtypeStruct((rows, features // 4), BF16)] * 4,
            in_specs=[pl.BlockSpec(memory_space=pltpu.SMEM)] + [vmem] * 3,
            out_specs=[vmem] * 4,
            compiler_params=pltpu.CompilerParams(vmem_limit_bytes=8 * 2**20),
            name="cut",
        )(at, route[None, :], weight[None, :], tokens)
    )


def finish_kernel(at_ref, weight_ref, pick_ref, residual_ref, *refs):
    *blocks, out_ref, rows, base, total, sem = refs
    count = len(blocks)
    column = rows.shape[-1]

    def cols(i):
        return pl.ds(pl.multiple_of(at_ref[i] * column, column), column)

    ins = []
    for i in range(count):
        ins.append(
            (
                pltpu.make_async_copy(blocks[i], rows.at[i], sem.at[0, i]),
                pltpu.make_async_copy(residual_ref.at[:, cols(i)], base.at[i], sem.at[1, i]),
            )
        )
        for copy in ins[i]:
            copy.start()
    weight = column_of(weight_ref)
    outs = []
    for i in range(count):
        for copy in ins[i]:
            copy.wait()
        moe = jnp.dot(pick_ref[...], rows[i], preferred_element_type=F32)
        total[i] = (base[i].astype(F32) + weight * moe).astype(total.dtype)
        outs.append(pltpu.make_async_copy(total.at[i], out_ref.at[0, :, cols(i)], sem.at[2, i]))
        outs[i].start()
    for copy in outs:
        copy.wait()


def finish(residual, weight, place, blocks, at):
    count, column = len(blocks), blocks[0].shape[-1]
    tokens, features = residual.shape
    vmem = pl.BlockSpec(memory_space=pltpu.VMEM)
    anywhere = pl.BlockSpec(memory_space=pl.ANY)
    return pl.pallas_call(
        finish_kernel,
        out_shape=jax.ShapeDtypeStruct((1, tokens, features), BF16),
        in_specs=[pl.BlockSpec(memory_space=pltpu.SMEM)] + [vmem] * 2 + [anywhere] * (1 + count),
        out_specs=anywhere,
        scratch_shapes=[pltpu.VMEM((count, tokens, column), BF16)] * 3
        + [pltpu.SemaphoreType.DMA((3, count))],
        compiler_params=pltpu.CompilerParams(vmem_limit_bytes=8 * 2**20),
        name="finish",
    )(at, weight[None, :], one_hot(place, tokens), residual, *blocks)


def body_pair(
    act_fwd, routes_fwd, weight_fwd, grad_bwd, routes_bwd, weight_bwd, saved_bwd, w_gate_up, w_down
):
    node = lax.axis_index("node")
    local = lax.axis_index("local")
    tokens_here = act_fwd.shape[1]
    capacity = 5 * tokens_here // 8
    w_gu = w_gate_up[0, 0]
    w_dn = w_down[0, 0]
    hidden_units = w_dn.shape[0]
    shape = (4, 2, capacity)

    act, grad = act_fwd[0], grad_bwd[0]
    route_a, route_b = routes_fwd[0, :, 0], routes_bwd[0, :, 0]
    sort_a, sort_b = sorter(route_a), sorter(route_b)
    zeros = tokens_here - jnp.stack([jnp.sum(route_a), jnp.sum(route_b)]).astype(F32)

    def in_rows(cuts, got):
        return windows(jnp.stack([cuts[0], got[1], got[0], got[2]]), node, capacity)

    def by_node(own, got, axis):
        return jnp.stack([jnp.where(node == 0, own, got), jnp.where(node == 0, got, own)], axis=axis)

    def split(done):
        own = lax.dynamic_index_in_dim(done, node, axis=1, keepdims=False)
        other = lax.dynamic_index_in_dim(done, 1 - node, axis=1, keepdims=False)
        return own, other

    def turn(chain, back, *others):
        pieces = chain.send(after(back, *others))
        return operands(pieces), send(pieces)

    cut_b = scaled_cut(grad, weight_bwd[0], route_b, local)
    c1, c2, c3, saved_in = join(*cut_b[1:], saved_bwd[0])
    got_b = [move(c2, by_local=-2), move(c1, by_local=-1), move(c3, by_local=-3)]
    saved = jnp.dot(sort_b, saved_in, preferred_element_type=F32).astype(BF16)
    saved_own, saved_other = windows(saved, node, capacity)
    saved_got = move(saved_other, by_node=1)
    (zeros_wait,) = after([zeros], saved_other)
    zeros_got = move(zeros_wait, by_node=1)
    cut_a = cut(act, sort_a, local)
    *got_b, saved_got, zeros_got, a0, a1, a2, a3 = join(*got_b, saved_got, zeros_got, *cut_a)
    cut_a = [a0, a1, a2, a3]
    zeros = by_node(zeros, zeros_got, 0)
    got_a = [move(cut_a[m], by_local=-m) for m in (2, 1, 3)]
    own_b, other_b = in_rows(cut_b, got_b)
    column = own_b.shape[-1]
    got_bx = move(other_b, by_node=1)

    rows_b = by_node(own_b, got_bx, 1).reshape(-1, column)
    part_b = dot_t(rows_b, w_dn).astype(BF16).reshape(shape + (hidden_units,))
    back_b = [move(part_b[m], by_local=m) for m in (2, 1, 3)]
    both = join(*back_b, *got_a)
    back_b, got_a = both[:3], both[3:]
    own_a, other_a = in_rows(cut_a, got_a)
    got_ax = move(other_a, by_node=1)
    dh = part_b[0].astype(F32) + sum(part.astype(F32) for part in back_b)
    dh = jnp.where(valid(zeros[:, 1], node, tokens_here, capacity)[..., None], dh, 0.0)
    saved_rows = by_node(saved_own, saved_got, 0)
    g = saved_rows[..., :hidden_units].astype(F32)
    u = saved_rows[..., hidden_units:].astype(F32)
    q = 1.0 / (1.0 + jnp.exp(-g))
    grad_gu = jnp.concatenate([dh * u * q * (1.0 + g * (1.0 - q)), dh * g * q], axis=-1).astype(
        BF16
    )

    chain_b = gathers(grad_gu, local)
    back_b = send(next(chain_b))
    small_wait, route_wait = after(
        [jnp.stack([route_a.astype(F32), weight_fwd[0]]), route_b], grad_gu
    )
    small_next = move(small_wait, by_pp=1)
    route_b_next = move(route_wait, by_pp=-1)
    rows_a = by_node(own_a, got_ax, 1).reshape(-1, column)
    part_a = jnp.dot(rows_a, w_gu, preferred_element_type=F32).astype(BF16)
    *back_b, part_a, small_next, route_b_next = join(*back_b, part_a, small_next, route_b_next)
    part_a = part_a.reshape(shape + (2 * hidden_units,))
    chain_a = sums(lambda slot: part_a[slot])
    values_b, back_b = turn(chain_b, back_b)
    pieces = next(chain_a)
    back_a = send(pieces)
    act_next = move(after([act], *operands(pieces))[0], by_pp=1)
    *back_b, act_next = join(*back_b, act_next)
    values_b, back_b = turn(chain_b, back_b)
    grad_next = move(join(grad, *values_b)[0], by_pp=-1)
    *back_b, grad_next = join(*back_b, grad_next)
    values_a, back_a = turn(chain_a, back_a)
    values_a, back_a = turn(chain_a, back_a)
    all_gu = chain_b.send(back_b)
    done_b = dot_t(all_gu.reshape(-1, 2 * hidden_units), w_gu).astype(BF16)
    own_b, other_b = split(done_b.reshape(shape + (column,)))
    got_b = move(other_b, by_node=1)

    preact = chain_a.send(back_a)
    preact = jnp.where(valid(zeros[:, 0], node, tokens_here, capacity)[..., None], preact, 0.0)
    hidden = (jax.nn.silu(preact[..., :hidden_units]) * preact[..., hidden_units:]).astype(BF16)
    all_hidden = [move(hidden, by_local=-m) for m in (1, 2, 3)]
    merged_b = merge(own_b, got_b, node, tokens_here)
    h1, h2, h3, merged_b = join(*all_hidden, merged_b)
    all_hidden = jnp.stack([hidden, h1, h2, h3])
    home_b = send(homeward(merged_b, -1))
    done_a = jnp.dot(
        all_hidden.reshape(-1, hidden_units), w_dn, preferred_element_type=F32
    ).astype(BF16)
    own_a, other_a = split(done_a.reshape(shape + (column,)))
    got_a = move(other_a, by_node=1)
    home_a = send(homeward(merge(own_a, got_a, node, tokens_here), 1))

    at = jnp.stack([(local - m) % 4 for m in (2, 1, 3, 0)]).astype(jnp.int32)
    ones = jnp.ones((tokens_here,), F32)
    prev_grad = finish(grad_next, ones, sorted_places(route_b_next), home_b, at)
    place_a = sorted_places(small_next[0].astype(jnp.int32))
    next_input = finish(act_next, small_next[1], place_a, home_a, at)
    return next_input, prev_grad


def from_behind(value, axis, by):
    length = lax.axis_size(axis)
    return lax.ppermute(value, axis, [(i, (i + by) % length) for i in range(length)])


def place_matrix(route, expert_count, capacity):
    onehot = (route[:, None] == jnp.arange(expert_count, dtype=jnp.int32)[None, :]).astype(
        jnp.int32
    )
    before = jnp.cumsum(onehot, axis=0) - onehot
    slot_index = jnp.sum(before * onehot, axis=1)
    target = route * capacity + slot_index
    positions = jnp.arange(expert_count * capacity, dtype=jnp.int32)
    return (positions[:, None] == target[None, :]).astype(jnp.bfloat16)


def pack_rows(placer, values, expert_count, capacity):
    packed = jnp.dot(placer, values, preferred_element_type=jnp.float32).astype(jnp.bfloat16)
    return packed.reshape(expert_count, capacity, values.shape[1])


def unpack_rows(placer, packed):
    flattened = packed.reshape(-1, packed.shape[-1])
    result = lax.dot_general(
        placer, flattened, (((0,), (0,)), ((), ())), preferred_element_type=jnp.float32
    )
    return result.astype(jnp.bfloat16)


def flat_outgoing(packed, local_count):
    expert_count, capacity, feature_count = packed.shape
    column = feature_count // local_count
    outgoing = packed.reshape(expert_count, capacity, local_count, column).transpose(0, 2, 1, 3)
    return outgoing.reshape(expert_count * local_count, capacity, column)


def flat_layout(received, expert_count, local_count):
    capacity = received.shape[1]
    column = received.shape[2]
    rows_in = received.reshape(expert_count, local_count, capacity, column).transpose(1, 0, 2, 3)
    return rows_in.reshape(-1, column)


def send_rows(packs, local_count):
    expert_count = packs[0].shape[0]
    outgoing = tuple((flat_outgoing(packed, local_count) for packed in packs))
    received = (
        lax.all_to_all(outgoing[0], ("node", "local"), split_axis=0, concat_axis=0, tiled=True),
        lax.all_to_all(outgoing[1], ("node", "local"), split_axis=0, concat_axis=0, tiled=True),
    )
    return tuple((flat_layout(item, expert_count, local_count) for item in received))


def return_rows(finished_pair, expert_count, capacity, local_count):
    column = finished_pair[0].shape[1]
    blocks = tuple(
        (item.reshape(local_count, expert_count, capacity, column) for item in finished_pair)
    )
    outgoing = tuple(
        (
            item.transpose(1, 0, 2, 3).reshape(expert_count * local_count, capacity, column)
            for item in blocks
        )
    )
    received = (
        lax.all_to_all(outgoing[0], ("node", "local"), split_axis=0, concat_axis=0, tiled=True),
        lax.all_to_all(outgoing[1], ("node", "local"), split_axis=0, concat_axis=0, tiled=True),
    )
    results = []
    for item in received:
        arranged = item.reshape(expert_count, local_count, capacity, column).transpose(0, 2, 1, 3)
        results.append(arranged.reshape(expert_count, capacity, local_count * column))
    return tuple(results)


def body(
    act_fwd, routes_fwd, weight_fwd, grad_bwd, routes_bwd, weight_bwd, saved_bwd, w_gate_up, w_down
):
    node_count = lax.axis_size("node")
    local_count = lax.axis_size("local")
    tokens_here = act_fwd.shape[1]
    capacity = 5 * tokens_here // (4 * node_count)
    rows_each = node_count * capacity
    w_gu = w_gate_up[0, 0]
    w_dn = w_down[0, 0]
    hidden_units = w_dn.shape[0]
    tokens_a = act_fwd[0]
    placer_a = place_matrix(routes_fwd[0, :, 0], node_count, capacity)
    cotangent = grad_bwd[0]
    placer_b = place_matrix(routes_bwd[0, :, 0], node_count, capacity)
    scaled = (weight_bwd[0][:, None] * cotangent.astype(jnp.float32)).astype(jnp.bfloat16)
    packed_a = pack_rows(placer_a, tokens_a, node_count, capacity)
    packed_b = pack_rows(placer_b, scaled, node_count, capacity)
    rows_a, rows_b = send_rows((packed_a, packed_b), local_count)
    saved_packed = pack_rows(placer_b, saved_bwd[0], node_count, capacity)
    saved_rows = lax.all_to_all(
        saved_packed, "node", split_axis=0, concat_axis=0, tiled=True
    ).reshape(rows_each, -1)
    row_block = rows_a
    preact = lax.psum_scatter(
        jnp.dot(row_block, w_gu, preferred_element_type=jnp.float32).astype(jnp.bfloat16),
        "local",
        scatter_dimension=0,
        tiled=True,
    ).astype(jnp.float32)
    row_block = rows_b
    grad_hidden = lax.psum_scatter(
        lax.dot_general(
            row_block, w_dn, (((1,), (1,)), ((), ())), preferred_element_type=jnp.float32
        ).astype(jnp.bfloat16),
        "local",
        scatter_dimension=0,
        tiled=True,
    ).astype(jnp.float32)
    hidden = (jax.nn.silu(preact[:, :hidden_units]) * preact[:, hidden_units:]).astype(jnp.bfloat16)
    done_a = jnp.dot(
        lax.all_gather(hidden, "local", axis=0, tiled=True),
        w_dn,
        preferred_element_type=jnp.float32,
    ).astype(jnp.bfloat16)
    gate_pre = saved_rows[:, :hidden_units].astype(jnp.float32)
    up_pre = saved_rows[:, hidden_units:].astype(jnp.float32)
    sigmoid_g = 1.0 / (1.0 + jnp.exp(-gate_pre))
    grad_gate = grad_hidden * up_pre * sigmoid_g * (1.0 + gate_pre * (1.0 - sigmoid_g))
    grad_up = grad_hidden * gate_pre * sigmoid_g
    grad_gu = jnp.concatenate([grad_gate, grad_up], axis=1).astype(jnp.bfloat16)
    product = lax.dot_general(
        lax.all_gather(grad_gu, "local", axis=0, tiled=True),
        w_gu,
        (((1,), (1,)), ((), ())),
        preferred_element_type=jnp.float32,
    )
    done_b = product.astype(jnp.bfloat16)
    back_a, back_b = return_rows((done_a, done_b), node_count, capacity, local_count)
    moe_a = unpack_rows(placer_a, back_a)
    result_a = tokens_a.astype(jnp.float32) + weight_fwd[0][:, None] * moe_a.astype(jnp.float32)
    result_a = result_a.astype(jnp.bfloat16)
    moe_b = unpack_rows(placer_b, back_b)
    result_b = (cotangent.astype(jnp.float32) + moe_b.astype(jnp.float32)).astype(jnp.bfloat16)
    next_input = from_behind(result_a[None], "pp", 1)
    prev_grad = from_behind(result_b[None], "pp", -1)
    return (next_input, prev_grad)


def solution(mesh):
    in_specs = (
        P("pp", ("node", "local"), None),
        P("pp", ("node", "local"), None),
        P("pp", ("node", "local")),
        P("pp", ("node", "local"), None),
        P("pp", ("node", "local"), None),
        P("pp", ("node", "local")),
        P("pp", ("node", "local"), None),
        P("pp", "node", "local", None),
        P("pp", "node", None, "local"),
    )
    out_specs = (P("pp", ("node", "local"), None), P("pp", ("node", "local"), None))
    paired = mesh.shape["node"] == 2 and mesh.shape["local"] == 4
    plan = body_pair if paired else body
    return jax.shard_map(plan, mesh=mesh, in_specs=in_specs, out_specs=out_specs, check_vma=False)
```

profile of v0, /device:TPU:0, one launch (start us, length us, event | category | flops | bytes accessed | tf_op | source)
XLA Modules:
  0.0 259.3 jit_solution(3004494539891435556)
XLA Ops:
  4.5 4.1 %collective-permute-start = (bf16[128,1024]{1,0:T(8,128)(2,1)S(1)}, bf16[128,1024]{1,0:T(8,128)(2,1)}, u32[]{:S(2)}, u32[]{:S(2)}) collective-permute-start(bf16[128,1024]{1,0:T(8,128)(2,1)S(1)} %get-tuple-element.56), channel_id=1, source_target_pairs={{0,2},{1,3},{2,0},{3,1},{4,6},{5,7},{6,4},{7,5},{8,10},{9,11},{10,... | collective-permute-start | bytes 786440 | tf_op jit(solution)/shard_map/ppermute | solution.py:26
  31.6 6.0 %collective-permute-start.9 = (bf16[128,1024]{1,0:T(8,128)(2,1)S(1)}, bf16[128,1024]{1,0:T(8,128)(2,1)S(1)}, u32[]{:S(2)}, u32[]{:S(2)}) collective-permute-start(bf16[128,1024]{1,0:T(8,128)(2,1)S(1)} %copy-done.19), channel_id=1, source_target_pairs={{0,2},{1,3},{2,0},{3,1},{4,6},{5,7},{6,4},{7,5},{8,10},{9,11},{10,... | collective-permute-start | bytes 786440 | tf_op jit(solution)/shard_map/ppermute | solution.py:26
  40.7 4.5 %collective-permute-done.5 = bf16[4,80,1024]{2,1,0:T(8,128)(2,1)S(1)} collective-permute-done((bf16[4,80,1024]{2,1,0:T(8,128)(2,1)S(1)}, bf16[4,80,1024]{2,1,0:T(8,128)(2,1)S(1)}, u32[]{:S(2)}, u32[]{:S(2)}) %collective-permute-start.5) | collective-permute-done | bytes 655392 | tf_op jit(solution)/shard_map/ppermute | solution.py:26
  47.2 3.2 %collective-permute-start.8 = (bf16[2,80,1024]{2,1,0:T(8,128)(2,1)S(1)}, bf16[2,80,1024]{2,1,0:T(8,128)(2,1)S(1)}, u32[]{:S(2)}, u32[]{:S(2)}) collective-permute-start(bf16[2,80,1024]{2,1,0:T(8,128)(2,1)S(1)} %bitcast.212), channel_id=1, source_target_pairs={{0,3},{1,0},{2,1},{3,2},{4,7},{5,4},{6,5},{7,6},{8,11},{9,8},{10,9... | collective-permute-start | bytes 983048 | tf_op jit(solution)/shard_map/ppermute | solution.py:26
  50.4 2.4 collective-permute-start.7
  52.8 4.0 %collective-permute-start.6 = (bf16[2,80,1024]{2,1,0:T(8,128)(2,1)S(1)}, bf16[2,80,1024]{2,1,0:T(8,128)(2,1)S(1)}, u32[]{:S(2)}, u32[]{:S(2)}) collective-permute-start(bf16[2,80,1024]{2,1,0:T(8,128)(2,1)S(1)} %bitcast.210), channel_id=1, source_target_pairs={{0,2},{1,3},{2,0},{3,1},{4,6},{5,7},{6,4},{7,5},{8,10},{9,11},{10,... | collective-permute-start | bytes 983048 | tf_op jit(solution)/shard_map/ppermute | solution.py:26
  58.3 10.5 %collective-permute-done.8 = bf16[2,80,1024]{2,1,0:T(8,128)(2,1)S(1)} collective-permute-done((bf16[2,80,1024]{2,1,0:T(8,128)(2,1)S(1)}, bf16[2,80,1024]{2,1,0:T(8,128)(2,1)S(1)}, u32[]{:S(2)}, u32[]{:S(2)}) %collective-permute-start.8) | collective-permute-done | bytes 327712 | tf_op jit(solution)/shard_map/ppermute | solution.py:26
  68.8 3.2 %collective-permute-done.7 = bf16[2,80,1024]{2,1,0:T(8,128)(2,1)S(1)} collective-permute-done((bf16[2,80,1024]{2,1,0:T(8,128)(2,1)S(1)}, bf16[2,80,1024]{2,1,0:T(8,128)(2,1)S(1)}, u32[]{:S(2)}, u32[]{:S(2)}) %collective-permute-start.7) | collective-permute-done | bytes 327712 | tf_op jit(solution)/shard_map/ppermute | solution.py:26
  72.0 16.8 %collective-permute-done.6 = bf16[2,80,1024]{2,1,0:T(8,128)(2,1)S(1)} collective-permute-done((bf16[2,80,1024]{2,1,0:T(8,128)(2,1)S(1)}, bf16[2,80,1024]{2,1,0:T(8,128)(2,1)S(1)}, u32[]{:S(2)}, u32[]{:S(2)}) %collective-permute-start.6) | collective-permute-done | bytes 327712 | tf_op jit(solution)/shard_map/ppermute | solution.py:26
  92.1 4.6 %collective-permute-start.12 = (bf16[2,80,2048]{2,1,0:T(8,128)(2,1)S(1)}, bf16[2,80,2048]{2,1,0:T(8,128)(2,1)S(1)}, u32[]{:S(2)}, u32[]{:S(2)}) collective-permute-start(bf16[2,80,2048]{2,1,0:T(8,128)(2,1)S(1)} %pad_maximum_fusion.6), channel_id=1, source_target_pairs={{0,1},{1,2},{2,3},{4,5},{5,6},{6,7},{8,9},{9,10},{10,11},{12,13},{... | collective-permute-start | bytes 1966088 | tf_op jit(solution)/shard_map/ppermute | solution.py:26
  97.2 8.5 %collective-permute-done.14 = bf16[4,80,1024]{2,1,0:T(8,128)(2,1)S(1)} collective-permute-done((bf16[4,80,1024]{2,1,0:T(8,128)(2,1)S(1)}, bf16[4,80,1024]{2,1,0:T(8,128)(2,1)S(1)}, u32[]{:S(2)}, u32[]{:S(2)}) %collective-permute-start.14) | collective-permute-done | bytes 655392 | tf_op jit(solution)/shard_map/ppermute | solution.py:26
  108.0 3.1 %fusion.4 = bf16[640,2048]{1,0:T(8,128)(2,1)S(1)} fusion(bf16[640,1024]{1,0:T(8,128)(2,1)S(1)} %bitcast.202, bf16[1,1,1024,2048]{3,2,1,0:T(8,128)(2,1)S(1)} %copy-done.21), kind=kOutput, calls=%fused_computation.4 | convolution fusion | flops 2685665280 | bytes 8126464 | tf_op jit(solution)/shard_map/dot_general | solution.py:302
  114.3 4.1 %collective-permute-start.20 = (bf16[2,80,2048]{2,1,0:T(8,128)(2,1)}, bf16[2,80,2048]{2,1,0:T(8,128)(2,1)}, u32[]{:S(2)}, u32[]{:S(2)}) collective-permute-start(bf16[2,80,2048]{2,1,0:T(8,128)(2,1)} %bitcast.50), channel_id=1, source_target_pairs={{0,1},{4,5},{8,9},{12,13},{16,17},{20,21},{24,25},{28,29}} | collective-permute-start | bytes 1966088 | tf_op jit(solution)/shard_map/ppermute | solution.py:26
  122.7 7.8 %collective-permute-done.20 = bf16[2,80,2048]{2,1,0:T(8,128)(2,1)} collective-permute-done((bf16[2,80,2048]{2,1,0:T(8,128)(2,1)}, bf16[2,80,2048]{2,1,0:T(8,128)(2,1)}, u32[]{:S(2)}, u32[]{:S(2)}) %collective-permute-start.20) | collective-permute-done | bytes 655392 | tf_op jit(solution)/shard_map/ppermute | solution.py:26
  130.5 3.0 %fusion.21 = (bf16[2,80,2048]{2,1,0:T(8,128)(2,1)}, bf16[2,80,2048]{2,1,0:T(8,128)(2,1)}) fusion(bf16[2,80,2048]{2,1,0:T(8,128)(2,1)} %bitcast.199, bf16[2,80,2048]{2,1,0:T(8,128)(2,1)} %collective-permute-done.21, bf16[2,80,2048]{2,1,0:T(8,128)(2,1)} %collective-permute-done.20), kind=kLoop, calls=%fused_computation.17 | loop fusion | flops 2293760 | bytes 3276800 | tf_op jit(solution)/shard_map/convert_element_type | solution.py:84
  135.0 5.0 %collective-permute-start.22 = (bf16[2,80,2048]{2,1,0:T(8,128)(2,1)}, bf16[2,80,2048]{2,1,0:T(8,128)(2,1)}, u32[]{:S(2)}, u32[]{:S(2)}) collective-permute-start(bf16[2,80,2048]{2,1,0:T(8,128)(2,1)} %get-tuple-element.135), channel_id=1, source_target_pairs={{0,1},{1,2},{4,5},{5,6},{8,9},{9,10},{12,13},{13,14},{16,17},{17,1... | collective-permute-start | bytes 1966088 | tf_op jit(solution)/shard_map/ppermute | solution.py:26
  145.1 6.1 %collective-permute-done.22 = bf16[2,80,2048]{2,1,0:T(8,128)(2,1)} collective-permute-done((bf16[2,80,2048]{2,1,0:T(8,128)(2,1)}, bf16[2,80,2048]{2,1,0:T(8,128)(2,1)}, u32[]{:S(2)}, u32[]{:S(2)}) %collective-permute-start.22) | collective-permute-done | bytes 655392 | tf_op jit(solution)/shard_map/ppermute | solution.py:26
  155.4 7.0 %collective-permute-start.24 = (bf16[2,80,2048]{2,1,0:T(8,128)(2,1)S(1)}, bf16[2,80,2048]{2,1,0:T(8,128)(2,1)S(1)}, u32[]{:S(2)}, u32[]{:S(2)}) collective-permute-start(bf16[2,80,2048]{2,1,0:T(8,128)(2,1)S(1)} %add_convert_fusion.1), channel_id=1, source_target_pairs={{0,1},{1,2},{2,3},{4,5},{5,6},{6,7},{8,9},{9,10},{10,11},{12,13},{... | collective-permute-start | bytes 1966088 | tf_op jit(solution)/shard_map/ppermute | solution.py:26
  164.9 2.9 %fusion.11 = bf16[640,1024]{1,0:T(8,128)(2,1)S(1)} fusion(bf16[640,2048]{1,0:T(8,128)(2,1)S(1)} %bitcast.195, bf16[1,1,1024,2048]{3,2,1,0:T(8,128)(2,1)S(1)} %copy-done.22), kind=kOutput, calls=%fused_computation.13 | convolution fusion | flops 2685009920 | bytes 8126464 | tf_op jit(solution)/shard_map/dot_general | solution.py:51
  169.0 5.5 %collective-permute-done.25 = bf16[2,80,2048]{2,1,0:T(8,128)(2,1)S(1)} collective-permute-done((bf16[2,80,2048]{2,1,0:T(8,128)(2,1)S(1)}, bf16[2,80,2048]{2,1,0:T(8,128)(2,1)S(1)}, u32[]{:S(2)}, u32[]{:S(2)}) %collective-permute-start.25) | collective-permute-done | bytes 655392 | tf_op jit(solution)/shard_map/ppermute | solution.py:26
  176.5 3.7 %collective-permute-start.27 = (bf16[2,80,1024]{2,1,0:T(8,128)(2,1)S(1)}, bf16[2,80,1024]{2,1,0:T(8,128)(2,1)S(1)}, u32[]{:S(2)}, u32[]{:S(2)}) collective-permute-start(bf16[2,80,1024]{2,1,0:T(8,128)(2,1)S(1)} %fusion.32), channel_id=1, source_target_pairs={{0,2},{1,3},{2,0},{3,1},{4,6},{5,7},{6,4},{7,5},{8,10},{9,11},{10,... | collective-permute-start | bytes 983048 | tf_op jit(solution)/shard_map/ppermute | solution.py:26
  184.1 17.8 %collective-permute-done.27 = bf16[2,80,1024]{2,1,0:T(8,128)(2,1)S(1)} collective-permute-done((bf16[2,80,1024]{2,1,0:T(8,128)(2,1)S(1)}, bf16[2,80,1024]{2,1,0:T(8,128)(2,1)S(1)}, u32[]{:S(2)}, u32[]{:S(2)}) %collective-permute-start.27) | collective-permute-done | bytes 327712 | tf_op jit(solution)/shard_map/ppermute | solution.py:26
  205.2 2.2 collective-permute-start.40
  207.4 3.9 %collective-permute-start.39 = (bf16[128,1024]{1,0:T(8,128)(2,1)S(1)}, bf16[128,1024]{1,0:T(8,128)(2,1)S(1)}, u32[]{:S(2)}, u32[]{:S(2)}) collective-permute-start(bf16[128,1024]{1,0:T(8,128)(2,1)S(1)} %get-tuple-element.130), channel_id=1, source_target_pairs={{0,25},{1,26},{2,27},{3,24},{4,29},{5,30},{6,31},{7,28},{8,1},{9,2... | collective-permute-start | bytes 786440 | tf_op jit(solution)/shard_map/ppermute | solution.py:26
  211.4 3.2 %collective-permute-start.38 = (bf16[128,1024]{1,0:T(8,128)(2,1)S(1)}, bf16[128,1024]{1,0:T(8,128)(2,1)S(1)}, u32[]{:S(2)}, u32[]{:S(2)}) collective-permute-start(bf16[128,1024]{1,0:T(8,128)(2,1)S(1)} %get-tuple-element.131), channel_id=1, source_target_pairs={{0,26},{1,27},{2,24},{3,25},{4,30},{5,31},{6,28},{7,29},{8,2},{9,3... | collective-permute-start | bytes 786440 | tf_op jit(solution)/shard_map/ppermute | solution.py:26
  214.6 3.5 %collective-permute-done.33 = bf16[4,80,1024]{2,1,0:T(8,128)(2,1)S(1)} collective-permute-done((bf16[4,80,1024]{2,1,0:T(8,128)(2,1)S(1)}, bf16[4,80,1024]{2,1,0:T(8,128)(2,1)S(1)}, u32[]{:S(2)}, u32[]{:S(2)}) %collective-permute-start.33) | collective-permute-done | bytes 655392 | tf_op jit(solution)/shard_map/ppermute | solution.py:26
  218.4 6.6 %collective-permute-start.34 = (bf16[128,1024]{1,0:T(8,128)(2,1)S(1)}, bf16[128,1024]{1,0:T(8,128)(2,1)S(1)}, u32[]{:S(2)}, u32[]{:S(2)}) collective-permute-start(bf16[128,1024]{1,0:T(8,128)(2,1)S(1)} %get-tuple-element.121), channel_id=1, source_target_pairs={{0,10},{1,11},{2,8},{3,9},{4,14},{5,15},{6,12},{7,13},{8,18},{9,19... | collective-permute-start | bytes 786440 | tf_op jit(solution)/shard_map/ppermute | solution.py:26
  225.0 18.7 %collective-permute-start.35 = (bf16[128,1024]{1,0:T(8,128)(2,1)S(1)}, bf16[128,1024]{1,0:T(8,128)(2,1)S(1)}, u32[]{:S(2)}, u32[]{:S(2)}) collective-permute-start(bf16[128,1024]{1,0:T(8,128)(2,1)S(1)} %get-tuple-element.122), channel_id=1, source_target_pairs={{0,9},{1,10},{2,11},{3,8},{4,13},{5,14},{6,15},{7,12},{8,17},{9,18... | collective-permute-start | bytes 786440 | tf_op jit(solution)/shard_map/ppermute | solution.py:26
  243.9 3.5 %collective-permute-done.38.refs_0_ = bf16[128,1024]{1,0:T(8,128)(2,1)S(1)} collective-permute-done((bf16[128,1024]{1,0:T(8,128)(2,1)S(1)}, bf16[128,1024]{1,0:T(8,128)(2,1)S(1)}, u32[]{:S(2)}, u32[]{:S(2)}) %collective-permute-start.38) | collective-permute-done | bytes 262176 | tf_op jit(solution)/shard_map/ppermute | solution.py:26
  247.4 2.5 finish.3
  251.4 4.5 %collective-permute-done.36.refs_2_ = bf16[128,1024]{1,0:T(8,128)(2,1)S(1)} collective-permute-done((bf16[128,1024]{1,0:T(8,128)(2,1)S(1)}, bf16[128,1024]{1,0:T(8,128)(2,1)S(1)}, u32[]{:S(2)}, u32[]{:S(2)}) %collective-permute-start.36) | collective-permute-done | bytes 262176 | tf_op jit(solution)/shard_map/ppermute | solution.py:26
  255.9 3.2 %finish.2 = bf16[1,128,4096]{2,1,0:T(8,128)(2,1)} custom-call(s32[4]{0:T(128)S(1)} %pad_add_fusion.2.at_ref, f32[1,128]{1,0:T(1,128)S(1)} %get-tuple-element.137.weight_ref, bf16[128,128]{1,0:T(8,128)(2,1)S(1)} %fusion.50.pick_ref, bf16[128,4096]{1,0:T(8,128)(2,1)} %collective-permute-done.19.residual_ref, ...), custom_call_target="tpu_custom_call" | custom-call | tf_op jit(solution)/shard_map/finish/pallas_call | solution.py:216
  (167 shorter events, 69.4 us)
Async XLA Ops:
  4.5 24.1 %collective-permute-start = (bf16[128,1024]{1,0:T(8,128)(2,1)S(1)}, bf16[128,1024]{1,0:T(8,128)(2,1)}, u32[]{:S(2)}, u32[]{:S(2)}) collective-permute-start(bf16[128,1024]{1,0:T(8,128)(2,1)S(1)} %get-tuple-element.56), channel_id=1, source_target_pairs={{0,2},{1,3},{2,0},{3,1},{4,6},{5,7},{6,4},{7,5},{8,10},{9,11},{10,... | collective-permute-start | bytes 786440 | tf_op jit(solution)/shard_map/ppermute | solution.py:26
  8.6 20.0 %collective-permute-start.1 = (bf16[128,1024]{1,0:T(8,128)(2,1)S(1)}, bf16[128,1024]{1,0:T(8,128)(2,1)}, u32[]{:S(2)}, u32[]{:S(2)}) collective-permute-start(bf16[128,1024]{1,0:T(8,128)(2,1)S(1)} %get-tuple-element.57), channel_id=1, source_target_pairs={{0,3},{1,0},{2,1},{3,2},{4,7},{5,4},{6,5},{7,6},{8,11},{9,8},{10,9... | collective-permute-start | bytes 786440 | tf_op jit(solution)/shard_map/ppermute | solution.py:26
  10.0 18.6 %collective-permute-start.2 = (bf16[128,1024]{1,0:T(8,128)(2,1)S(1)}, bf16[128,1024]{1,0:T(8,128)(2,1)}, u32[]{:S(2)}, u32[]{:S(2)}) collective-permute-start(bf16[128,1024]{1,0:T(8,128)(2,1)S(1)} %get-tuple-element.58), channel_id=1, source_target_pairs={{0,1},{1,2},{2,3},{3,0},{4,5},{5,6},{6,7},{7,4},{8,9},{9,10},{10,1... | collective-permute-start | bytes 786440 | tf_op jit(solution)/shard_map/ppermute | solution.py:26
  31.6 21.2 %collective-permute-start.9 = (bf16[128,1024]{1,0:T(8,128)(2,1)S(1)}, bf16[128,1024]{1,0:T(8,128)(2,1)S(1)}, u32[]{:S(2)}, u32[]{:S(2)}) collective-permute-start(bf16[128,1024]{1,0:T(8,128)(2,1)S(1)} %copy-done.19), channel_id=1, source_target_pairs={{0,2},{1,3},{2,0},{3,1},{4,6},{5,7},{6,4},{7,5},{8,10},{9,11},{10,... | collective-permute-start | bytes 786440 | tf_op jit(solution)/shard_map/ppermute | solution.py:26
  37.6 20.7 %collective-permute-start.10 = (bf16[128,1024]{1,0:T(8,128)(2,1)S(1)}, bf16[128,1024]{1,0:T(8,128)(2,1)S(1)}, u32[]{:S(2)}, u32[]{:S(2)}) collective-permute-start(bf16[128,1024]{1,0:T(8,128)(2,1)S(1)} %copy-done.18), channel_id=1, source_target_pairs={{0,3},{1,0},{2,1},{3,2},{4,7},{5,4},{6,5},{7,6},{8,11},{9,8},{10,9... | collective-permute-start | bytes 786440 | tf_op jit(solution)/shard_map/ppermute | solution.py:26
  38.0 20.3 %collective-permute-start.11 = (bf16[128,1024]{1,0:T(8,128)(2,1)S(1)}, bf16[128,1024]{1,0:T(8,128)(2,1)S(1)}, u32[]{:S(2)}, u32[]{:S(2)}) collective-permute-start(bf16[128,1024]{1,0:T(8,128)(2,1)S(1)} %copy-done.17), channel_id=1, source_target_pairs={{0,1},{1,2},{2,3},{3,0},{4,5},{5,6},{6,7},{7,4},{8,9},{9,10},{10,1... | collective-permute-start | bytes 786440 | tf_op jit(solution)/shard_map/ppermute | solution.py:26
  47.2 21.6 %collective-permute-start.8 = (bf16[2,80,1024]{2,1,0:T(8,128)(2,1)S(1)}, bf16[2,80,1024]{2,1,0:T(8,128)(2,1)S(1)}, u32[]{:S(2)}, u32[]{:S(2)}) collective-permute-start(bf16[2,80,1024]{2,1,0:T(8,128)(2,1)S(1)} %bitcast.212), channel_id=1, source_target_pairs={{0,3},{1,0},{2,1},{3,2},{4,7},{5,4},{6,5},{7,6},{8,11},{9,8},{10,9... | collective-permute-start | bytes 983048 | tf_op jit(solution)/shard_map/ppermute | solution.py:26
  50.4 21.6 %collective-permute-start.7 = (bf16[2,80,1024]{2,1,0:T(8,128)(2,1)S(1)}, bf16[2,80,1024]{2,1,0:T(8,128)(2,1)S(1)}, u32[]{:S(2)}, u32[]{:S(2)}) collective-permute-start(bf16[2,80,1024]{2,1,0:T(8,128)(2,1)S(1)} %bitcast.211), channel_id=1, source_target_pairs={{0,1},{1,2},{2,3},{3,0},{4,5},{5,6},{6,7},{7,4},{8,9},{9,10},{10,1... | collective-permute-start | bytes 983048 | tf_op jit(solution)/shard_map/ppermute | solution.py:26
  52.8 36.0 %collective-permute-start.6 = (bf16[2,80,1024]{2,1,0:T(8,128)(2,1)S(1)}, bf16[2,80,1024]{2,1,0:T(8,128)(2,1)S(1)}, u32[]{:S(2)}, u32[]{:S(2)}) collective-permute-start(bf16[2,80,1024]{2,1,0:T(8,128)(2,1)S(1)} %bitcast.210), channel_id=1, source_target_pairs={{0,2},{1,3},{2,0},{3,1},{4,6},{5,7},{6,4},{7,5},{8,10},{9,11},{10,... | collective-permute-start | bytes 983048 | tf_op jit(solution)/shard_map/ppermute | solution.py:26
  89.0 16.7 %collective-permute-start.14 = (bf16[4,80,1024]{2,1,0:T(8,128)(2,1)S(1)}, bf16[4,80,1024]{2,1,0:T(8,128)(2,1)S(1)}, u32[]{:S(2)}, u32[]{:S(2)}) collective-permute-start(bf16[4,80,1024]{2,1,0:T(8,128)(2,1)S(1)} %broadcast_select_fusion), channel_id=1, source_target_pairs={{0,4},{1,5},{2,6},{3,7},{4,0},{5,1},{6,2},{7,3},{8,12},{9,13},{10,... | collective-permute-start | bytes 1966088 | tf_op jit(solution)/shard_map/ppermute | solution.py:26
  90.8 20.4 %collective-permute-start.13 = (bf16[2,80,2048]{2,1,0:T(8,128)(2,1)S(1)}, bf16[2,80,2048]{2,1,0:T(8,128)(2,1)S(1)}, u32[]{:S(2)}, u32[]{:S(2)}) collective-permute-start(bf16[2,80,2048]{2,1,0:T(8,128)(2,1)S(1)} %pad_maximum_fusion.6), channel_id=1, source_target_pairs={{1,0},{2,1},{3,2},{5,4},{6,5},{7,6},{9,8},{10,9},{11,10},{13,12},{... | collective-permute-start | bytes 1966088 | tf_op jit(solution)/shard_map/ppermute | solution.py:26
  92.1 19.1 %collective-permute-start.12 = (bf16[2,80,2048]{2,1,0:T(8,128)(2,1)S(1)}, bf16[2,80,2048]{2,1,0:T(8,128)(2,1)S(1)}, u32[]{:S(2)}, u32[]{:S(2)}) collective-permute-start(bf16[2,80,2048]{2,1,0:T(8,128)(2,1)S(1)} %pad_maximum_fusion.6), channel_id=1, source_target_pairs={{0,1},{1,2},{2,3},{4,5},{5,6},{6,7},{8,9},{9,10},{10,11},{12,13},{... | collective-permute-start | bytes 1966088 | tf_op jit(solution)/shard_map/ppermute | solution.py:26
  114.3 16.1 %collective-permute-start.20 = (bf16[2,80,2048]{2,1,0:T(8,128)(2,1)}, bf16[2,80,2048]{2,1,0:T(8,128)(2,1)}, u32[]{:S(2)}, u32[]{:S(2)}) collective-permute-start(bf16[2,80,2048]{2,1,0:T(8,128)(2,1)} %bitcast.50), channel_id=1, source_target_pairs={{0,1},{4,5},{8,9},{12,13},{16,17},{20,21},{24,25},{28,29}} | collective-permute-start | bytes 1966088 | tf_op jit(solution)/shard_map/ppermute | solution.py:26
  118.4 23.0 %collective-permute-start.19 = (bf16[128,4096]{1,0:T(8,128)(2,1)}, bf16[128,4096]{1,0:T(8,128)(2,1)}, u32[]{:S(2)}, u32[]{:S(2)}) collective-permute-start(bf16[128,4096]{1,0:T(8,128)(2,1)} %bitcast.49), channel_id=1, source_target_pairs={{0,8},{1,9},{2,10},{3,11},{4,12},{5,13},{6,14},{7,15},{8,16},{9,17... | collective-permute-start | bytes 3145736 | tf_op jit(solution)/shard_map/ppermute | solution.py:26
  119.8 21.6 %collective-permute-start.17 = (bf16[2,80,2048]{2,1,0:T(8,128)(2,1)}, bf16[2,80,2048]{2,1,0:T(8,128)(2,1)}, u32[]{:S(2)}, u32[]{:S(2)}) collective-permute-start(bf16[2,80,2048]{2,1,0:T(8,128)(2,1)} %copy-done.15), channel_id=1, source_target_pairs={{1,2},{2,3},{5,6},{6,7},{9,10},{10,11},{13,14},{14,15},{17,18},{18... | collective-permute-start | bytes 1966088 | tf_op jit(solution)/shard_map/ppermute | solution.py:26
  121.4 20.0 %collective-permute-start.18 = (bf16[2,80,2048]{2,1,0:T(8,128)(2,1)}, bf16[2,80,2048]{2,1,0:T(8,128)(2,1)}, u32[]{:S(2)}, u32[]{:S(2)}) collective-permute-start(bf16[2,80,2048]{2,1,0:T(8,128)(2,1)} %copy-done.13), channel_id=1, source_target_pairs={{1,0},{2,1},{5,4},{6,5},{9,8},{10,9},{13,12},{14,13},{17,16},{18,1... | collective-permute-start | bytes 1966088 | tf_op jit(solution)/shard_map/ppermute | solution.py:26
  135.0 16.2 %collective-permute-start.22 = (bf16[2,80,2048]{2,1,0:T(8,128)(2,1)}, bf16[2,80,2048]{2,1,0:T(8,128)(2,1)}, u32[]{:S(2)}, u32[]{:S(2)}) collective-permute-start(bf16[2,80,2048]{2,1,0:T(8,128)(2,1)} %get-tuple-element.135), channel_id=1, source_target_pairs={{0,1},{1,2},{4,5},{5,6},{8,9},{9,10},{12,13},{13,14},{16,17},{17,1... | collective-permute-start | bytes 1966088 | tf_op jit(solution)/shard_map/ppermute | solution.py:26
  141.4 21.0 %collective-permute-start.29 = (bf16[2,80,2048]{2,1,0:T(8,128)(2,1)}, bf16[2,80,2048]{2,1,0:T(8,128)(2,1)S(1)}, u32[]{:S(2)}, u32[]{:S(2)}) collective-permute-start(bf16[2,80,2048]{2,1,0:T(8,128)(2,1)} %collective-permute-done.17), channel_id=1, source_target_pairs={{2,3},{6,7},{10,11},{14,15},{18,19},{22,23},{26,27},{30,31}} | collective-permute-start | bytes 1966088 | tf_op jit(solution)/shard_map/ppermute | solution.py:26
  142.1 20.3 %collective-permute-start.30 = (bf16[2,80,2048]{2,1,0:T(8,128)(2,1)}, bf16[2,80,2048]{2,1,0:T(8,128)(2,1)S(1)}, u32[]{:S(2)}, u32[]{:S(2)}) collective-permute-start(bf16[2,80,2048]{2,1,0:T(8,128)(2,1)} %collective-permute-done.18), channel_id=1, source_target_pairs={{1,0},{5,4},{9,8},{13,12},{17,16},{21,20},{25,24},{29,28}} | collective-permute-start | bytes 1966088 | tf_op jit(solution)/shard_map/ppermute | solution.py:26
  143.5 19.0 %collective-permute-start.31 = (bf16[128,4096]{1,0:T(8,128)(2,1)S(1)}, bf16[128,4096]{1,0:T(8,128)(2,1)S(1)}, u32[]{:S(2)}, u32[]{:S(2)}) collective-permute-start(bf16[128,4096]{1,0:T(8,128)(2,1)S(1)} %bitcast.189), channel_id=1, source_target_pairs={{0,24},{1,25},{2,26},{3,27},{4,28},{5,29},{6,30},{7,31},{8,0},{9,1... | collective-permute-start | bytes 3145736 | tf_op jit(solution)/shard_map/ppermute | solution.py:26
  152.7 21.8 %collective-permute-start.25 = (bf16[2,80,2048]{2,1,0:T(8,128)(2,1)S(1)}, bf16[2,80,2048]{2,1,0:T(8,128)(2,1)S(1)}, u32[]{:S(2)}, u32[]{:S(2)}) collective-permute-start(bf16[2,80,2048]{2,1,0:T(8,128)(2,1)S(1)} %add_convert_fusion), channel_id=1, source_target_pairs={{1,0},{2,1},{3,2},{5,4},{6,5},{7,6},{9,8},{10,9},{11,10},{13,12},{... | collective-permute-start | bytes 1966088 | tf_op jit(solution)/shard_map/ppermute | solution.py:26
  155.4 20.5 %collective-permute-start.24 = (bf16[2,80,2048]{2,1,0:T(8,128)(2,1)S(1)}, bf16[2,80,2048]{2,1,0:T(8,128)(2,1)S(1)}, u32[]{:S(2)}, u32[]{:S(2)}) collective-permute-start(bf16[2,80,2048]{2,1,0:T(8,128)(2,1)S(1)} %add_convert_fusion.1), channel_id=1, source_target_pairs={{0,1},{1,2},{2,3},{4,5},{5,6},{6,7},{8,9},{9,10},{10,11},{12,13},{... | collective-permute-start | bytes 1966088 | tf_op jit(solution)/shard_map/ppermute | solution.py:26
  167.8 16.0 %collective-permute-start.32 = (bf16[4,80,1024]{2,1,0:T(8,128)(2,1)S(1)}, bf16[4,80,1024]{2,1,0:T(8,128)(2,1)S(1)}, u32[]{:S(2)}, u32[]{:S(2)}) collective-permute-start(bf16[4,80,1024]{2,1,0:T(8,128)(2,1)S(1)} %dynamic-slice_bitcast_fusion.1), channel_id=1, source_target_pairs={{0,4},{1,5},{2,6},{3,7},{4,0},{5,1},{6,2},{7,3},{8,12},{9,13},{10,... | collective-permute-start | bytes 1966088 | tf_op jit(solution)/shard_map/ppermute | solution.py:26
  176.5 25.4 %collective-permute-start.27 = (bf16[2,80,1024]{2,1,0:T(8,128)(2,1)S(1)}, bf16[2,80,1024]{2,1,0:T(8,128)(2,1)S(1)}, u32[]{:S(2)}, u32[]{:S(2)}) collective-permute-start(bf16[2,80,1024]{2,1,0:T(8,128)(2,1)S(1)} %fusion.32), channel_id=1, source_target_pairs={{0,2},{1,3},{2,0},{3,1},{4,6},{5,7},{6,4},{7,5},{8,10},{9,11},{10,... | collective-permute-start | bytes 983048 | tf_op jit(solution)/shard_map/ppermute | solution.py:26
  180.2 21.7 %collective-permute-start.26 = (bf16[2,80,1024]{2,1,0:T(8,128)(2,1)S(1)}, bf16[2,80,1024]{2,1,0:T(8,128)(2,1)S(1)}, u32[]{:S(2)}, u32[]{:S(2)}) collective-permute-start(bf16[2,80,1024]{2,1,0:T(8,128)(2,1)S(1)} %fusion.32), channel_id=1, source_target_pairs={{0,3},{1,0},{2,1},{3,2},{4,7},{5,4},{6,5},{7,6},{8,11},{9,8},{10,9... | collective-permute-start | bytes 983048 | tf_op jit(solution)/shard_map/ppermute | solution.py:26
  181.4 20.5 %collective-permute-start.28 = (bf16[2,80,1024]{2,1,0:T(8,128)(2,1)S(1)}, bf16[2,80,1024]{2,1,0:T(8,128)(2,1)S(1)}, u32[]{:S(2)}, u32[]{:S(2)}) collective-permute-start(bf16[2,80,1024]{2,1,0:T(8,128)(2,1)S(1)} %fusion.32), channel_id=1, source_target_pairs={{0,1},{1,2},{2,3},{3,0},{4,5},{5,6},{6,7},{7,4},{8,9},{9,10},{10,1... | collective-permute-start | bytes 983048 | tf_op jit(solution)/shard_map/ppermute | solution.py:26
  205.2 19.7 %collective-permute-start.40 = (bf16[128,1024]{1,0:T(8,128)(2,1)S(1)}, bf16[128,1024]{1,0:T(8,128)(2,1)S(1)}, u32[]{:S(2)}, u32[]{:S(2)}) collective-permute-start(bf16[128,1024]{1,0:T(8,128)(2,1)S(1)} %get-tuple-element.129), channel_id=1, source_target_pairs={{0,27},{1,24},{2,25},{3,26},{4,31},{5,28},{6,29},{7,30},{8,3},{9,0... | collective-permute-start | bytes 786440 | tf_op jit(solution)/shard_map/ppermute | solution.py:26
  207.4 36.2 %collective-permute-start.39 = (bf16[128,1024]{1,0:T(8,128)(2,1)S(1)}, bf16[128,1024]{1,0:T(8,128)(2,1)S(1)}, u32[]{:S(2)}, u32[]{:S(2)}) collective-permute-start(bf16[128,1024]{1,0:T(8,128)(2,1)S(1)} %get-tuple-element.130), channel_id=1, source_target_pairs={{0,25},{1,26},{2,27},{3,24},{4,29},{5,30},{6,31},{7,28},{8,1},{9,2... | collective-permute-start | bytes 786440 | tf_op jit(solution)/shard_map/ppermute | solution.py:26
  211.4 36.0 %collective-permute-start.38 = (bf16[128,1024]{1,0:T(8,128)(2,1)S(1)}, bf16[128,1024]{1,0:T(8,128)(2,1)S(1)}, u32[]{:S(2)}, u32[]{:S(2)}) collective-permute-start(bf16[128,1024]{1,0:T(8,128)(2,1)S(1)} %get-tuple-element.131), channel_id=1, source_target_pairs={{0,26},{1,27},{2,24},{3,25},{4,30},{5,31},{6,28},{7,29},{8,2},{9,3... | collective-permute-start | bytes 786440 | tf_op jit(solution)/shard_map/ppermute | solution.py:26
  218.3 31.6 %collective-permute-start.37 = (bf16[128,1024]{1,0:T(8,128)(2,1)S(1)}, bf16[128,1024]{1,0:T(8,128)(2,1)S(1)}, u32[]{:S(2)}, u32[]{:S(2)}) collective-permute-start(bf16[128,1024]{1,0:T(8,128)(2,1)S(1)} %get-tuple-element.120), channel_id=1, source_target_pairs={{0,8},{1,9},{2,10},{3,11},{4,12},{5,13},{6,14},{7,15},{8,16},{9,17... | collective-permute-start | bytes 786440 | tf_op jit(solution)/shard_map/ppermute | solution.py:26
  218.4 33.0 %collective-permute-start.34 = (bf16[128,1024]{1,0:T(8,128)(2,1)S(1)}, bf16[128,1024]{1,0:T(8,128)(2,1)S(1)}, u32[]{:S(2)}, u32[]{:S(2)}) collective-permute-start(bf16[128,1024]{1,0:T(8,128)(2,1)S(1)} %get-tuple-element.121), channel_id=1, source_target_pairs={{0,10},{1,11},{2,8},{3,9},{4,14},{5,15},{6,12},{7,13},{8,18},{9,19... | collective-permute-start | bytes 786440 | tf_op jit(solution)/shard_map/ppermute | solution.py:26
  225.0 26.5 %collective-permute-start.35 = (bf16[128,1024]{1,0:T(8,128)(2,1)S(1)}, bf16[128,1024]{1,0:T(8,128)(2,1)S(1)}, u32[]{:S(2)}, u32[]{:S(2)}) collective-permute-start(bf16[128,1024]{1,0:T(8,128)(2,1)S(1)} %get-tuple-element.122), channel_id=1, source_target_pairs={{0,9},{1,10},{2,11},{3,8},{4,13},{5,14},{6,15},{7,12},{8,17},{9,18... | collective-permute-start | bytes 786440 | tf_op jit(solution)/shard_map/ppermute | solution.py:26
  (34 other events, 329.7 us)
where the time goes:
time: 261 us; the launch traced here: 259 us
  starting transfers between devices  103 us (39%)
  waiting for transfers between devices  96.6 us (37%)
  other arithmetic  19.9 us (8%)
  matrix products  18.6 us (7%)
  local copies, waits for them, and re-layouts  9.71 us (4%)
  Pallas kernels  6.78 us (3%)
  between operations  4.28 us (2%)
    ppermute x42, starting transfers between devices, move(): return lax.ppermute(value, AXES, pairs)  103 us
    ppermute x42, waiting for transfers between devices, move(): return lax.ppermute(value, AXES, pairs)  96.6 us
    unnamed x48, local copies, waits for them, and re-layouts  7.49 us
    dot_general x4, matrix products, cut(): jnp.dot(placer, block, preferred_element_type=F32).astype(BF16)  6.86 us
    convert_element_type x3, other arithmetic, sums(): right, left = (right.astype(BF16), left.astype(BF16))  5.79 us
    pallas_call x2, Pallas kernels, finish(): pl.pallas_call(finish_kernel, out_shape=jax.ShapeDtypeStruct((1, tokens,...  5.68 us
  transfers between devices with their start and end apart: 42, of which 15 were waited for; matrix products, arithmetic and copies ran while one was open for 14% of the time, Pallas kernels for 1%

commit v1 on v0

--- a/solution.py
+++ b/solution.py
@@ -298,10 +298,13 @@
     )
     small_next = move(small_wait, by_pp=1)
     route_b_next = move(route_wait, by_pp=-1)
-    rows_a = by_node(own_a, got_ax, 1).reshape(-1, column)
-    part_a = jnp.dot(rows_a, w_gu, preferred_element_type=F32).astype(BF16)
-    *back_b, part_a, small_next, route_b_next = join(*back_b, part_a, small_next, route_b_next)
-    part_a = part_a.reshape(shape + (2 * hidden_units,))
+    part_a = []
+    for m in range(4):
+        rows = by_node(own_a[m], got_ax[m], 0).reshape(-1, column)
+        part = jnp.dot(rows, w_gu, preferred_element_type=F32).astype(BF16)
+        part_a.append(part.reshape(2, capacity, 2 * hidden_units))
+    r, l, *part_a, small_next, route_b_next = join(*back_b, *part_a, small_next, route_b_next)
+    back_b = [r, l]
     chain_a = sums(lambda slot: part_a[slot])
     values_b, back_b = turn(chain_b, back_b)
     pieces = next(chain_a)

time: 261 us -> 261 us (level)
  local copies, waits for them, and re-layouts: 9.71 us -> 6 us
  matrix products: 18.6 us -> 22.3 us
    dot_general x1 -> x4, matrix products: 3.1 us -> 6.83 us  [body_pair(): part = jnp.dot(rows, w_gu, preferred_element_type=F32).astype(BF16)]
    unnamed x48 -> x36, local copies, waits for them, and re-layouts: 7.49 us -> 5.4 us
  transfers between devices with their start and end apart: 42 -> 42, of which waited for: 15 -> 16; matrix products, arithmetic and copies ran while one was open for 14% -> 16% of each run, Pallas kernels for 1% -> 1%
where the time goes in v1:
time: 261 us; the launch traced here: 259 us
  starting transfers between devices  104 us (40%)
  waiting for transfers between devices  95.4 us (37%)
  matrix products  22.3 us (9%)
  other arithmetic  21.1 us (8%)
  Pallas kernels  6.78 us (3%)
  local copies, waits for them, and re-layouts  6 us (2%)
  between operations  3.98 us (2%)
    ppermute x42, starting transfers between devices, move(): return lax.ppermute(value, AXES, pairs)  104 us
    ppermute x42, waiting for transfers between devices, move(): return lax.ppermute(value, AXES, pairs)  95.4 us
    dot_general x4, matrix products, body_pair(): part = jnp.dot(rows, w_gu, preferred_element_type=F32).astype(BF16)  6.83 us
    dot_general x4, matrix products, cut(): jnp.dot(placer, block, preferred_element_type=F32).astype(BF16)  6.82 us
    convert_element_type x3, other arithmetic, sums(): right, left = (right.astype(BF16), left.astype(BF16))  5.92 us
    pallas_call x2, Pallas kernels, finish(): pl.pallas_call(finish_kernel, out_shape=jax.ShapeDtypeStruct((1, tokens,...  5.69 us
    unnamed x36, local copies, waits for them, and re-layouts  5.4 us
  transfers between devices with their start and end apart: 42, of which 16 were waited for; matrix products, arithmetic and copies ran while one was open for 16% of the time, Pallas kernels for 1%

profile of v1, /device:TPU:0, one launch (start us, length us, event | category | flops | bytes accessed | tf_op | source)
XLA Modules:
  0.0 259.1 jit_solution(12348207228285721355)
XLA Ops:
  4.5 4.1 %collective-permute-start = (bf16[128,1024]{1,0:T(8,128)(2,1)S(1)}, bf16[128,1024]{1,0:T(8,128)(2,1)}, u32[]{:S(2)}, u32[]{:S(2)}) collective-permute-start(bf16[128,1024]{1,0:T(8,128)(2,1)S(1)} %get-tuple-element.59), channel_id=1, source_target_pairs={{0,2},{1,3},{2,0},{3,1},{4,6},{5,7},{6,4},{7,5},{8,10},{9,11},{10,... | collective-permute-start | bytes 786440 | tf_op jit(solution)/shard_map/ppermute | solution.py:26
  31.6 6.0 %collective-permute-start.9 = (bf16[128,1024]{1,0:T(8,128)(2,1)S(1)}, bf16[128,1024]{1,0:T(8,128)(2,1)S(1)}, u32[]{:S(2)}, u32[]{:S(2)}) collective-permute-start(bf16[128,1024]{1,0:T(8,128)(2,1)S(1)} %copy-done.15), channel_id=1, source_target_pairs={{0,2},{1,3},{2,0},{3,1},{4,6},{5,7},{6,4},{7,5},{8,10},{9,11},{10,... | collective-permute-start | bytes 786440 | tf_op jit(solution)/shard_map/ppermute | solution.py:26
  40.7 4.5 %collective-permute-done.5 = bf16[4,80,1024]{2,1,0:T(8,128)(2,1)S(1)} collective-permute-done((bf16[4,80,1024]{2,1,0:T(8,128)(2,1)S(1)}, bf16[4,80,1024]{2,1,0:T(8,128)(2,1)S(1)}, u32[]{:S(2)}, u32[]{:S(2)}) %collective-permute-start.5) | collective-permute-done | bytes 655392 | tf_op jit(solution)/shard_map/ppermute | solution.py:26
  47.2 3.2 %collective-permute-start.8 = (bf16[2,80,1024]{2,1,0:T(8,128)(2,1)S(1)}, bf16[2,80,1024]{2,1,0:T(8,128)(2,1)S(1)}, u32[]{:S(2)}, u32[]{:S(2)}) collective-permute-start(bf16[2,80,1024]{2,1,0:T(8,128)(2,1)S(1)} %bitcast.225), channel_id=1, source_target_pairs={{0,3},{1,0},{2,1},{3,2},{4,7},{5,4},{6,5},{7,6},{8,11},{9,8},{10,9... | collective-permute-start | bytes 983048 | tf_op jit(solution)/shard_map/ppermute | solution.py:26
  50.4 2.4 collective-permute-start.7
  52.9 4.0 %collective-permute-start.6 = (bf16[2,80,1024]{2,1,0:T(8,128)(2,1)S(1)}, bf16[2,80,1024]{2,1,0:T(8,128)(2,1)S(1)}, u32[]{:S(2)}, u32[]{:S(2)}) collective-permute-start(bf16[2,80,1024]{2,1,0:T(8,128)(2,1)S(1)} %bitcast.223), channel_id=1, source_target_pairs={{0,2},{1,3},{2,0},{3,1},{4,6},{5,7},{6,4},{7,5},{8,10},{9,11},{10,... | collective-permute-start | bytes 983048 | tf_op jit(solution)/shard_map/ppermute | solution.py:26
  58.4 10.4 %collective-permute-done.8 = bf16[2,80,1024]{2,1,0:T(8,128)(2,1)S(1)} collective-permute-done((bf16[2,80,1024]{2,1,0:T(8,128)(2,1)S(1)}, bf16[2,80,1024]{2,1,0:T(8,128)(2,1)S(1)}, u32[]{:S(2)}, u32[]{:S(2)}) %collective-permute-start.8) | collective-permute-done | bytes 327712 | tf_op jit(solution)/shard_map/ppermute | solution.py:26
  68.8 3.2 %collective-permute-done.7 = bf16[2,80,1024]{2,1,0:T(8,128)(2,1)S(1)} collective-permute-done((bf16[2,80,1024]{2,1,0:T(8,128)(2,1)S(1)}, bf16[2,80,1024]{2,1,0:T(8,128)(2,1)S(1)}, u32[]{:S(2)}, u32[]{:S(2)}) %collective-permute-start.7) | collective-permute-done | bytes 327712 | tf_op jit(solution)/shard_map/ppermute | solution.py:26
  72.0 16.8 %collective-permute-done.6 = bf16[2,80,1024]{2,1,0:T(8,128)(2,1)S(1)} collective-permute-done((bf16[2,80,1024]{2,1,0:T(8,128)(2,1)S(1)}, bf16[2,80,1024]{2,1,0:T(8,128)(2,1)S(1)}, u32[]{:S(2)}, u32[]{:S(2)}) %collective-permute-start.6) | collective-permute-done | bytes 327712 | tf_op jit(solution)/shard_map/ppermute | solution.py:26
  92.4 5.4 %collective-permute-start.12 = (bf16[2,80,2048]{2,1,0:T(8,128)(2,1)S(1)}, bf16[2,80,2048]{2,1,0:T(8,128)(2,1)}, u32[]{:S(2)}, u32[]{:S(2)}) collective-permute-start(bf16[2,80,2048]{2,1,0:T(8,128)(2,1)S(1)} %pad_maximum_fusion.5), channel_id=1, source_target_pairs={{0,1},{1,2},{2,3},{4,5},{5,6},{6,7},{8,9},{9,10},{10,11},{12,13},{... | collective-permute-start | bytes 1966088 | tf_op jit(solution)/shard_map/ppermute | solution.py:26
  98.3 7.4 %collective-permute-done.14 = bf16[4,80,1024]{2,1,0:T(8,128)(2,1)S(1)} collective-permute-done((bf16[4,80,1024]{2,1,0:T(8,128)(2,1)S(1)}, bf16[4,80,1024]{2,1,0:T(8,128)(2,1)S(1)}, u32[]{:S(2)}, u32[]{:S(2)}) %collective-permute-start.14) | collective-permute-done | bytes 655392 | tf_op jit(solution)/shard_map/ppermute | solution.py:26
  112.8 3.0 %collective-permute-start.20 = (bf16[2,80,2048]{2,1,0:T(8,128)(2,1)}, bf16[2,80,2048]{2,1,0:T(8,128)(2,1)}, u32[]{:S(2)}, u32[]{:S(2)}) collective-permute-start(bf16[2,80,2048]{2,1,0:T(8,128)(2,1)} %bitcast.48), channel_id=1, source_target_pairs={{0,1},{4,5},{8,9},{12,13},{16,17},{20,21},{24,25},{28,29}} | collective-permute-start | bytes 1966088 | tf_op jit(solution)/shard_map/ppermute | solution.py:26
  121.5 6.6 %collective-permute-done.20 = bf16[2,80,2048]{2,1,0:T(8,128)(2,1)} collective-permute-done((bf16[2,80,2048]{2,1,0:T(8,128)(2,1)}, bf16[2,80,2048]{2,1,0:T(8,128)(2,1)}, u32[]{:S(2)}, u32[]{:S(2)}) %collective-permute-start.20) | collective-permute-done | bytes 655392 | tf_op jit(solution)/shard_map/ppermute | solution.py:26
  128.1 3.0 %fusion.36 = (bf16[2,80,2048]{2,1,0:T(8,128)(2,1)}, bf16[2,80,2048]{2,1,0:T(8,128)(2,1)}) fusion(bf16[2,80,2048]{2,1,0:T(8,128)(2,1)} %bitcast.209, bf16[2,80,2048]{2,1,0:T(8,128)(2,1)} %collective-permute-done.21, bf16[2,80,2048]{2,1,0:T(8,128)(2,1)} %collective-permute-done.20), kind=kLoop, calls=%fused_computation.26 | loop fusion | flops 2293760 | bytes 3276800 | tf_op jit(solution)/shard_map/convert_element_type | solution.py:84
  132.5 5.0 %collective-permute-start.22 = (bf16[2,80,2048]{2,1,0:T(8,128)(2,1)}, bf16[2,80,2048]{2,1,0:T(8,128)(2,1)}, u32[]{:S(2)}, u32[]{:S(2)}) collective-permute-start(bf16[2,80,2048]{2,1,0:T(8,128)(2,1)} %get-tuple-element.145), channel_id=1, source_target_pairs={{0,1},{1,2},{4,5},{5,6},{8,9},{9,10},{12,13},{13,14},{16,17},{17,1... | collective-permute-start | bytes 1966088 | tf_op jit(solution)/shard_map/ppermute | solution.py:26
  143.8 5.1 %collective-permute-done.22 = bf16[2,80,2048]{2,1,0:T(8,128)(2,1)} collective-permute-done((bf16[2,80,2048]{2,1,0:T(8,128)(2,1)}, bf16[2,80,2048]{2,1,0:T(8,128)(2,1)}, u32[]{:S(2)}, u32[]{:S(2)}) %collective-permute-start.22) | collective-permute-done | bytes 655392 | tf_op jit(solution)/shard_map/ppermute | solution.py:26
  153.2 7.5 %collective-permute-start.24 = (bf16[2,80,2048]{2,1,0:T(8,128)(2,1)S(1)}, bf16[2,80,2048]{2,1,0:T(8,128)(2,1)S(1)}, u32[]{:S(2)}, u32[]{:S(2)}) collective-permute-start(bf16[2,80,2048]{2,1,0:T(8,128)(2,1)S(1)} %add_convert_fusion.1), channel_id=1, source_target_pairs={{0,1},{1,2},{2,3},{4,5},{5,6},{6,7},{8,9},{9,10},{10,11},{12,13},{... | collective-permute-start | bytes 1966088 | tf_op jit(solution)/shard_map/ppermute | solution.py:26
  164.2 2.9 %fusion.26 = bf16[640,1024]{1,0:T(8,128)(2,1)S(1)} fusion(bf16[640,2048]{1,0:T(8,128)(2,1)S(1)} %bitcast.207, bf16[1,1,1024,2048]{3,2,1,0:T(8,128)(2,1)S(1)} %copy-done.7), kind=kOutput, calls=%fused_computation.22 | convolution fusion | flops 2685009920 | bytes 8126464 | tf_op jit(solution)/shard_map/dot_general | solution.py:51
  168.4 4.9 %collective-permute-done.25 = bf16[2,80,2048]{2,1,0:T(8,128)(2,1)S(1)} collective-permute-done((bf16[2,80,2048]{2,1,0:T(8,128)(2,1)S(1)}, bf16[2,80,2048]{2,1,0:T(8,128)(2,1)S(1)}, u32[]{:S(2)}, u32[]{:S(2)}) %collective-permute-start.25) | collective-permute-done | bytes 655392 | tf_op jit(solution)/shard_map/ppermute | solution.py:26
  175.5 3.7 %collective-permute-start.27 = (bf16[2,80,1024]{2,1,0:T(8,128)(2,1)S(1)}, bf16[2,80,1024]{2,1,0:T(8,128)(2,1)S(1)}, u32[]{:S(2)}, u32[]{:S(2)}) collective-permute-start(bf16[2,80,1024]{2,1,0:T(8,128)(2,1)S(1)} %fusion.45), channel_id=1, source_target_pairs={{0,2},{1,3},{2,0},{3,1},{4,6},{5,7},{6,4},{7,5},{8,10},{9,11},{10,... | collective-permute-start | bytes 983048 | tf_op jit(solution)/shard_map/ppermute | solution.py:26
  181.4 2.6 collective-permute-done.32
  184.2 17.5 %collective-permute-done.27 = bf16[2,80,1024]{2,1,0:T(8,128)(2,1)S(1)} collective-permute-done((bf16[2,80,1024]{2,1,0:T(8,128)(2,1)S(1)}, bf16[2,80,1024]{2,1,0:T(8,128)(2,1)S(1)}, u32[]{:S(2)}, u32[]{:S(2)}) %collective-permute-start.27) | collective-permute-done | bytes 327712 | tf_op jit(solution)/shard_map/ppermute | solution.py:26
  205.1 2.2 collective-permute-start.40
  207.3 3.9 %collective-permute-start.39 = (bf16[128,1024]{1,0:T(8,128)(2,1)S(1)}, bf16[128,1024]{1,0:T(8,128)(2,1)S(1)}, u32[]{:S(2)}, u32[]{:S(2)}) collective-permute-start(bf16[128,1024]{1,0:T(8,128)(2,1)S(1)} %get-tuple-element.138), channel_id=1, source_target_pairs={{0,25},{1,26},{2,27},{3,24},{4,29},{5,30},{6,31},{7,28},{8,1},{9,2... | collective-permute-start | bytes 786440 | tf_op jit(solution)/shard_map/ppermute | solution.py:26
  211.2 3.5 %collective-permute-start.38 = (bf16[128,1024]{1,0:T(8,128)(2,1)S(1)}, bf16[128,1024]{1,0:T(8,128)(2,1)S(1)}, u32[]{:S(2)}, u32[]{:S(2)}) collective-permute-start(bf16[128,1024]{1,0:T(8,128)(2,1)S(1)} %get-tuple-element.139), channel_id=1, source_target_pairs={{0,26},{1,27},{2,24},{3,25},{4,30},{5,31},{6,28},{7,29},{8,2},{9,3... | collective-permute-start | bytes 786440 | tf_op jit(solution)/shard_map/ppermute | solution.py:26
  214.7 4.1 %collective-permute-done.33 = bf16[4,80,1024]{2,1,0:T(8,128)(2,1)S(1)} collective-permute-done((bf16[4,80,1024]{2,1,0:T(8,128)(2,1)S(1)}, bf16[4,80,1024]{2,1,0:T(8,128)(2,1)S(1)}, u32[]{:S(2)}, u32[]{:S(2)}) %collective-permute-start.33) | collective-permute-done | bytes 655392 | tf_op jit(solution)/shard_map/ppermute | solution.py:26
  219.1 7.2 %collective-permute-start.34 = (bf16[128,1024]{1,0:T(8,128)(2,1)S(1)}, bf16[128,1024]{1,0:T(8,128)(2,1)S(1)}, u32[]{:S(2)}, u32[]{:S(2)}) collective-permute-start(bf16[128,1024]{1,0:T(8,128)(2,1)S(1)} %get-tuple-element.121), channel_id=1, source_target_pairs={{0,10},{1,11},{2,8},{3,9},{4,14},{5,15},{6,12},{7,13},{8,18},{9,19... | collective-permute-start | bytes 786440 | tf_op jit(solution)/shard_map/ppermute | solution.py:26
  226.3 16.6 %collective-permute-start.35 = (bf16[128,1024]{1,0:T(8,128)(2,1)S(1)}, bf16[128,1024]{1,0:T(8,128)(2,1)S(1)}, u32[]{:S(2)}, u32[]{:S(2)}) collective-permute-start(bf16[128,1024]{1,0:T(8,128)(2,1)S(1)} %get-tuple-element.122), channel_id=1, source_target_pairs={{0,9},{1,10},{2,11},{3,8},{4,13},{5,14},{6,15},{7,12},{8,17},{9,18... | collective-permute-start | bytes 786440 | tf_op jit(solution)/shard_map/ppermute | solution.py:26
  243.2 4.0 %collective-permute-done.38.refs_0_ = bf16[128,1024]{1,0:T(8,128)(2,1)S(1)} collective-permute-done((bf16[128,1024]{1,0:T(8,128)(2,1)S(1)}, bf16[128,1024]{1,0:T(8,128)(2,1)S(1)}, u32[]{:S(2)}, u32[]{:S(2)}) %collective-permute-start.38) | collective-permute-done | bytes 262176 | tf_op jit(solution)/shard_map/ppermute | solution.py:26
  247.2 2.5 finish.3
  251.3 4.5 %collective-permute-done.36.refs_2_ = bf16[128,1024]{1,0:T(8,128)(2,1)S(1)} collective-permute-done((bf16[128,1024]{1,0:T(8,128)(2,1)S(1)}, bf16[128,1024]{1,0:T(8,128)(2,1)S(1)}, u32[]{:S(2)}, u32[]{:S(2)}) %collective-permute-start.36) | collective-permute-done | bytes 262176 | tf_op jit(solution)/shard_map/ppermute | solution.py:26
  255.8 3.2 %finish.2 = bf16[1,128,4096]{2,1,0:T(8,128)(2,1)} custom-call(s32[4]{0:T(128)S(1)} %pad_add_fusion.2.at_ref, f32[1,128]{1,0:T(1,128)S(1)} %get-tuple-element.147.weight_ref, bf16[128,128]{1,0:T(8,128)(2,1)S(1)} %fusion.63.pick_ref, bf16[128,4096]{1,0:T(8,128)(2,1)} %collective-permute-done.19.residual_ref, ...), custom_call_target="tpu_custom_call" | custom-call | tf_op jit(solution)/shard_map/finish/pallas_call | solution.py:216
  (158 shorter events, 74.2 us)
Async XLA Ops:
  4.5 24.0 %collective-permute-start = (bf16[128,1024]{1,0:T(8,128)(2,1)S(1)}, bf16[128,1024]{1,0:T(8,128)(2,1)}, u32[]{:S(2)}, u32[]{:S(2)}) collective-permute-start(bf16[128,1024]{1,0:T(8,128)(2,1)S(1)} %get-tuple-element.59), channel_id=1, source_target_pairs={{0,2},{1,3},{2,0},{3,1},{4,6},{5,7},{6,4},{7,5},{8,10},{9,11},{10,... | collective-permute-start | bytes 786440 | tf_op jit(solution)/shard_map/ppermute | solution.py:26
  8.6 20.0 %collective-permute-start.1 = (bf16[128,1024]{1,0:T(8,128)(2,1)S(1)}, bf16[128,1024]{1,0:T(8,128)(2,1)}, u32[]{:S(2)}, u32[]{:S(2)}) collective-permute-start(bf16[128,1024]{1,0:T(8,128)(2,1)S(1)} %get-tuple-element.60), channel_id=1, source_target_pairs={{0,3},{1,0},{2,1},{3,2},{4,7},{5,4},{6,5},{7,6},{8,11},{9,8},{10,9... | collective-permute-start | bytes 786440 | tf_op jit(solution)/shard_map/ppermute | solution.py:26
  10.0 18.6 %collective-permute-start.2 = (bf16[128,1024]{1,0:T(8,128)(2,1)S(1)}, bf16[128,1024]{1,0:T(8,128)(2,1)}, u32[]{:S(2)}, u32[]{:S(2)}) collective-permute-start(bf16[128,1024]{1,0:T(8,128)(2,1)S(1)} %get-tuple-element.61), channel_id=1, source_target_pairs={{0,1},{1,2},{2,3},{3,0},{4,5},{5,6},{6,7},{7,4},{8,9},{9,10},{10,1... | collective-permute-start | bytes 786440 | tf_op jit(solution)/shard_map/ppermute | solution.py:26
  31.6 21.3 %collective-permute-start.9 = (bf16[128,1024]{1,0:T(8,128)(2,1)S(1)}, bf16[128,1024]{1,0:T(8,128)(2,1)S(1)}, u32[]{:S(2)}, u32[]{:S(2)}) collective-permute-start(bf16[128,1024]{1,0:T(8,128)(2,1)S(1)} %copy-done.15), channel_id=1, source_target_pairs={{0,2},{1,3},{2,0},{3,1},{4,6},{5,7},{6,4},{7,5},{8,10},{9,11},{10,... | collective-permute-start | bytes 786440 | tf_op jit(solution)/shard_map/ppermute | solution.py:26
  37.6 20.7 %collective-permute-start.10 = (bf16[128,1024]{1,0:T(8,128)(2,1)S(1)}, bf16[128,1024]{1,0:T(8,128)(2,1)S(1)}, u32[]{:S(2)}, u32[]{:S(2)}) collective-permute-start(bf16[128,1024]{1,0:T(8,128)(2,1)S(1)} %copy-done.14), channel_id=1, source_target_pairs={{0,3},{1,0},{2,1},{3,2},{4,7},{5,4},{6,5},{7,6},{8,11},{9,8},{10,9... | collective-permute-start | bytes 786440 | tf_op jit(solution)/shard_map/ppermute | solution.py:26
  38.0 20.4 %collective-permute-start.11 = (bf16[128,1024]{1,0:T(8,128)(2,1)S(1)}, bf16[128,1024]{1,0:T(8,128)(2,1)S(1)}, u32[]{:S(2)}, u32[]{:S(2)}) collective-permute-start(bf16[128,1024]{1,0:T(8,128)(2,1)S(1)} %copy-done.13), channel_id=1, source_target_pairs={{0,1},{1,2},{2,3},{3,0},{4,5},{5,6},{6,7},{7,4},{8,9},{9,10},{10,1... | collective-permute-start | bytes 786440 | tf_op jit(solution)/shard_map/ppermute | solution.py:26
  47.2 21.6 %collective-permute-start.8 = (bf16[2,80,1024]{2,1,0:T(8,128)(2,1)S(1)}, bf16[2,80,1024]{2,1,0:T(8,128)(2,1)S(1)}, u32[]{:S(2)}, u32[]{:S(2)}) collective-permute-start(bf16[2,80,1024]{2,1,0:T(8,128)(2,1)S(1)} %bitcast.225), channel_id=1, source_target_pairs={{0,3},{1,0},{2,1},{3,2},{4,7},{5,4},{6,5},{7,6},{8,11},{9,8},{10,9... | collective-permute-start | bytes 983048 | tf_op jit(solution)/shard_map/ppermute | solution.py:26
  50.4 21.6 %collective-permute-start.7 = (bf16[2,80,1024]{2,1,0:T(8,128)(2,1)S(1)}, bf16[2,80,1024]{2,1,0:T(8,128)(2,1)S(1)}, u32[]{:S(2)}, u32[]{:S(2)}) collective-permute-start(bf16[2,80,1024]{2,1,0:T(8,128)(2,1)S(1)} %bitcast.224), channel_id=1, source_target_pairs={{0,1},{1,2},{2,3},{3,0},{4,5},{5,6},{6,7},{7,4},{8,9},{9,10},{10,1... | collective-permute-start | bytes 983048 | tf_op jit(solution)/shard_map/ppermute | solution.py:26
  52.9 36.0 %collective-permute-start.6 = (bf16[2,80,1024]{2,1,0:T(8,128)(2,1)S(1)}, bf16[2,80,1024]{2,1,0:T(8,128)(2,1)S(1)}, u32[]{:S(2)}, u32[]{:S(2)}) collective-permute-start(bf16[2,80,1024]{2,1,0:T(8,128)(2,1)S(1)} %bitcast.223), channel_id=1, source_target_pairs={{0,2},{1,3},{2,0},{3,1},{4,6},{5,7},{6,4},{7,5},{8,10},{9,11},{10,... | collective-permute-start | bytes 983048 | tf_op jit(solution)/shard_map/ppermute | solution.py:26
  89.0 16.7 %collective-permute-start.14 = (bf16[4,80,1024]{2,1,0:T(8,128)(2,1)S(1)}, bf16[4,80,1024]{2,1,0:T(8,128)(2,1)S(1)}, u32[]{:S(2)}, u32[]{:S(2)}) collective-permute-start(bf16[4,80,1024]{2,1,0:T(8,128)(2,1)S(1)} %get-tuple-element.141), channel_id=1, source_target_pairs={{0,4},{1,5},{2,6},{3,7},{4,0},{5,1},{6,2},{7,3},{8,12},{9,13},{10,... | collective-permute-start | bytes 1966088 | tf_op jit(solution)/shard_map/ppermute | solution.py:26
  90.8 22.0 %collective-permute-start.13 = (bf16[2,80,2048]{2,1,0:T(8,128)(2,1)S(1)}, bf16[2,80,2048]{2,1,0:T(8,128)(2,1)}, u32[]{:S(2)}, u32[]{:S(2)}) collective-permute-start(bf16[2,80,2048]{2,1,0:T(8,128)(2,1)S(1)} %pad_maximum_fusion.5), channel_id=1, source_target_pairs={{1,0},{2,1},{3,2},{5,4},{6,5},{7,6},{9,8},{10,9},{11,10},{13,12},{... | collective-permute-start | bytes 1966088 | tf_op jit(solution)/shard_map/ppermute | solution.py:26
  92.4 20.4 %collective-permute-start.12 = (bf16[2,80,2048]{2,1,0:T(8,128)(2,1)S(1)}, bf16[2,80,2048]{2,1,0:T(8,128)(2,1)}, u32[]{:S(2)}, u32[]{:S(2)}) collective-permute-start(bf16[2,80,2048]{2,1,0:T(8,128)(2,1)S(1)} %pad_maximum_fusion.5), channel_id=1, source_target_pairs={{0,1},{1,2},{2,3},{4,5},{5,6},{6,7},{8,9},{9,10},{10,11},{12,13},{... | collective-permute-start | bytes 1966088 | tf_op jit(solution)/shard_map/ppermute | solution.py:26
  117.3 22.1 %collective-permute-start.19 = (bf16[128,4096]{1,0:T(8,128)(2,1)}, bf16[128,4096]{1,0:T(8,128)(2,1)}, u32[]{:S(2)}, u32[]{:S(2)}) collective-permute-start(bf16[128,4096]{1,0:T(8,128)(2,1)} %bitcast.54), channel_id=1, source_target_pairs={{0,8},{1,9},{2,10},{3,11},{4,12},{5,13},{6,14},{7,15},{8,16},{9,17... | collective-permute-start | bytes 3145736 | tf_op jit(solution)/shard_map/ppermute | solution.py:26
  118.5 20.3 %collective-permute-start.17 = (bf16[2,80,2048]{2,1,0:T(8,128)(2,1)}, bf16[2,80,2048]{2,1,0:T(8,128)(2,1)}, u32[]{:S(2)}, u32[]{:S(2)}) collective-permute-start(bf16[2,80,2048]{2,1,0:T(8,128)(2,1)} %collective-permute-done.12), channel_id=1, source_target_pairs={{1,2},{2,3},{5,6},{6,7},{9,10},{10,11},{13,14},{14,15},{17,18},{18... | collective-permute-start | bytes 1966088 | tf_op jit(solution)/shard_map/ppermute | solution.py:26
  120.2 19.2 %collective-permute-start.18 = (bf16[2,80,2048]{2,1,0:T(8,128)(2,1)}, bf16[2,80,2048]{2,1,0:T(8,128)(2,1)}, u32[]{:S(2)}, u32[]{:S(2)}) collective-permute-start(bf16[2,80,2048]{2,1,0:T(8,128)(2,1)} %collective-permute-done.13), channel_id=1, source_target_pairs={{1,0},{2,1},{5,4},{6,5},{9,8},{10,9},{13,12},{14,13},{17,16},{18,1... | collective-permute-start | bytes 1966088 | tf_op jit(solution)/shard_map/ppermute | solution.py:26
  132.5 16.4 %collective-permute-start.22 = (bf16[2,80,2048]{2,1,0:T(8,128)(2,1)}, bf16[2,80,2048]{2,1,0:T(8,128)(2,1)}, u32[]{:S(2)}, u32[]{:S(2)}) collective-permute-start(bf16[2,80,2048]{2,1,0:T(8,128)(2,1)} %get-tuple-element.145), channel_id=1, source_target_pairs={{0,1},{1,2},{4,5},{5,6},{8,9},{9,10},{12,13},{13,14},{16,17},{17,1... | collective-permute-start | bytes 1966088 | tf_op jit(solution)/shard_map/ppermute | solution.py:26
  139.4 21.3 %collective-permute-start.29 = (bf16[2,80,2048]{2,1,0:T(8,128)(2,1)}, bf16[2,80,2048]{2,1,0:T(8,128)(2,1)S(1)}, u32[]{:S(2)}, u32[]{:S(2)}) collective-permute-start(bf16[2,80,2048]{2,1,0:T(8,128)(2,1)} %collective-permute-done.17), channel_id=1, source_target_pairs={{2,3},{6,7},{10,11},{14,15},{18,19},{22,23},{26,27},{30,31}} | collective-permute-start | bytes 1966088 | tf_op jit(solution)/shard_map/ppermute | solution.py:26
  140.1 20.7 %collective-permute-start.30 = (bf16[2,80,2048]{2,1,0:T(8,128)(2,1)}, bf16[2,80,2048]{2,1,0:T(8,128)(2,1)S(1)}, u32[]{:S(2)}, u32[]{:S(2)}) collective-permute-start(bf16[2,80,2048]{2,1,0:T(8,128)(2,1)} %collective-permute-done.18), channel_id=1, source_target_pairs={{1,0},{5,4},{9,8},{13,12},{17,16},{21,20},{25,24},{29,28}} | collective-permute-start | bytes 1966088 | tf_op jit(solution)/shard_map/ppermute | solution.py:26
  141.4 19.4 %collective-permute-start.31 = (bf16[128,4096]{1,0:T(8,128)(2,1)S(1)}, bf16[128,4096]{1,0:T(8,128)(2,1)S(1)}, u32[]{:S(2)}, u32[]{:S(2)}) collective-permute-start(bf16[128,4096]{1,0:T(8,128)(2,1)S(1)} %bitcast.201), channel_id=1, source_target_pairs={{0,24},{1,25},{2,26},{3,27},{4,28},{5,29},{6,30},{7,31},{8,0},{9,1... | collective-permute-start | bytes 3145736 | tf_op jit(solution)/shard_map/ppermute | solution.py:26
  150.4 22.9 %collective-permute-start.25 = (bf16[2,80,2048]{2,1,0:T(8,128)(2,1)S(1)}, bf16[2,80,2048]{2,1,0:T(8,128)(2,1)S(1)}, u32[]{:S(2)}, u32[]{:S(2)}) collective-permute-start(bf16[2,80,2048]{2,1,0:T(8,128)(2,1)S(1)} %add_convert_fusion), channel_id=1, source_target_pairs={{1,0},{2,1},{3,2},{5,4},{6,5},{7,6},{9,8},{10,9},{11,10},{13,12},{... | collective-permute-start | bytes 1966088 | tf_op jit(solution)/shard_map/ppermute | solution.py:26
  153.2 21.8 %collective-permute-start.24 = (bf16[2,80,2048]{2,1,0:T(8,128)(2,1)S(1)}, bf16[2,80,2048]{2,1,0:T(8,128)(2,1)S(1)}, u32[]{:S(2)}, u32[]{:S(2)}) collective-permute-start(bf16[2,80,2048]{2,1,0:T(8,128)(2,1)S(1)} %add_convert_fusion.1), channel_id=1, source_target_pairs={{0,1},{1,2},{2,3},{4,5},{5,6},{6,7},{8,9},{9,10},{10,11},{12,13},{... | collective-permute-start | bytes 1966088 | tf_op jit(solution)/shard_map/ppermute | solution.py:26
  167.2 16.8 %collective-permute-start.32 = (bf16[4,80,1024]{2,1,0:T(8,128)(2,1)S(1)}, bf16[4,80,1024]{2,1,0:T(8,128)(2,1)S(1)}, u32[]{:S(2)}, u32[]{:S(2)}) collective-permute-start(bf16[4,80,1024]{2,1,0:T(8,128)(2,1)S(1)} %dynamic-slice_bitcast_fusion.1), channel_id=1, source_target_pairs={{0,4},{1,5},{2,6},{3,7},{4,0},{5,1},{6,2},{7,3},{8,12},{9,13},{10,... | collective-permute-start | bytes 1966088 | tf_op jit(solution)/shard_map/ppermute | solution.py:26
  175.5 26.3 %collective-permute-start.27 = (bf16[2,80,1024]{2,1,0:T(8,128)(2,1)S(1)}, bf16[2,80,1024]{2,1,0:T(8,128)(2,1)S(1)}, u32[]{:S(2)}, u32[]{:S(2)}) collective-permute-start(bf16[2,80,1024]{2,1,0:T(8,128)(2,1)S(1)} %fusion.45), channel_id=1, source_target_pairs={{0,2},{1,3},{2,0},{3,1},{4,6},{5,7},{6,4},{7,5},{8,10},{9,11},{10,... | collective-permute-start | bytes 983048 | tf_op jit(solution)/shard_map/ppermute | solution.py:26
  179.2 22.6 %collective-permute-start.26 = (bf16[2,80,1024]{2,1,0:T(8,128)(2,1)S(1)}, bf16[2,80,1024]{2,1,0:T(8,128)(2,1)S(1)}, u32[]{:S(2)}, u32[]{:S(2)}) collective-permute-start(bf16[2,80,1024]{2,1,0:T(8,128)(2,1)S(1)} %fusion.45), channel_id=1, source_target_pairs={{0,3},{1,0},{2,1},{3,2},{4,7},{5,4},{6,5},{7,6},{8,11},{9,8},{10,9... | collective-permute-start | bytes 983048 | tf_op jit(solution)/shard_map/ppermute | solution.py:26
  180.4 21.4 %collective-permute-start.28 = (bf16[2,80,1024]{2,1,0:T(8,128)(2,1)S(1)}, bf16[2,80,1024]{2,1,0:T(8,128)(2,1)S(1)}, u32[]{:S(2)}, u32[]{:S(2)}) collective-permute-start(bf16[2,80,1024]{2,1,0:T(8,128)(2,1)S(1)} %fusion.45), channel_id=1, source_target_pairs={{0,1},{1,2},{2,3},{3,0},{4,5},{5,6},{6,7},{7,4},{8,9},{9,10},{10,1... | collective-permute-start | bytes 983048 | tf_op jit(solution)/shard_map/ppermute | solution.py:26
  203.6 15.2 %collective-permute-start.33 = (bf16[4,80,1024]{2,1,0:T(8,128)(2,1)S(1)}, bf16[4,80,1024]{2,1,0:T(8,128)(2,1)S(1)}, u32[]{:S(2)}, u32[]{:S(2)}) collective-permute-start(bf16[4,80,1024]{2,1,0:T(8,128)(2,1)S(1)} %dynamic-slice_bitcast_fusion), channel_id=1, source_target_pairs={{0,4},{1,5},{2,6},{3,7},{4,0},{5,1},{6,2},{7,3},{8,12},{9,13},{10,... | collective-permute-start | bytes 1966088 | tf_op jit(solution)/shard_map/ppermute | solution.py:26
  205.1 21.2 %collective-permute-start.40 = (bf16[128,1024]{1,0:T(8,128)(2,1)S(1)}, bf16[128,1024]{1,0:T(8,128)(2,1)S(1)}, u32[]{:S(2)}, u32[]{:S(2)}) collective-permute-start(bf16[128,1024]{1,0:T(8,128)(2,1)S(1)} %get-tuple-element.137), channel_id=1, source_target_pairs={{0,27},{1,24},{2,25},{3,26},{4,31},{5,28},{6,29},{7,30},{8,3},{9,0... | collective-permute-start | bytes 786440 | tf_op jit(solution)/shard_map/ppermute | solution.py:26
  207.3 35.6 %collective-permute-start.39 = (bf16[128,1024]{1,0:T(8,128)(2,1)S(1)}, bf16[128,1024]{1,0:T(8,128)(2,1)S(1)}, u32[]{:S(2)}, u32[]{:S(2)}) collective-permute-start(bf16[128,1024]{1,0:T(8,128)(2,1)S(1)} %get-tuple-element.138), channel_id=1, source_target_pairs={{0,25},{1,26},{2,27},{3,24},{4,29},{5,30},{6,31},{7,28},{8,1},{9,2... | collective-permute-start | bytes 786440 | tf_op jit(solution)/shard_map/ppermute | solution.py:26
  211.2 36.0 %collective-permute-start.38 = (bf16[128,1024]{1,0:T(8,128)(2,1)S(1)}, bf16[128,1024]{1,0:T(8,128)(2,1)S(1)}, u32[]{:S(2)}, u32[]{:S(2)}) collective-permute-start(bf16[128,1024]{1,0:T(8,128)(2,1)S(1)} %get-tuple-element.139), channel_id=1, source_target_pairs={{0,26},{1,27},{2,24},{3,25},{4,30},{5,31},{6,28},{7,29},{8,2},{9,3... | collective-permute-start | bytes 786440 | tf_op jit(solution)/shard_map/ppermute | solution.py:26
  219.0 30.7 %collective-permute-start.37 = (bf16[128,1024]{1,0:T(8,128)(2,1)S(1)}, bf16[128,1024]{1,0:T(8,128)(2,1)S(1)}, u32[]{:S(2)}, u32[]{:S(2)}) collective-permute-start(bf16[128,1024]{1,0:T(8,128)(2,1)S(1)} %get-tuple-element.120), channel_id=1, source_target_pairs={{0,8},{1,9},{2,10},{3,11},{4,12},{5,13},{6,14},{7,15},{8,16},{9,17... | collective-permute-start | bytes 786440 | tf_op jit(solution)/shard_map/ppermute | solution.py:26
  219.1 32.2 %collective-permute-start.34 = (bf16[128,1024]{1,0:T(8,128)(2,1)S(1)}, bf16[128,1024]{1,0:T(8,128)(2,1)S(1)}, u32[]{:S(2)}, u32[]{:S(2)}) collective-permute-start(bf16[128,1024]{1,0:T(8,128)(2,1)S(1)} %get-tuple-element.121), channel_id=1, source_target_pairs={{0,10},{1,11},{2,8},{3,9},{4,14},{5,15},{6,12},{7,13},{8,18},{9,19... | collective-permute-start | bytes 786440 | tf_op jit(solution)/shard_map/ppermute | solution.py:26
  226.3 24.9 %collective-permute-start.35 = (bf16[128,1024]{1,0:T(8,128)(2,1)S(1)}, bf16[128,1024]{1,0:T(8,128)(2,1)S(1)}, u32[]{:S(2)}, u32[]{:S(2)}) collective-permute-start(bf16[128,1024]{1,0:T(8,128)(2,1)S(1)} %get-tuple-element.122), channel_id=1, source_target_pairs={{0,9},{1,10},{2,11},{3,8},{4,13},{5,14},{6,15},{7,12},{8,17},{9,18... | collective-permute-start | bytes 786440 | tf_op jit(solution)/shard_map/ppermute | solution.py:26
  (28 other events, 303.6 us)

commit v2 on v0

--- a/solution.py
+++ b/solution.py
@@ -239,7 +239,7 @@
 
     act, grad = act_fwd[0], grad_bwd[0]
     route_a, route_b = routes_fwd[0, :, 0], routes_bwd[0, :, 0]
-    sort_a, sort_b = sorter(route_a), sorter(route_b)
+    sort_b = sorter(route_b)
     zeros = tokens_here - jnp.stack([jnp.sum(route_a), jnp.sum(route_b)]).astype(F32)
 
     def in_rows(cuts, got):
@@ -257,30 +257,47 @@
         pieces = chain.send(after(back, *others))
         return operands(pieces), send(pieces)
 
-    cut_b = scaled_cut(grad, weight_bwd[0], route_b, local)
-    c1, c2, c3, saved_in = join(*cut_b[1:], saved_bwd[0])
-    got_b = [move(c2, by_local=-2), move(c1, by_local=-1), move(c3, by_local=-3)]
+    cut_a = scaled_cut(act, jnp.ones((tokens_here,), F32), route_a, local)
+    c1, c2, c3, saved_in, grad_in = join(*cut_a[1:], saved_bwd[0], grad)
+    got_a = [move(c2, by_local=-2), move(c1, by_local=-1), move(c3, by_local=-3)]
     saved = jnp.dot(sort_b, saved_in, preferred_element_type=F32).astype(BF16)
     saved_own, saved_other = windows(saved, node, capacity)
     saved_got = move(saved_other, by_node=1)
-    (zeros_wait,) = after([zeros], saved_other)
-    zeros_got = move(zeros_wait, by_node=1)
-    cut_a = cut(act, sort_a, local)
-    *got_b, saved_got, zeros_got, a0, a1, a2, a3 = join(*got_b, saved_got, zeros_got, *cut_a)
-    cut_a = [a0, a1, a2, a3]
+    zeros_got = move(zeros, by_node=1)
+    cut_b = scaled_cut(grad_in, weight_bwd[0], route_b, local)
+    *got_a, saved_got, zeros_got, b0, b1, b2, b3 = join(*got_a, saved_got, zeros_got, *cut_b)
+    cut_b = [b0, b1, b2, b3]
     zeros = by_node(zeros, zeros_got, 0)
-    got_a = [move(cut_a[m], by_local=-m) for m in (2, 1, 3)]
+    got_b = [move(cut_b[m], by_local=-m) for m in (2, 1, 3)]
+    own_a, other_a = in_rows(cut_a, got_a)
+    column = own_a.shape[-1]
+    got_ax = move(other_a, by_node=1)
+    *got_b, got_ax, act_in, small, route_in, grad_in = join(
+        *got_b, got_ax, act, jnp.stack([route_a.astype(F32), weight_fwd[0]]), route_b, grad
+    )
+
     own_b, other_b = in_rows(cut_b, got_b)
-    column = own_b.shape[-1]
     got_bx = move(other_b, by_node=1)
-
+    part_a = []
+    for m in range(4):
+        rows = by_node(own_a[m], got_ax[m], 0).reshape(-1, column)
+        part = jnp.dot(rows, w_gu, preferred_element_type=F32).astype(BF16)
+        part_a.append(part.reshape(2, capacity, 2 * hidden_units))
+    chain_a = sums(lambda slot: part_a[slot])
+    back_a = send(next(chain_a))
+    act_next = move(act_in, by_pp=1)
+    *back_a, got_bx, act_next = join(*back_a, got_bx, act_next)
+
+    back_a = send(chain_a.send(back_a))
     rows_b = by_node(own_b, got_bx, 1).reshape(-1, column)
     part_b = dot_t(rows_b, w_dn).astype(BF16).reshape(shape + (hidden_units,))
     back_b = [move(part_b[m], by_local=m) for m in (2, 1, 3)]
-    both = join(*back_b, *got_a)
-    back_b, got_a = both[:3], both[3:]
-    own_a, other_a = in_rows(cut_a, got_a)
-    got_ax = move(other_a, by_node=1)
+    back_a = send(chain_a.send(back_a))
+    preact = chain_a.send(back_a)
+    preact = jnp.where(valid(zeros[:, 0], node, tokens_here, capacity)[..., None], preact, 0.0)
+    hidden = (jax.nn.silu(preact[..., :hidden_units]) * preact[..., hidden_units:]).astype(BF16)
+    all_hidden = [move(hidden, by_local=-m) for m in (1, 2, 3)]
+
     dh = part_b[0].astype(F32) + sum(part.astype(F32) for part in back_b)
     dh = jnp.where(valid(zeros[:, 1], node, tokens_here, capacity)[..., None], dh, 0.0)
     saved_rows = by_node(saved_own, saved_got, 0)
@@ -293,51 +310,36 @@
 
     chain_b = gathers(grad_gu, local)
     back_b = send(next(chain_b))
-    small_wait, route_wait = after(
-        [jnp.stack([route_a.astype(F32), weight_fwd[0]]), route_b], grad_gu
-    )
-    small_next = move(small_wait, by_pp=1)
-    route_b_next = move(route_wait, by_pp=-1)
-    rows_a = by_node(own_a, got_ax, 1).reshape(-1, column)
-    part_a = jnp.dot(rows_a, w_gu, preferred_element_type=F32).astype(BF16)
-    *back_b, part_a, small_next, route_b_next = join(*back_b, part_a, small_next, route_b_next)
-    part_a = part_a.reshape(shape + (2 * hidden_units,))
-    chain_a = sums(lambda slot: part_a[slot])
-    values_b, back_b = turn(chain_b, back_b)
-    pieces = next(chain_a)
-    back_a = send(pieces)
-    act_next = move(after([act], *operands(pieces))[0], by_pp=1)
-    *back_b, act_next = join(*back_b, act_next)
-    values_b, back_b = turn(chain_b, back_b)
-    grad_next = move(join(grad, *values_b)[0], by_pp=-1)
-    *back_b, grad_next = join(*back_b, grad_next)
-    values_a, back_a = turn(chain_a, back_a)
-    values_a, back_a = turn(chain_a, back_a)
-    all_gu = chain_b.send(back_b)
-    done_b = dot_t(all_gu.reshape(-1, 2 * hidden_units), w_gu).astype(BF16)
-    own_b, other_b = split(done_b.reshape(shape + (column,)))
-    got_b = move(other_b, by_node=1)
-
-    preact = chain_a.send(back_a)
-    preact = jnp.where(valid(zeros[:, 0], node, tokens_here, capacity)[..., None], preact, 0.0)
-    hidden = (jax.nn.silu(preact[..., :hidden_units]) * preact[..., hidden_units:]).astype(BF16)
-    all_hidden = [move(hidden, by_local=-m) for m in (1, 2, 3)]
-    merged_b = merge(own_b, got_b, node, tokens_here)
-    h1, h2, h3, merged_b = join(*all_hidden, merged_b)
+    *back_b, h1, h2, h3, small, route_in, grad_in = join(
+        *back_b, *all_hidden, small, route_in, grad_in
+    )
+    back_b = send(chain_b.send(back_b))
     all_hidden = jnp.stack([hidden, h1, h2, h3])
-    home_b = send(homeward(merged_b, -1))
     done_a = jnp.dot(
         all_hidden.reshape(-1, hidden_units), w_dn, preferred_element_type=F32
     ).astype(BF16)
     own_a, other_a = split(done_a.reshape(shape + (column,)))
     got_a = move(other_a, by_node=1)
+    small_next = move(small, by_pp=1)
+    route_b_next = move(route_in, by_pp=-1)
+    *back_b, got_a, small_next, route_b_next = join(*back_b, got_a, small_next, route_b_next)
+    back_b = send(chain_b.send(back_b))
     home_a = send(homeward(merge(own_a, got_a, node, tokens_here), 1))
+    *back_b, h0, h1, h2, h3 = join(*back_b, *home_a)
+    home_a = [h0, h1, h2, h3]
+    grad_next = move(grad_in, by_pp=-1)
+    all_gu = chain_b.send(back_b)
+    done_b = dot_t(all_gu.reshape(-1, 2 * hidden_units), w_gu).astype(BF16)
+    own_b, other_b = split(done_b.reshape(shape + (column,)))
+    got_b = move(other_b, by_node=1)
+    got_b, grad_next = join(got_b, grad_next)
+    home_b = send(homeward(merge(own_b, got_b, node, tokens_here), -1))
 
     at = jnp.stack([(local - m) % 4 for m in (2, 1, 3, 0)]).astype(jnp.int32)
+    place_a = sorted_places(small_next[0].astype(jnp.int32))
+    next_input = finish(act_next, small_next[1], place_a, home_a, at)
     ones = jnp.ones((tokens_here,), F32)
     prev_grad = finish(grad_next, ones, sorted_places(route_b_next), home_b, at)
-    place_a = sorted_places(small_next[0].astype(jnp.int32))
-    next_input = finish(act_next, small_next[1], place_a, home_a, at)
     return next_input, prev_grad
 
 

time: 261 us -> 313 us (1.20)
  waiting for transfers between devices: 96.6 us -> 168 us
  starting transfers between devices: 103 us -> 83.8 us
  matrix products: 18.6 us -> 12 us
  other arithmetic: 19.9 us -> 25.1 us
    ppermute x42, waiting for transfers between devices: 96.6 us -> 168 us  [move(): return lax.ppermute(value, AXES, pairs)]
    ppermute x42, starting transfers between devices: 103 us -> 83.8 us  [move(): return lax.ppermute(value, AXES, pairs)]
    dot_general x5 -> x4, matrix products: 9.95 us -> 3.49 us  [body_pair(): part = jnp.dot(rows, w_gu, preferred_element_type=F32).astype(BF16)]
    convert_element_type x3, other arithmetic: 5.79 us -> 0.8 us  [sums(): right, left = (right.astype(BF16), left.astype(BF16))]
    unnamed x48 -> x62, local copies, waits for them, and re-layouts: 7.49 us -> 8.57 us
  transfers between devices with their start and end apart: 42 -> 42, of which waited for: 15 -> 20; matrix products, arithmetic and copies ran while one was open for 14% -> 8% of each run, Pallas kernels for 1% -> 1%
where the time goes in v2:
time: 313 us; the launch traced here: 310 us
  waiting for transfers between devices  168 us (54%)
  starting transfers between devices  83.8 us (27%)
  other arithmetic  25.1 us (8%)
  matrix products  12 us (4%)
  local copies, waits for them, and re-layouts  9.1 us (3%)
  Pallas kernels  7.89 us (3%)
  between operations  3.57 us (1%)
    ppermute x42, waiting for transfers between devices, move(): return lax.ppermute(value, AXES, pairs)  168 us
    ppermute x42, starting transfers between devices, move(): return lax.ppermute(value, AXES, pairs)  83.8 us
    unnamed x62, local copies, waits for them, and re-layouts  8.57 us
  transfers between devices with their start and end apart: 42, of which 20 were waited for; matrix products, arithmetic and copies ran while one was open for 8% of the time, Pallas kernels for 1%

profile of v2, /device:TPU:0, one launch (start us, length us, event | category | flops | bytes accessed | tf_op | source)
XLA Modules:
  0.0 309.7 jit_solution(8908643783913592740)
XLA Ops:
  10.3 2.9 collective-permute-start.3
  13.3 2.6 collective-permute-start
  24.3 10.4 %collective-permute-done = bf16[128,1024]{1,0:T(8,128)(2,1)} collective-permute-done((bf16[128,1024]{1,0:T(8,128)(2,1)}, bf16[128,1024]{1,0:T(8,128)(2,1)}, u32[]{:S(2)}, u32[]{:S(2)}) %collective-permute-start) | collective-permute-done | bytes 262176 | tf_op jit(solution)/shard_map/ppermute | solution.py:26
  36.6 7.1 %collective-permute-start.5 = (bf16[128,1024]{1,0:T(8,128)(2,1)S(1)}, bf16[128,1024]{1,0:T(8,128)(2,1)S(1)}, u32[]{:S(2)}, u32[]{:S(2)}) collective-permute-start(bf16[128,1024]{1,0:T(8,128)(2,1)S(1)} %get-tuple-element.71), channel_id=1, source_target_pairs={{0,2},{1,3},{2,0},{3,1},{4,6},{5,7},{6,4},{7,5},{8,10},{9,11},{10,... | collective-permute-start | bytes 786440 | tf_op jit(solution)/shard_map/ppermute | solution.py:26
  48.4 8.6 %collective-permute-done.5 = bf16[128,1024]{1,0:T(8,128)(2,1)S(1)} collective-permute-done((bf16[128,1024]{1,0:T(8,128)(2,1)S(1)}, bf16[128,1024]{1,0:T(8,128)(2,1)S(1)}, u32[]{:S(2)}, u32[]{:S(2)}) %collective-permute-start.5) | collective-permute-done | bytes 262176 | tf_op jit(solution)/shard_map/ppermute | solution.py:26
  57.1 5.3 %collective-permute-done.6 = bf16[128,1024]{1,0:T(8,128)(2,1)S(1)} collective-permute-done((bf16[128,1024]{1,0:T(8,128)(2,1)S(1)}, bf16[128,1024]{1,0:T(8,128)(2,1)S(1)}, u32[]{:S(2)}, u32[]{:S(2)}) %collective-permute-start.6) | collective-permute-done | bytes 262176 | tf_op jit(solution)/shard_map/ppermute | solution.py:26
  67.2 7.0 %collective-permute-start.9 = (bf16[2,80,2048]{2,1,0:T(8,128)(2,1)S(1)}, bf16[2,80,2048]{2,1,0:T(8,128)(2,1)S(1)}, u32[]{:S(2)}, u32[]{:S(2)}) collective-permute-start(bf16[2,80,2048]{2,1,0:T(8,128)(2,1)S(1)} %bitcast.189), channel_id=1, source_target_pairs={{0,1},{4,5},{8,9},{12,13},{16,17},{20,21},{24,25},{28,29}} | collective-permute-start | bytes 1966088 | tf_op jit(solution)/shard_map/ppermute | solution.py:26
  75.2 2.0 collective-permute-done.11
  77.2 11.4 %collective-permute-done.9 = bf16[2,80,2048]{2,1,0:T(8,128)(2,1)S(1)} collective-permute-done((bf16[2,80,2048]{2,1,0:T(8,128)(2,1)S(1)}, bf16[2,80,2048]{2,1,0:T(8,128)(2,1)S(1)}, u32[]{:S(2)}, u32[]{:S(2)}) %collective-permute-start.9) | collective-permute-done | bytes 655392 | tf_op jit(solution)/shard_map/ppermute | solution.py:26
  89.6 4.4 %collective-permute-start.18 = (bf16[2,80,2048]{2,1,0:T(8,128)(2,1)S(1)}, bf16[2,80,2048]{2,1,0:T(8,128)(2,1)S(1)}, u32[]{:S(2)}, u32[]{:S(2)}) collective-permute-start(bf16[2,80,2048]{2,1,0:T(8,128)(2,1)S(1)} %get-tuple-element.146), channel_id=1, source_target_pairs={{0,1},{1,2},{4,5},{5,6},{8,9},{9,10},{12,13},{13,14},{16,17},{17,1... | collective-permute-start | bytes 1966088 | tf_op jit(solution)/shard_map/ppermute | solution.py:26
  96.9 2.7 collective-permute-start.13
  99.6 3.8 %collective-permute-start.15 = (bf16[2,80,1024]{2,1,0:T(8,128)(2,1)S(1)}, bf16[2,80,1024]{2,1,0:T(8,128)(2,1)S(1)}, u32[]{:S(2)}, u32[]{:S(2)}) collective-permute-start(bf16[2,80,1024]{2,1,0:T(8,128)(2,1)S(1)} %bitcast.205), channel_id=1, source_target_pairs={{0,3},{1,0},{2,1},{3,2},{4,7},{5,4},{6,5},{7,6},{8,11},{9,8},{10,9... | collective-permute-start | bytes 983048 | tf_op jit(solution)/shard_map/ppermute | solution.py:26
  103.4 5.7 %collective-permute-done.18 = bf16[2,80,2048]{2,1,0:T(8,128)(2,1)S(1)} collective-permute-done((bf16[2,80,2048]{2,1,0:T(8,128)(2,1)S(1)}, bf16[2,80,2048]{2,1,0:T(8,128)(2,1)S(1)}, u32[]{:S(2)}, u32[]{:S(2)}) %collective-permute-start.18) | collective-permute-done | bytes 655392 | tf_op jit(solution)/shard_map/ppermute | solution.py:26
  109.3 4.4 %collective-permute-start.19 = (bf16[2,80,2048]{2,1,0:T(8,128)(2,1)S(1)}, bf16[2,80,2048]{2,1,0:T(8,128)(2,1)S(1)}, u32[]{:S(2)}, u32[]{:S(2)}) collective-permute-start(bf16[2,80,2048]{2,1,0:T(8,128)(2,1)S(1)} %add_convert_fusion.1), channel_id=1, source_target_pairs={{0,1},{1,2},{2,3},{4,5},{5,6},{6,7},{8,9},{9,10},{10,11},{12,13},{... | collective-permute-start | bytes 1966088 | tf_op jit(solution)/shard_map/ppermute | solution.py:26
  116.1 17.9 %collective-permute-done.13 = bf16[2,80,1024]{2,1,0:T(8,128)(2,1)S(1)} collective-permute-done((bf16[2,80,1024]{2,1,0:T(8,128)(2,1)S(1)}, bf16[2,80,1024]{2,1,0:T(8,128)(2,1)S(1)}, u32[]{:S(2)}, u32[]{:S(2)}) %collective-permute-start.13) | collective-permute-done | bytes 327712 | tf_op jit(solution)/shard_map/ppermute | solution.py:26
  135.6 10.3 %collective-permute-start.16 = (bf16[2,80,2048]{2,1,0:T(8,128)(2,1)}, bf16[2,80,2048]{2,1,0:T(8,128)(2,1)}, u32[]{:S(2)}, u32[]{:S(2)}) collective-permute-start(bf16[2,80,2048]{2,1,0:T(8,128)(2,1)} %pad_maximum_fusion.5), channel_id=1, source_target_pairs={{0,1},{1,2},{2,3},{4,5},{5,6},{6,7},{8,9},{9,10},{10,11},{12,13},{... | collective-permute-start | bytes 1966088 | tf_op jit(solution)/shard_map/ppermute | solution.py:26
  150.7 8.8 %collective-permute-start.23 = (bf16[2,80,1024]{2,1,0:T(8,128)(2,1)}, bf16[2,80,1024]{2,1,0:T(8,128)(2,1)}, u32[]{:S(2)}, u32[]{:S(2)}) collective-permute-start(bf16[2,80,1024]{2,1,0:T(8,128)(2,1)} %fusion.47), channel_id=1, source_target_pairs={{0,2},{1,3},{2,0},{3,1},{4,6},{5,7},{6,4},{7,5},{8,10},{9,11},{10,... | collective-permute-start | bytes 983048 | tf_op jit(solution)/shard_map/ppermute | solution.py:26
  161.0 4.8 %collective-permute-done.17 = bf16[2,80,2048]{2,1,0:T(8,128)(2,1)} collective-permute-done((bf16[2,80,2048]{2,1,0:T(8,128)(2,1)}, bf16[2,80,2048]{2,1,0:T(8,128)(2,1)}, u32[]{:S(2)}, u32[]{:S(2)}) %collective-permute-start.17) | collective-permute-done | bytes 655392 | tf_op jit(solution)/shard_map/ppermute | solution.py:26
  165.8 4.8 %collective-permute-done.22 = bf16[2,80,1024]{2,1,0:T(8,128)(2,1)S(1)} collective-permute-done((bf16[2,80,1024]{2,1,0:T(8,128)(2,1)}, bf16[2,80,1024]{2,1,0:T(8,128)(2,1)S(1)}, u32[]{:S(2)}, u32[]{:S(2)}) %collective-permute-start.22) | collective-permute-done | bytes 327712 | tf_op jit(solution)/shard_map/ppermute | solution.py:26
  170.6 26.2 %collective-permute-done.23 = bf16[2,80,1024]{2,1,0:T(8,128)(2,1)} collective-permute-done((bf16[2,80,1024]{2,1,0:T(8,128)(2,1)}, bf16[2,80,1024]{2,1,0:T(8,128)(2,1)}, u32[]{:S(2)}, u32[]{:S(2)}) %collective-permute-start.23) | collective-permute-done | bytes 327712 | tf_op jit(solution)/shard_map/ppermute | solution.py:26
  207.2 8.9 %collective-permute-done.27 = bf16[4,80,1024]{2,1,0:T(8,128)(2,1)S(1)} collective-permute-done((bf16[4,80,1024]{2,1,0:T(8,128)(2,1)S(1)}, bf16[4,80,1024]{2,1,0:T(8,128)(2,1)S(1)}, u32[]{:S(2)}, u32[]{:S(2)}) %collective-permute-start.27) | collective-permute-done | bytes 655392 | tf_op jit(solution)/shard_map/ppermute | solution.py:26
  216.1 4.9 %collective-permute-done.26 = bf16[2,80,2048]{2,1,0:T(8,128)(2,1)} collective-permute-done((bf16[2,80,2048]{2,1,0:T(8,128)(2,1)}, bf16[2,80,2048]{2,1,0:T(8,128)(2,1)}, u32[]{:S(2)}, u32[]{:S(2)}) %collective-permute-start.26) | collective-permute-done | bytes 655392 | tf_op jit(solution)/shard_map/ppermute | solution.py:26
  226.0 2.9 collective-permute-start.33
  230.7 11.6 %collective-permute-done.32.refs_0_ = bf16[128,1024]{1,0:T(8,128)(2,1)S(1)} collective-permute-done((bf16[128,1024]{1,0:T(8,128)(2,1)}, bf16[128,1024]{1,0:T(8,128)(2,1)S(1)}, u32[]{:S(2)}, u32[]{:S(2)}) %collective-permute-start.32) | collective-permute-done | bytes 262176 | tf_op jit(solution)/shard_map/ppermute | solution.py:26
  245.9 14.5 %collective-permute-done.34.refs_2_ = bf16[128,1024]{1,0:T(8,128)(2,1)S(1)} collective-permute-done((bf16[128,1024]{1,0:T(8,128)(2,1)}, bf16[128,1024]{1,0:T(8,128)(2,1)S(1)}, u32[]{:S(2)}, u32[]{:S(2)}) %collective-permute-start.34) | collective-permute-done | bytes 262176 | tf_op jit(solution)/shard_map/ppermute | solution.py:26
  263.4 1.9 copy-done.20
  265.3 2.9 fusion.26
  271.4 14.3 %collective-permute-done.36 = bf16[4,80,1024]{2,1,0:T(8,128)(2,1)} collective-permute-done((bf16[4,80,1024]{2,1,0:T(8,128)(2,1)S(1)}, bf16[4,80,1024]{2,1,0:T(8,128)(2,1)}, u32[]{:S(2)}, u32[]{:S(2)}) %collective-permute-start.36) | collective-permute-done | bytes 655392 | tf_op jit(solution)/shard_map/ppermute | solution.py:26
  288.1 2.8 collective-permute-start.40
  291.3 2.5 finish.2
  293.8 12.6 %collective-permute-done.38.refs_0_ = bf16[128,1024]{1,0:T(8,128)(2,1)S(1)} collective-permute-done((bf16[128,1024]{1,0:T(8,128)(2,1)S(1)}, bf16[128,1024]{1,0:T(8,128)(2,1)S(1)}, u32[]{:S(2)}, u32[]{:S(2)}) %collective-permute-start.38) | collective-permute-done | bytes 262176 | tf_op jit(solution)/shard_map/ppermute | solution.py:26
  307.0 2.5 finish.3
  (178 shorter events, 72.5 us)
Async XLA Ops:
  10.3 24.4 %collective-permute-start.3 = (bf16[80,2048]{1,0:T(8,128)(2,1)}, bf16[80,2048]{1,0:T(8,128)(2,1)}, u32[]{:S(2)}, u32[]{:S(2)}) collective-permute-start(bf16[80,2048]{1,0:T(8,128)(2,1)} %broadcast_select_fusion.5), channel_id=1, source_target_pairs={{0,4},{1,5},{2,6},{3,7},{4,0},{5,1},{6,2},{7,3},{8,12},{9,13},{10,... | collective-permute-start | bytes 983048 | tf_op jit(solution)/shard_map/ppermute | solution.py:26
  13.3 21.4 %collective-permute-start = (bf16[128,1024]{1,0:T(8,128)(2,1)}, bf16[128,1024]{1,0:T(8,128)(2,1)}, u32[]{:S(2)}, u32[]{:S(2)}) collective-permute-start(bf16[128,1024]{1,0:T(8,128)(2,1)} %get-tuple-element.60), channel_id=1, source_target_pairs={{0,2},{1,3},{2,0},{3,1},{4,6},{5,7},{6,4},{7,5},{8,10},{9,11},{10,... | collective-permute-start | bytes 786440 | tf_op jit(solution)/shard_map/ppermute | solution.py:26
  15.9 18.8 %collective-permute-start.1 = (bf16[128,1024]{1,0:T(8,128)(2,1)}, bf16[128,1024]{1,0:T(8,128)(2,1)}, u32[]{:S(2)}, u32[]{:S(2)}) collective-permute-start(bf16[128,1024]{1,0:T(8,128)(2,1)} %get-tuple-element.61), channel_id=1, source_target_pairs={{0,3},{1,0},{2,1},{3,2},{4,7},{5,4},{6,5},{7,6},{8,11},{9,8},{10,9... | collective-permute-start | bytes 786440 | tf_op jit(solution)/shard_map/ppermute | solution.py:26
  36.1 26.3 %collective-permute-start.8 = (bf16[4,80,1024]{2,1,0:T(8,128)(2,1)S(1)}, bf16[4,80,1024]{2,1,0:T(8,128)(2,1)S(1)}, u32[]{:S(2)}, u32[]{:S(2)}) collective-permute-start(bf16[4,80,1024]{2,1,0:T(8,128)(2,1)S(1)} %get-tuple-element.142), channel_id=1, source_target_pairs={{0,4},{1,5},{2,6},{3,7},{4,0},{5,1},{6,2},{7,3},{8,12},{9,13},{10,... | collective-permute-start | bytes 1966088 | tf_op jit(solution)/shard_map/ppermute | solution.py:26
  36.6 20.4 %collective-permute-start.5 = (bf16[128,1024]{1,0:T(8,128)(2,1)S(1)}, bf16[128,1024]{1,0:T(8,128)(2,1)S(1)}, u32[]{:S(2)}, u32[]{:S(2)}) collective-permute-start(bf16[128,1024]{1,0:T(8,128)(2,1)S(1)} %get-tuple-element.71), channel_id=1, source_target_pairs={{0,2},{1,3},{2,0},{3,1},{4,6},{5,7},{6,4},{7,5},{8,10},{9,11},{10,... | collective-permute-start | bytes 786440 | tf_op jit(solution)/shard_map/ppermute | solution.py:26
  43.7 18.6 %collective-permute-start.6 = (bf16[128,1024]{1,0:T(8,128)(2,1)S(1)}, bf16[128,1024]{1,0:T(8,128)(2,1)S(1)}, u32[]{:S(2)}, u32[]{:S(2)}) collective-permute-start(bf16[128,1024]{1,0:T(8,128)(2,1)S(1)} %get-tuple-element.72), channel_id=1, source_target_pairs={{0,3},{1,0},{2,1},{3,2},{4,7},{5,4},{6,5},{7,6},{8,11},{9,8},{10,9... | collective-permute-start | bytes 786440 | tf_op jit(solution)/shard_map/ppermute | solution.py:26
  44.2 18.2 %collective-permute-start.7 = (bf16[128,1024]{1,0:T(8,128)(2,1)S(1)}, bf16[128,1024]{1,0:T(8,128)(2,1)S(1)}, u32[]{:S(2)}, u32[]{:S(2)}) collective-permute-start(bf16[128,1024]{1,0:T(8,128)(2,1)S(1)} %get-tuple-element.73), channel_id=1, source_target_pairs={{0,1},{1,2},{2,3},{3,0},{4,5},{5,6},{6,7},{7,4},{8,9},{9,10},{10,1... | collective-permute-start | bytes 786440 | tf_op jit(solution)/shard_map/ppermute | solution.py:26
  66.3 22.4 %collective-permute-start.12 = (bf16[128,4096]{1,0:T(8,128)(2,1)S(1)}, bf16[128,4096]{1,0:T(8,128)(2,1)S(1)}, u32[]{:S(2)}, u32[]{:S(2)}) collective-permute-start(bf16[128,4096]{1,0:T(8,128)(2,1)S(1)} %bitcast.176), channel_id=1, source_target_pairs={{0,8},{1,9},{2,10},{3,11},{4,12},{5,13},{6,14},{7,15},{8,16},{9,17... | collective-permute-start | bytes 3145736 | tf_op jit(solution)/shard_map/ppermute | solution.py:26
  67.2 21.4 %collective-permute-start.9 = (bf16[2,80,2048]{2,1,0:T(8,128)(2,1)S(1)}, bf16[2,80,2048]{2,1,0:T(8,128)(2,1)S(1)}, u32[]{:S(2)}, u32[]{:S(2)}) collective-permute-start(bf16[2,80,2048]{2,1,0:T(8,128)(2,1)S(1)} %bitcast.189), channel_id=1, source_target_pairs={{0,1},{4,5},{8,9},{12,13},{16,17},{20,21},{24,25},{28,29}} | collective-permute-start | bytes 1966088 | tf_op jit(solution)/shard_map/ppermute | solution.py:26
  89.6 19.4 %collective-permute-start.18 = (bf16[2,80,2048]{2,1,0:T(8,128)(2,1)S(1)}, bf16[2,80,2048]{2,1,0:T(8,128)(2,1)S(1)}, u32[]{:S(2)}, u32[]{:S(2)}) collective-permute-start(bf16[2,80,2048]{2,1,0:T(8,128)(2,1)S(1)} %get-tuple-element.146), channel_id=1, source_target_pairs={{0,1},{1,2},{4,5},{5,6},{8,9},{9,10},{12,13},{13,14},{16,17},{17,1... | collective-permute-start | bytes 1966088 | tf_op jit(solution)/shard_map/ppermute | solution.py:26
  94.1 19.6 %collective-permute-start.20 = (bf16[2,80,2048]{2,1,0:T(8,128)(2,1)S(1)}, bf16[2,80,2048]{2,1,0:T(8,128)(2,1)S(1)}, u32[]{:S(2)}, u32[]{:S(2)}) collective-permute-start(bf16[2,80,2048]{2,1,0:T(8,128)(2,1)S(1)} %get-tuple-element.147), channel_id=1, source_target_pairs={{2,1},{3,2},{6,5},{7,6},{10,9},{11,10},{14,13},{15,14},{18,17},{19... | collective-permute-start | bytes 1966088 | tf_op jit(solution)/shard_map/ppermute | solution.py:26
  96.9 37.2 %collective-permute-start.13 = (bf16[2,80,1024]{2,1,0:T(8,128)(2,1)S(1)}, bf16[2,80,1024]{2,1,0:T(8,128)(2,1)S(1)}, u32[]{:S(2)}, u32[]{:S(2)}) collective-permute-start(bf16[2,80,1024]{2,1,0:T(8,128)(2,1)S(1)} %bitcast.207), channel_id=1, source_target_pairs={{0,2},{1,3},{2,0},{3,1},{4,6},{5,7},{6,4},{7,5},{8,10},{9,11},{10,... | collective-permute-start | bytes 983048 | tf_op jit(solution)/shard_map/ppermute | solution.py:26
  99.6 34.5 %collective-permute-start.14 = (bf16[2,80,1024]{2,1,0:T(8,128)(2,1)S(1)}, bf16[2,80,1024]{2,1,0:T(8,128)(2,1)S(1)}, u32[]{:S(2)}, u32[]{:S(2)}) collective-permute-start(bf16[2,80,1024]{2,1,0:T(8,128)(2,1)S(1)} %bitcast.206), channel_id=1, source_target_pairs={{0,1},{1,2},{2,3},{3,0},{4,5},{5,6},{6,7},{7,4},{8,9},{9,10},{10,1... | collective-permute-start | bytes 983048 | tf_op jit(solution)/shard_map/ppermute | solution.py:26
  99.6 34.5 %collective-permute-start.15 = (bf16[2,80,1024]{2,1,0:T(8,128)(2,1)S(1)}, bf16[2,80,1024]{2,1,0:T(8,128)(2,1)S(1)}, u32[]{:S(2)}, u32[]{:S(2)}) collective-permute-start(bf16[2,80,1024]{2,1,0:T(8,128)(2,1)S(1)} %bitcast.205), channel_id=1, source_target_pairs={{0,3},{1,0},{2,1},{3,2},{4,7},{5,4},{6,5},{7,6},{8,11},{9,8},{10,9... | collective-permute-start | bytes 983048 | tf_op jit(solution)/shard_map/ppermute | solution.py:26
  109.3 38.0 %collective-permute-start.19 = (bf16[2,80,2048]{2,1,0:T(8,128)(2,1)S(1)}, bf16[2,80,2048]{2,1,0:T(8,128)(2,1)S(1)}, u32[]{:S(2)}, u32[]{:S(2)}) collective-permute-start(bf16[2,80,2048]{2,1,0:T(8,128)(2,1)S(1)} %add_convert_fusion.1), channel_id=1, source_target_pairs={{0,1},{1,2},{2,3},{4,5},{5,6},{6,7},{8,9},{9,10},{10,11},{12,13},{... | collective-permute-start | bytes 1966088 | tf_op jit(solution)/shard_map/ppermute | solution.py:26
  113.9 33.6 %collective-permute-start.21 = (bf16[2,80,2048]{2,1,0:T(8,128)(2,1)S(1)}, bf16[2,80,2048]{2,1,0:T(8,128)(2,1)S(1)}, u32[]{:S(2)}, u32[]{:S(2)}) collective-permute-start(bf16[2,80,2048]{2,1,0:T(8,128)(2,1)S(1)} %add_convert_fusion), channel_id=1, source_target_pairs={{1,0},{2,1},{3,2},{5,4},{6,5},{7,6},{9,8},{10,9},{11,10},{13,12},{... | collective-permute-start | bytes 1966088 | tf_op jit(solution)/shard_map/ppermute | solution.py:26
  135.6 25.3 %collective-permute-start.16 = (bf16[2,80,2048]{2,1,0:T(8,128)(2,1)}, bf16[2,80,2048]{2,1,0:T(8,128)(2,1)}, u32[]{:S(2)}, u32[]{:S(2)}) collective-permute-start(bf16[2,80,2048]{2,1,0:T(8,128)(2,1)} %pad_maximum_fusion.5), channel_id=1, source_target_pairs={{0,1},{1,2},{2,3},{4,5},{5,6},{6,7},{8,9},{9,10},{10,11},{12,13},{... | collective-permute-start | bytes 1966088 | tf_op jit(solution)/shard_map/ppermute | solution.py:26
  146.0 19.9 %collective-permute-start.17 = (bf16[2,80,2048]{2,1,0:T(8,128)(2,1)}, bf16[2,80,2048]{2,1,0:T(8,128)(2,1)}, u32[]{:S(2)}, u32[]{:S(2)}) collective-permute-start(bf16[2,80,2048]{2,1,0:T(8,128)(2,1)} %pad_maximum_fusion.5), channel_id=1, source_target_pairs={{1,0},{2,1},{3,2},{5,4},{6,5},{7,6},{9,8},{10,9},{11,10},{13,12},{... | collective-permute-start | bytes 1966088 | tf_op jit(solution)/shard_map/ppermute | solution.py:26
  149.9 20.7 %collective-permute-start.22 = (bf16[2,80,1024]{2,1,0:T(8,128)(2,1)}, bf16[2,80,1024]{2,1,0:T(8,128)(2,1)S(1)}, u32[]{:S(2)}, u32[]{:S(2)}) collective-permute-start(bf16[2,80,1024]{2,1,0:T(8,128)(2,1)} %fusion.47), channel_id=1, source_target_pairs={{0,3},{1,0},{2,1},{3,2},{4,7},{5,4},{6,5},{7,6},{8,11},{9,8},{10,9... | collective-permute-start | bytes 983048 | tf_op jit(solution)/shard_map/ppermute | solution.py:26
  150.7 46.1 %collective-permute-start.23 = (bf16[2,80,1024]{2,1,0:T(8,128)(2,1)}, bf16[2,80,1024]{2,1,0:T(8,128)(2,1)}, u32[]{:S(2)}, u32[]{:S(2)}) collective-permute-start(bf16[2,80,1024]{2,1,0:T(8,128)(2,1)} %fusion.47), channel_id=1, source_target_pairs={{0,2},{1,3},{2,0},{3,1},{4,6},{5,7},{6,4},{7,5},{8,10},{9,11},{10,... | collective-permute-start | bytes 983048 | tf_op jit(solution)/shard_map/ppermute | solution.py:26
  159.5 37.4 %collective-permute-start.24 = (bf16[2,80,1024]{2,1,0:T(8,128)(2,1)}, bf16[2,80,1024]{2,1,0:T(8,128)(2,1)}, u32[]{:S(2)}, u32[]{:S(2)}) collective-permute-start(bf16[2,80,1024]{2,1,0:T(8,128)(2,1)} %fusion.47), channel_id=1, source_target_pairs={{0,1},{1,2},{2,3},{3,0},{4,5},{5,6},{6,7},{7,4},{8,9},{9,10},{10,1... | collective-permute-start | bytes 983048 | tf_op jit(solution)/shard_map/ppermute | solution.py:26
  202.8 18.2 %collective-permute-start.26 = (bf16[2,80,2048]{2,1,0:T(8,128)(2,1)}, bf16[2,80,2048]{2,1,0:T(8,128)(2,1)}, u32[]{:S(2)}, u32[]{:S(2)}) collective-permute-start(bf16[2,80,2048]{2,1,0:T(8,128)(2,1)} %collective-permute-done.17), channel_id=1, source_target_pairs={{1,0},{2,1},{5,4},{6,5},{9,8},{10,9},{13,12},{14,13},{17,16},{18,1... | collective-permute-start | bytes 1966088 | tf_op jit(solution)/shard_map/ppermute | solution.py:26
  223.1 19.2 %collective-permute-start.32 = (bf16[128,1024]{1,0:T(8,128)(2,1)}, bf16[128,1024]{1,0:T(8,128)(2,1)S(1)}, u32[]{:S(2)}, u32[]{:S(2)}) collective-permute-start(bf16[128,1024]{1,0:T(8,128)(2,1)} %get-tuple-element.127), channel_id=1, source_target_pairs={{0,10},{1,11},{2,8},{3,9},{4,14},{5,15},{6,12},{7,13},{8,18},{9,19... | collective-permute-start | bytes 786440 | tf_op jit(solution)/shard_map/ppermute | solution.py:26
  223.1 37.3 %collective-permute-start.30 = (bf16[2,80,2048]{2,1,0:T(8,128)(2,1)}, bf16[2,80,2048]{2,1,0:T(8,128)(2,1)}, u32[]{:S(2)}, u32[]{:S(2)}) collective-permute-start(bf16[2,80,2048]{2,1,0:T(8,128)(2,1)} %collective-permute-done.25), channel_id=1, source_target_pairs={{2,3},{6,7},{10,11},{14,15},{18,19},{22,23},{26,27},{30,31}} | collective-permute-start | bytes 1966088 | tf_op jit(solution)/shard_map/ppermute | solution.py:26
  224.6 35.9 %collective-permute-start.31 = (bf16[2,80,2048]{2,1,0:T(8,128)(2,1)}, bf16[2,80,2048]{2,1,0:T(8,128)(2,1)}, u32[]{:S(2)}, u32[]{:S(2)}) collective-permute-start(bf16[2,80,2048]{2,1,0:T(8,128)(2,1)} %collective-permute-done.26), channel_id=1, source_target_pairs={{1,0},{5,4},{9,8},{13,12},{17,16},{21,20},{25,24},{29,28}} | collective-permute-start | bytes 1966088 | tf_op jit(solution)/shard_map/ppermute | solution.py:26
  226.0 17.6 %collective-permute-start.33 = (bf16[128,1024]{1,0:T(8,128)(2,1)S(1)}, bf16[128,1024]{1,0:T(8,128)(2,1)S(1)}, u32[]{:S(2)}, u32[]{:S(2)}) collective-permute-start(bf16[128,1024]{1,0:T(8,128)(2,1)S(1)} %get-tuple-element.128), channel_id=1, source_target_pairs={{0,9},{1,10},{2,11},{3,8},{4,13},{5,14},{6,15},{7,12},{8,17},{9,18... | collective-permute-start | bytes 786440 | tf_op jit(solution)/shard_map/ppermute | solution.py:26
  228.9 31.5 %collective-permute-start.34 = (bf16[128,1024]{1,0:T(8,128)(2,1)}, bf16[128,1024]{1,0:T(8,128)(2,1)S(1)}, u32[]{:S(2)}, u32[]{:S(2)}) collective-permute-start(bf16[128,1024]{1,0:T(8,128)(2,1)} %get-tuple-element.129), channel_id=1, source_target_pairs={{0,11},{1,8},{2,9},{3,10},{4,15},{5,12},{6,13},{7,14},{8,19},{9,16... | collective-permute-start | bytes 786440 | tf_op jit(solution)/shard_map/ppermute | solution.py:26
  242.3 18.2 %collective-permute-start.35 = (bf16[128,1024]{1,0:T(8,128)(2,1)}, bf16[128,1024]{1,0:T(8,128)(2,1)S(1)}, u32[]{:S(2)}, u32[]{:S(2)}) collective-permute-start(bf16[128,1024]{1,0:T(8,128)(2,1)} %get-tuple-element.126), channel_id=1, source_target_pairs={{0,8},{1,9},{2,10},{3,11},{4,12},{5,13},{6,14},{7,15},{8,16},{9,17... | collective-permute-start | bytes 786440 | tf_op jit(solution)/shard_map/ppermute | solution.py:26
  244.3 27.0 %collective-permute-start.37 = (bf16[128,4096]{1,0:T(8,128)(2,1)S(1)}, bf16[128,4096]{1,0:T(8,128)(2,1)S(1)}, u32[]{:S(2)}, u32[]{:S(2)}) collective-permute-start(bf16[128,4096]{1,0:T(8,128)(2,1)S(1)} %bitcast.178), channel_id=1, source_target_pairs={{0,24},{1,25},{2,26},{3,27},{4,28},{5,29},{6,30},{7,31},{8,0},{9,1... | collective-permute-start | bytes 3145736 | tf_op jit(solution)/shard_map/ppermute | solution.py:26
  287.3 19.1 %collective-permute-start.38 = (bf16[128,1024]{1,0:T(8,128)(2,1)S(1)}, bf16[128,1024]{1,0:T(8,128)(2,1)S(1)}, u32[]{:S(2)}, u32[]{:S(2)}) collective-permute-start(bf16[128,1024]{1,0:T(8,128)(2,1)S(1)} %get-tuple-element.123), channel_id=1, source_target_pairs={{0,26},{1,27},{2,24},{3,25},{4,30},{5,31},{6,28},{7,29},{8,2},{9,3... | collective-permute-start | bytes 786440 | tf_op jit(solution)/shard_map/ppermute | solution.py:26
  287.4 19.0 %collective-permute-start.39 = (bf16[128,1024]{1,0:T(8,128)(2,1)S(1)}, bf16[128,1024]{1,0:T(8,128)(2,1)S(1)}, u32[]{:S(2)}, u32[]{:S(2)}) collective-permute-start(bf16[128,1024]{1,0:T(8,128)(2,1)S(1)} %get-tuple-element.124), channel_id=1, source_target_pairs={{0,25},{1,26},{2,27},{3,24},{4,29},{5,30},{6,31},{7,28},{8,1},{9,2... | collective-permute-start | bytes 786440 | tf_op jit(solution)/shard_map/ppermute | solution.py:26
  288.1 18.9 %collective-permute-start.40 = (bf16[128,1024]{1,0:T(8,128)(2,1)S(1)}, bf16[128,1024]{1,0:T(8,128)(2,1)S(1)}, u32[]{:S(2)}, u32[]{:S(2)}) collective-permute-start(bf16[128,1024]{1,0:T(8,128)(2,1)S(1)} %get-tuple-element.125), channel_id=1, source_target_pairs={{0,27},{1,24},{2,25},{3,26},{4,31},{5,28},{6,29},{7,30},{8,3},{9,0... | collective-permute-start | bytes 786440 | tf_op jit(solution)/shard_map/ppermute | solution.py:26
  (41 other events, 421.5 us)

commit v3 on v0

--- a/solution.py
+++ b/solution.py
@@ -139,9 +139,15 @@
     return jnp.sum(jnp.where(row == col, row_ref[...], 0.0), axis=1, keepdims=True)
 
 
-def cut_kernel(at_ref, route_ref, weight_ref, values_ref, *blocks):
+def cut_kernel(at_ref, route_ref, weight_ref, values_ref, *refs):
+    *blocks, values, sem = refs
     tokens = route_ref.shape[1]
     column = blocks[0].shape[1]
+    copies = []
+    for i in range(len(blocks)):
+        cols = pl.ds(pl.multiple_of(at_ref[i] * column, column), column)
+        copies.append(pltpu.make_async_copy(values_ref.at[:, cols], values.at[i], sem.at[i]))
+        copies[i].start()
     row = lax.broadcasted_iota(jnp.int32, (tokens, tokens), 0)
     col = lax.broadcasted_iota(jnp.int32, (tokens, tokens), 1)
     ones = route_ref[...].astype(F32)
@@ -156,8 +162,8 @@
     picker = (row == place).astype(BF16)
     weight = column_of(weight_ref)
     for i, block_ref in enumerate(blocks):
-        cols = pl.ds(pl.multiple_of(at_ref[i] * column, column), column)
-        block = (weight * values_ref[:, cols].astype(F32)).astype(BF16)
+        copies[i].wait()
+        block = (weight * values[i].astype(F32)).astype(BF16)
         block_ref[...] = jnp.dot(picker, block, preferred_element_type=F32).astype(BF16)
 
 
@@ -169,9 +175,15 @@
         pl.pallas_call(
             cut_kernel,
             out_shape=[jax.ShapeDtypeStruct((rows, features // 4), BF16)] * 4,
-            in_specs=[pl.BlockSpec(memory_space=pltpu.SMEM)] + [vmem] * 3,
+            in_specs=[pl.BlockSpec(memory_space=pltpu.SMEM)]
+            + [vmem] * 2
+            + [pl.BlockSpec(memory_space=pl.ANY)],
             out_specs=[vmem] * 4,
-            compiler_params=pltpu.CompilerParams(vmem_limit_bytes=8 * 2**20),
+            scratch_shapes=[
+                pltpu.VMEM((4, rows, features // 4), BF16),
+                pltpu.SemaphoreType.DMA((4,)),
+            ],
+            compiler_params=pltpu.CompilerParams(vmem_limit_bytes=56 * 2**20),
             name="cut",
         )(at, route[None, :], weight[None, :], tokens)
     )

time: 261 us -> 261 us (level)
  local copies, waits for them, and re-layouts: 9.71 us -> 6.5 us
  starting transfers between devices: 103 us -> 106 us
    unnamed x48 -> x32, local copies, waits for them, and re-layouts: 7.49 us -> 3.93 us
  transfers between devices with their start and end apart: 42 -> 42, of which waited for: 15 -> 16; matrix products, arithmetic and copies ran while one was open for 14% -> 13% of each run, Pallas kernels for 1% -> 1%
where the time goes in v3:
time: 261 us; the launch traced here: 260 us
  starting transfers between devices  106 us (41%)
  waiting for transfers between devices  97.6 us (37%)
  other arithmetic  20.5 us (8%)
  matrix products  16.9 us (6%)
  Pallas kernels  8.43 us (3%)
  local copies, waits for them, and re-layouts  6.5 us (2%)
  between operations  4.11 us (2%)
    ppermute x42, starting transfers between devices, move(): return lax.ppermute(value, AXES, pairs)  106 us
    ppermute x42, waiting for transfers between devices, move(): return lax.ppermute(value, AXES, pairs)  97.6 us
    dot_general x4, matrix products, cut(): jnp.dot(placer, block, preferred_element_type=F32).astype(BF16)  6.11 us
    convert_element_type x3, other arithmetic, sums(): right, left = (right.astype(BF16), left.astype(BF16))  5.93 us
  transfers between devices with their start and end apart: 42, of which 16 were waited for; matrix products, arithmetic and copies ran while one was open for 13% of the time, Pallas kernels for 1%

profile of v3, /device:TPU:0, one launch (start us, length us, event | category | flops | bytes accessed | tf_op | source)
XLA Modules:
  0.0 259.5 jit_solution(367391673936939567)
XLA Ops:
  1.3 3.5 %cut.1 = (bf16[128,1024]{1,0:T(8,128)(2,1)}, bf16[128,1024]{1,0:T(8,128)(2,1)}, bf16[128,1024]{1,0:T(8,128)(2,1)}, bf16[128,1024]{1,0:T(8,128)(2,1)}) custom-call(s32[4]{0:T(128)} %pad_add_fusion.3.at_ref, s32[1,128]{1,0:T(1,128)} %bitcast.215, f32[1,128]{1,0:T(1,128)} %weight_ref.1, bf16[128,4096]{1,0:T(8,128)(2,1)} %bitcast.201), custom_call_target="tpu_custom_call" | custom-call | tf_op jit(solution)/shard_map/cut/pallas_call | solution.py:175
  4.8 4.1 %collective-permute-start = (bf16[128,1024]{1,0:T(8,128)(2,1)}, bf16[128,1024]{1,0:T(8,128)(2,1)}, u32[]{:S(2)}, u32[]{:S(2)}) collective-permute-start(bf16[128,1024]{1,0:T(8,128)(2,1)} %get-tuple-element.56), channel_id=1, source_target_pairs={{0,2},{1,3},{2,0},{3,1},{4,6},{5,7},{6,4},{7,5},{8,10},{9,11},{10,... | collective-permute-start | bytes 786440 | tf_op jit(solution)/shard_map/ppermute | solution.py:26
  31.0 7.1 %collective-permute-start.9 = (bf16[128,1024]{1,0:T(8,128)(2,1)S(1)}, bf16[128,1024]{1,0:T(8,128)(2,1)S(1)}, u32[]{:S(2)}, u32[]{:S(2)}) collective-permute-start(bf16[128,1024]{1,0:T(8,128)(2,1)S(1)} %copy-done.10), channel_id=1, source_target_pairs={{0,2},{1,3},{2,0},{3,1},{4,6},{5,7},{6,4},{7,5},{8,10},{9,11},{10,... | collective-permute-start | bytes 786440 | tf_op jit(solution)/shard_map/ppermute | solution.py:26
  40.2 4.8 %collective-permute-done.5 = bf16[4,80,1024]{2,1,0:T(8,128)(2,1)S(1)} collective-permute-done((bf16[4,80,1024]{2,1,0:T(8,128)(2,1)S(1)}, bf16[4,80,1024]{2,1,0:T(8,128)(2,1)S(1)}, u32[]{:S(2)}, u32[]{:S(2)}) %collective-permute-start.5) | collective-permute-done | bytes 655392 | tf_op jit(solution)/shard_map/ppermute | solution.py:26
  47.1 3.5 %collective-permute-start.8 = (bf16[2,80,1024]{2,1,0:T(8,128)(2,1)S(1)}, bf16[2,80,1024]{2,1,0:T(8,128)(2,1)S(1)}, u32[]{:S(2)}, u32[]{:S(2)}) collective-permute-start(bf16[2,80,1024]{2,1,0:T(8,128)(2,1)S(1)} %bitcast.207), channel_id=1, source_target_pairs={{0,3},{1,0},{2,1},{3,2},{4,7},{5,4},{6,5},{7,6},{8,11},{9,8},{10,9... | collective-permute-start | bytes 983048 | tf_op jit(solution)/shard_map/ppermute | solution.py:26
  50.6 2.9 %collective-permute-start.7 = (bf16[2,80,1024]{2,1,0:T(8,128)(2,1)S(1)}, bf16[2,80,1024]{2,1,0:T(8,128)(2,1)S(1)}, u32[]{:S(2)}, u32[]{:S(2)}) collective-permute-start(bf16[2,80,1024]{2,1,0:T(8,128)(2,1)S(1)} %bitcast.206), channel_id=1, source_target_pairs={{0,1},{1,2},{2,3},{3,0},{4,5},{5,6},{6,7},{7,4},{8,9},{9,10},{10,1... | collective-permute-start | bytes 983048 | tf_op jit(solution)/shard_map/ppermute | solution.py:26
  53.5 3.9 %collective-permute-start.6 = (bf16[2,80,1024]{2,1,0:T(8,128)(2,1)S(1)}, bf16[2,80,1024]{2,1,0:T(8,128)(2,1)S(1)}, u32[]{:S(2)}, u32[]{:S(2)}) collective-permute-start(bf16[2,80,1024]{2,1,0:T(8,128)(2,1)S(1)} %bitcast.205), channel_id=1, source_target_pairs={{0,2},{1,3},{2,0},{3,1},{4,6},{5,7},{6,4},{7,5},{8,10},{9,11},{10,... | collective-permute-start | bytes 983048 | tf_op jit(solution)/shard_map/ppermute | solution.py:26
  59.0 10.2 %collective-permute-done.8 = bf16[2,80,1024]{2,1,0:T(8,128)(2,1)S(1)} collective-permute-done((bf16[2,80,1024]{2,1,0:T(8,128)(2,1)S(1)}, bf16[2,80,1024]{2,1,0:T(8,128)(2,1)S(1)}, u32[]{:S(2)}, u32[]{:S(2)}) %collective-permute-start.8) | collective-permute-done | bytes 327712 | tf_op jit(solution)/shard_map/ppermute | solution.py:26
  69.1 3.4 %collective-permute-done.7 = bf16[2,80,1024]{2,1,0:T(8,128)(2,1)S(1)} collective-permute-done((bf16[2,80,1024]{2,1,0:T(8,128)(2,1)S(1)}, bf16[2,80,1024]{2,1,0:T(8,128)(2,1)S(1)}, u32[]{:S(2)}, u32[]{:S(2)}) %collective-permute-start.7) | collective-permute-done | bytes 327712 | tf_op jit(solution)/shard_map/ppermute | solution.py:26
  72.5 16.8 %collective-permute-done.6 = bf16[2,80,1024]{2,1,0:T(8,128)(2,1)S(1)} collective-permute-done((bf16[2,80,1024]{2,1,0:T(8,128)(2,1)S(1)}, bf16[2,80,1024]{2,1,0:T(8,128)(2,1)S(1)}, u32[]{:S(2)}, u32[]{:S(2)}) %collective-permute-start.6) | collective-permute-done | bytes 327712 | tf_op jit(solution)/shard_map/ppermute | solution.py:26
  92.6 4.6 %collective-permute-start.12 = (bf16[2,80,2048]{2,1,0:T(8,128)(2,1)S(1)}, bf16[2,80,2048]{2,1,0:T(8,128)(2,1)S(1)}, u32[]{:S(2)}, u32[]{:S(2)}) collective-permute-start(bf16[2,80,2048]{2,1,0:T(8,128)(2,1)S(1)} %pad_maximum_fusion.6), channel_id=1, source_target_pairs={{0,1},{1,2},{2,3},{4,5},{5,6},{6,7},{8,9},{9,10},{10,11},{12,13},{... | collective-permute-start | bytes 1966088 | tf_op jit(solution)/shard_map/ppermute | solution.py:26
  97.7 8.3 %collective-permute-done.14 = bf16[4,80,1024]{2,1,0:T(8,128)(2,1)S(1)} collective-permute-done((bf16[4,80,1024]{2,1,0:T(8,128)(2,1)S(1)}, bf16[4,80,1024]{2,1,0:T(8,128)(2,1)S(1)}, u32[]{:S(2)}, u32[]{:S(2)}) %collective-permute-start.14) | collective-permute-done | bytes 655392 | tf_op jit(solution)/shard_map/ppermute | solution.py:26
  108.4 3.1 %fusion.4 = bf16[640,2048]{1,0:T(8,128)(2,1)S(1)} fusion(bf16[640,1024]{1,0:T(8,128)(2,1)S(1)} %bitcast.195, bf16[1,1,1024,2048]{3,2,1,0:T(8,128)(2,1)S(1)} %copy-done.13), kind=kOutput, calls=%fused_computation.4 | convolution fusion | flops 2685665280 | bytes 8126464 | tf_op jit(solution)/shard_map/dot_general | solution.py:314
  115.0 4.0 %collective-permute-start.20 = (bf16[2,80,2048]{2,1,0:T(8,128)(2,1)}, bf16[2,80,2048]{2,1,0:T(8,128)(2,1)}, u32[]{:S(2)}, u32[]{:S(2)}) collective-permute-start(bf16[2,80,2048]{2,1,0:T(8,128)(2,1)} %bitcast.50), channel_id=1, source_target_pairs={{0,1},{4,5},{8,9},{12,13},{16,17},{20,21},{24,25},{28,29}} | collective-permute-start | bytes 1966088 | tf_op jit(solution)/shard_map/ppermute | solution.py:26
  123.2 7.8 %collective-permute-done.20 = bf16[2,80,2048]{2,1,0:T(8,128)(2,1)} collective-permute-done((bf16[2,80,2048]{2,1,0:T(8,128)(2,1)}, bf16[2,80,2048]{2,1,0:T(8,128)(2,1)}, u32[]{:S(2)}, u32[]{:S(2)}) %collective-permute-start.20) | collective-permute-done | bytes 655392 | tf_op jit(solution)/shard_map/ppermute | solution.py:26
  131.0 3.0 %fusion.21 = (bf16[2,80,2048]{2,1,0:T(8,128)(2,1)}, bf16[2,80,2048]{2,1,0:T(8,128)(2,1)}) fusion(bf16[2,80,2048]{2,1,0:T(8,128)(2,1)} %bitcast.192, bf16[2,80,2048]{2,1,0:T(8,128)(2,1)} %collective-permute-done.21, bf16[2,80,2048]{2,1,0:T(8,128)(2,1)} %collective-permute-done.20), kind=kLoop, calls=%fused_computation.17 | loop fusion | flops 2293760 | bytes 3276800 | tf_op jit(solution)/shard_map/convert_element_type | solution.py:84
  135.5 5.0 %collective-permute-start.22 = (bf16[2,80,2048]{2,1,0:T(8,128)(2,1)}, bf16[2,80,2048]{2,1,0:T(8,128)(2,1)}, u32[]{:S(2)}, u32[]{:S(2)}) collective-permute-start(bf16[2,80,2048]{2,1,0:T(8,128)(2,1)} %get-tuple-element.135), channel_id=1, source_target_pairs={{0,1},{1,2},{4,5},{5,6},{8,9},{9,10},{12,13},{13,14},{16,17},{17,1... | collective-permute-start | bytes 1966088 | tf_op jit(solution)/shard_map/ppermute | solution.py:26
  145.6 6.0 %collective-permute-done.22 = bf16[2,80,2048]{2,1,0:T(8,128)(2,1)} collective-permute-done((bf16[2,80,2048]{2,1,0:T(8,128)(2,1)}, bf16[2,80,2048]{2,1,0:T(8,128)(2,1)}, u32[]{:S(2)}, u32[]{:S(2)}) %collective-permute-start.22) | collective-permute-done | bytes 655392 | tf_op jit(solution)/shard_map/ppermute | solution.py:26
  156.0 7.2 %collective-permute-start.24 = (bf16[2,80,2048]{2,1,0:T(8,128)(2,1)S(1)}, bf16[2,80,2048]{2,1,0:T(8,128)(2,1)S(1)}, u32[]{:S(2)}, u32[]{:S(2)}) collective-permute-start(bf16[2,80,2048]{2,1,0:T(8,128)(2,1)S(1)} %add_convert_fusion.1), channel_id=1, source_target_pairs={{0,1},{1,2},{2,3},{4,5},{5,6},{6,7},{8,9},{9,10},{10,11},{12,13},{... | collective-permute-start | bytes 1966088 | tf_op jit(solution)/shard_map/ppermute | solution.py:26
  165.6 2.9 %fusion.11 = bf16[640,1024]{1,0:T(8,128)(2,1)S(1)} fusion(bf16[640,2048]{1,0:T(8,128)(2,1)S(1)} %bitcast.190, bf16[1,1,1024,2048]{3,2,1,0:T(8,128)(2,1)S(1)} %copy-done.14), kind=kOutput, calls=%fused_computation.13 | convolution fusion | flops 2685009920 | bytes 8126464 | tf_op jit(solution)/shard_map/dot_general | solution.py:51
  169.7 5.3 %collective-permute-done.25 = bf16[2,80,2048]{2,1,0:T(8,128)(2,1)S(1)} collective-permute-done((bf16[2,80,2048]{2,1,0:T(8,128)(2,1)S(1)}, bf16[2,80,2048]{2,1,0:T(8,128)(2,1)S(1)}, u32[]{:S(2)}, u32[]{:S(2)}) %collective-permute-start.25) | collective-permute-done | bytes 655392 | tf_op jit(solution)/shard_map/ppermute | solution.py:26
  177.3 3.7 %collective-permute-start.27 = (bf16[2,80,1024]{2,1,0:T(8,128)(2,1)S(1)}, bf16[2,80,1024]{2,1,0:T(8,128)(2,1)S(1)}, u32[]{:S(2)}, u32[]{:S(2)}) collective-permute-start(bf16[2,80,1024]{2,1,0:T(8,128)(2,1)S(1)} %fusion.32), channel_id=1, source_target_pairs={{0,2},{1,3},{2,0},{3,1},{4,6},{5,7},{6,4},{7,5},{8,10},{9,11},{10,... | collective-permute-start | bytes 983048 | tf_op jit(solution)/shard_map/ppermute | solution.py:26
  184.9 17.9 %collective-permute-done.27 = bf16[2,80,1024]{2,1,0:T(8,128)(2,1)S(1)} collective-permute-done((bf16[2,80,1024]{2,1,0:T(8,128)(2,1)S(1)}, bf16[2,80,1024]{2,1,0:T(8,128)(2,1)S(1)}, u32[]{:S(2)}, u32[]{:S(2)}) %collective-permute-start.27) | collective-permute-done | bytes 327712 | tf_op jit(solution)/shard_map/ppermute | solution.py:26
  208.4 3.9 %collective-permute-start.39 = (bf16[128,1024]{1,0:T(8,128)(2,1)S(1)}, bf16[128,1024]{1,0:T(8,128)(2,1)S(1)}, u32[]{:S(2)}, u32[]{:S(2)}) collective-permute-start(bf16[128,1024]{1,0:T(8,128)(2,1)S(1)} %get-tuple-element.130), channel_id=1, source_target_pairs={{0,25},{1,26},{2,27},{3,24},{4,29},{5,30},{6,31},{7,28},{8,1},{9,2... | collective-permute-start | bytes 786440 | tf_op jit(solution)/shard_map/ppermute | solution.py:26
  212.3 3.3 %collective-permute-start.38 = (bf16[128,1024]{1,0:T(8,128)(2,1)S(1)}, bf16[128,1024]{1,0:T(8,128)(2,1)S(1)}, u32[]{:S(2)}, u32[]{:S(2)}) collective-permute-start(bf16[128,1024]{1,0:T(8,128)(2,1)S(1)} %get-tuple-element.131), channel_id=1, source_target_pairs={{0,26},{1,27},{2,24},{3,25},{4,30},{5,31},{6,28},{7,29},{8,2},{9,3... | collective-permute-start | bytes 786440 | tf_op jit(solution)/shard_map/ppermute | solution.py:26
  215.7 3.4 %collective-permute-done.33 = bf16[4,80,1024]{2,1,0:T(8,128)(2,1)S(1)} collective-permute-done((bf16[4,80,1024]{2,1,0:T(8,128)(2,1)S(1)}, bf16[4,80,1024]{2,1,0:T(8,128)(2,1)S(1)}, u32[]{:S(2)}, u32[]{:S(2)}) %collective-permute-start.33) | collective-permute-done | bytes 655392 | tf_op jit(solution)/shard_map/ppermute | solution.py:26
  219.4 7.0 %collective-permute-start.34 = (bf16[128,1024]{1,0:T(8,128)(2,1)S(1)}, bf16[128,1024]{1,0:T(8,128)(2,1)S(1)}, u32[]{:S(2)}, u32[]{:S(2)}) collective-permute-start(bf16[128,1024]{1,0:T(8,128)(2,1)S(1)} %get-tuple-element.121), channel_id=1, source_target_pairs={{0,10},{1,11},{2,8},{3,9},{4,14},{5,15},{6,12},{7,13},{8,18},{9,19... | collective-permute-start | bytes 786440 | tf_op jit(solution)/shard_map/ppermute | solution.py:26
  226.4 18.1 %collective-permute-start.35 = (bf16[128,1024]{1,0:T(8,128)(2,1)S(1)}, bf16[128,1024]{1,0:T(8,128)(2,1)S(1)}, u32[]{:S(2)}, u32[]{:S(2)}) collective-permute-start(bf16[128,1024]{1,0:T(8,128)(2,1)S(1)} %get-tuple-element.122), channel_id=1, source_target_pairs={{0,9},{1,10},{2,11},{3,8},{4,13},{5,14},{6,15},{7,12},{8,17},{9,18... | collective-permute-start | bytes 786440 | tf_op jit(solution)/shard_map/ppermute | solution.py:26
  244.8 3.4 %collective-permute-done.38.refs_0_ = bf16[128,1024]{1,0:T(8,128)(2,1)S(1)} collective-permute-done((bf16[128,1024]{1,0:T(8,128)(2,1)S(1)}, bf16[128,1024]{1,0:T(8,128)(2,1)S(1)}, u32[]{:S(2)}, u32[]{:S(2)}) %collective-permute-start.38) | collective-permute-done | bytes 262176 | tf_op jit(solution)/shard_map/ppermute | solution.py:26
  248.2 2.5 finish.3
  252.5 4.4 %collective-permute-done.36.refs_2_ = bf16[128,1024]{1,0:T(8,128)(2,1)S(1)} collective-permute-done((bf16[128,1024]{1,0:T(8,128)(2,1)S(1)}, bf16[128,1024]{1,0:T(8,128)(2,1)S(1)}, u32[]{:S(2)}, u32[]{:S(2)}) %collective-permute-start.36) | collective-permute-done | bytes 262176 | tf_op jit(solution)/shard_map/ppermute | solution.py:26
  256.9 2.5 finish.2
  (151 shorter events, 67.9 us)
Async XLA Ops:
  4.8 22.3 %collective-permute-start = (bf16[128,1024]{1,0:T(8,128)(2,1)}, bf16[128,1024]{1,0:T(8,128)(2,1)}, u32[]{:S(2)}, u32[]{:S(2)}) collective-permute-start(bf16[128,1024]{1,0:T(8,128)(2,1)} %get-tuple-element.56), channel_id=1, source_target_pairs={{0,2},{1,3},{2,0},{3,1},{4,6},{5,7},{6,4},{7,5},{8,10},{9,11},{10,... | collective-permute-start | bytes 786440 | tf_op jit(solution)/shard_map/ppermute | solution.py:26
  8.9 18.2 %collective-permute-start.1 = (bf16[128,1024]{1,0:T(8,128)(2,1)}, bf16[128,1024]{1,0:T(8,128)(2,1)}, u32[]{:S(2)}, u32[]{:S(2)}) collective-permute-start(bf16[128,1024]{1,0:T(8,128)(2,1)} %get-tuple-element.57), channel_id=1, source_target_pairs={{0,3},{1,0},{2,1},{3,2},{4,7},{5,4},{6,5},{7,6},{8,11},{9,8},{10,9... | collective-permute-start | bytes 786440 | tf_op jit(solution)/shard_map/ppermute | solution.py:26
  10.2 17.7 %collective-permute-start.2 = (bf16[128,1024]{1,0:T(8,128)(2,1)}, bf16[128,1024]{1,0:T(8,128)(2,1)}, u32[]{:S(2)}, u32[]{:S(2)}) collective-permute-start(bf16[128,1024]{1,0:T(8,128)(2,1)} %get-tuple-element.58), channel_id=1, source_target_pairs={{0,1},{1,2},{2,3},{3,0},{4,5},{5,6},{6,7},{7,4},{8,9},{9,10},{10,1... | collective-permute-start | bytes 786440 | tf_op jit(solution)/shard_map/ppermute | solution.py:26
  31.0 22.5 %collective-permute-start.9 = (bf16[128,1024]{1,0:T(8,128)(2,1)S(1)}, bf16[128,1024]{1,0:T(8,128)(2,1)S(1)}, u32[]{:S(2)}, u32[]{:S(2)}) collective-permute-start(bf16[128,1024]{1,0:T(8,128)(2,1)S(1)} %copy-done.10), channel_id=1, source_target_pairs={{0,2},{1,3},{2,0},{3,1},{4,6},{5,7},{6,4},{7,5},{8,10},{9,11},{10,... | collective-permute-start | bytes 786440 | tf_op jit(solution)/shard_map/ppermute | solution.py:26
  38.1 20.8 %collective-permute-start.10 = (bf16[128,1024]{1,0:T(8,128)(2,1)S(1)}, bf16[128,1024]{1,0:T(8,128)(2,1)S(1)}, u32[]{:S(2)}, u32[]{:S(2)}) collective-permute-start(bf16[128,1024]{1,0:T(8,128)(2,1)S(1)} %copy-done.9), channel_id=1, source_target_pairs={{0,3},{1,0},{2,1},{3,2},{4,7},{5,4},{6,5},{7,6},{8,11},{9,8},{10,9... | collective-permute-start | bytes 786440 | tf_op jit(solution)/shard_map/ppermute | solution.py:26
  38.6 20.4 %collective-permute-start.11 = (bf16[128,1024]{1,0:T(8,128)(2,1)S(1)}, bf16[128,1024]{1,0:T(8,128)(2,1)S(1)}, u32[]{:S(2)}, u32[]{:S(2)}) collective-permute-start(bf16[128,1024]{1,0:T(8,128)(2,1)S(1)} %convolution_convert_fusion.1), channel_id=1, source_target_pairs={{0,1},{1,2},{2,3},{3,0},{4,5},{5,6},{6,7},{7,4},{8,9},{9,10},{10,1... | collective-permute-start | bytes 786440 | tf_op jit(solution)/shard_map/ppermute | solution.py:26
  47.1 22.0 %collective-permute-start.8 = (bf16[2,80,1024]{2,1,0:T(8,128)(2,1)S(1)}, bf16[2,80,1024]{2,1,0:T(8,128)(2,1)S(1)}, u32[]{:S(2)}, u32[]{:S(2)}) collective-permute-start(bf16[2,80,1024]{2,1,0:T(8,128)(2,1)S(1)} %bitcast.207), channel_id=1, source_target_pairs={{0,3},{1,0},{2,1},{3,2},{4,7},{5,4},{6,5},{7,6},{8,11},{9,8},{10,9... | collective-permute-start | bytes 983048 | tf_op jit(solution)/shard_map/ppermute | solution.py:26
  50.6 21.9 %collective-permute-start.7 = (bf16[2,80,1024]{2,1,0:T(8,128)(2,1)S(1)}, bf16[2,80,1024]{2,1,0:T(8,128)(2,1)S(1)}, u32[]{:S(2)}, u32[]{:S(2)}) collective-permute-start(bf16[2,80,1024]{2,1,0:T(8,128)(2,1)S(1)} %bitcast.206), channel_id=1, source_target_pairs={{0,1},{1,2},{2,3},{3,0},{4,5},{5,6},{6,7},{7,4},{8,9},{9,10},{10,1... | collective-permute-start | bytes 983048 | tf_op jit(solution)/shard_map/ppermute | solution.py:26
  53.5 35.9 %collective-permute-start.6 = (bf16[2,80,1024]{2,1,0:T(8,128)(2,1)S(1)}, bf16[2,80,1024]{2,1,0:T(8,128)(2,1)S(1)}, u32[]{:S(2)}, u32[]{:S(2)}) collective-permute-start(bf16[2,80,1024]{2,1,0:T(8,128)(2,1)S(1)} %bitcast.205), channel_id=1, source_target_pairs={{0,2},{1,3},{2,0},{3,1},{4,6},{5,7},{6,4},{7,5},{8,10},{9,11},{10,... | collective-permute-start | bytes 983048 | tf_op jit(solution)/shard_map/ppermute | solution.py:26
  89.5 16.6 %collective-permute-start.14 = (bf16[4,80,1024]{2,1,0:T(8,128)(2,1)S(1)}, bf16[4,80,1024]{2,1,0:T(8,128)(2,1)S(1)}, u32[]{:S(2)}, u32[]{:S(2)}) collective-permute-start(bf16[4,80,1024]{2,1,0:T(8,128)(2,1)S(1)} %broadcast_select_fusion), channel_id=1, source_target_pairs={{0,4},{1,5},{2,6},{3,7},{4,0},{5,1},{6,2},{7,3},{8,12},{9,13},{10,... | collective-permute-start | bytes 1966088 | tf_op jit(solution)/shard_map/ppermute | solution.py:26
  91.3 20.3 %collective-permute-start.13 = (bf16[2,80,2048]{2,1,0:T(8,128)(2,1)S(1)}, bf16[2,80,2048]{2,1,0:T(8,128)(2,1)S(1)}, u32[]{:S(2)}, u32[]{:S(2)}) collective-permute-start(bf16[2,80,2048]{2,1,0:T(8,128)(2,1)S(1)} %pad_maximum_fusion.6), channel_id=1, source_target_pairs={{1,0},{2,1},{3,2},{5,4},{6,5},{7,6},{9,8},{10,9},{11,10},{13,12},{... | collective-permute-start | bytes 1966088 | tf_op jit(solution)/shard_map/ppermute | solution.py:26
  92.6 19.0 %collective-permute-start.12 = (bf16[2,80,2048]{2,1,0:T(8,128)(2,1)S(1)}, bf16[2,80,2048]{2,1,0:T(8,128)(2,1)S(1)}, u32[]{:S(2)}, u32[]{:S(2)}) collective-permute-start(bf16[2,80,2048]{2,1,0:T(8,128)(2,1)S(1)} %pad_maximum_fusion.6), channel_id=1, source_target_pairs={{0,1},{1,2},{2,3},{4,5},{5,6},{6,7},{8,9},{9,10},{10,11},{12,13},{... | collective-permute-start | bytes 1966088 | tf_op jit(solution)/shard_map/ppermute | solution.py:26
  115.0 16.0 %collective-permute-start.20 = (bf16[2,80,2048]{2,1,0:T(8,128)(2,1)}, bf16[2,80,2048]{2,1,0:T(8,128)(2,1)}, u32[]{:S(2)}, u32[]{:S(2)}) collective-permute-start(bf16[2,80,2048]{2,1,0:T(8,128)(2,1)} %bitcast.50), channel_id=1, source_target_pairs={{0,1},{4,5},{8,9},{12,13},{16,17},{20,21},{24,25},{28,29}} | collective-permute-start | bytes 1966088 | tf_op jit(solution)/shard_map/ppermute | solution.py:26
  119.1 22.7 %collective-permute-start.19 = (bf16[128,4096]{1,0:T(8,128)(2,1)}, bf16[128,4096]{1,0:T(8,128)(2,1)S(1)}, u32[]{:S(2)}, u32[]{:S(2)}) collective-permute-start(bf16[128,4096]{1,0:T(8,128)(2,1)} %bitcast.49), channel_id=1, source_target_pairs={{0,8},{1,9},{2,10},{3,11},{4,12},{5,13},{6,14},{7,15},{8,16},{9,17... | collective-permute-start | bytes 3145736 | tf_op jit(solution)/shard_map/ppermute | solution.py:26
  120.4 21.3 %collective-permute-start.17 = (bf16[2,80,2048]{2,1,0:T(8,128)(2,1)}, bf16[2,80,2048]{2,1,0:T(8,128)(2,1)}, u32[]{:S(2)}, u32[]{:S(2)}) collective-permute-start(bf16[2,80,2048]{2,1,0:T(8,128)(2,1)} %copy-done.6), channel_id=1, source_target_pairs={{1,2},{2,3},{5,6},{6,7},{9,10},{10,11},{13,14},{14,15},{17,18},{18... | collective-permute-start | bytes 1966088 | tf_op jit(solution)/shard_map/ppermute | solution.py:26
  121.9 19.8 %collective-permute-start.18 = (bf16[2,80,2048]{2,1,0:T(8,128)(2,1)}, bf16[2,80,2048]{2,1,0:T(8,128)(2,1)}, u32[]{:S(2)}, u32[]{:S(2)}) collective-permute-start(bf16[2,80,2048]{2,1,0:T(8,128)(2,1)} %copy-done.4), channel_id=1, source_target_pairs={{1,0},{2,1},{5,4},{6,5},{9,8},{10,9},{13,12},{14,13},{17,16},{18,1... | collective-permute-start | bytes 1966088 | tf_op jit(solution)/shard_map/ppermute | solution.py:26
  135.5 16.0 %collective-permute-start.22 = (bf16[2,80,2048]{2,1,0:T(8,128)(2,1)}, bf16[2,80,2048]{2,1,0:T(8,128)(2,1)}, u32[]{:S(2)}, u32[]{:S(2)}) collective-permute-start(bf16[2,80,2048]{2,1,0:T(8,128)(2,1)} %get-tuple-element.135), channel_id=1, source_target_pairs={{0,1},{1,2},{4,5},{5,6},{8,9},{9,10},{12,13},{13,14},{16,17},{17,1... | collective-permute-start | bytes 1966088 | tf_op jit(solution)/shard_map/ppermute | solution.py:26
  141.8 21.4 %collective-permute-start.29 = (bf16[2,80,2048]{2,1,0:T(8,128)(2,1)}, bf16[2,80,2048]{2,1,0:T(8,128)(2,1)S(1)}, u32[]{:S(2)}, u32[]{:S(2)}) collective-permute-start(bf16[2,80,2048]{2,1,0:T(8,128)(2,1)} %collective-permute-done.17), channel_id=1, source_target_pairs={{2,3},{6,7},{10,11},{14,15},{18,19},{22,23},{26,27},{30,31}} | collective-permute-start | bytes 1966088 | tf_op jit(solution)/shard_map/ppermute | solution.py:26
  142.5 20.7 %collective-permute-start.30 = (bf16[2,80,2048]{2,1,0:T(8,128)(2,1)}, bf16[2,80,2048]{2,1,0:T(8,128)(2,1)S(1)}, u32[]{:S(2)}, u32[]{:S(2)}) collective-permute-start(bf16[2,80,2048]{2,1,0:T(8,128)(2,1)} %collective-permute-done.18), channel_id=1, source_target_pairs={{1,0},{5,4},{9,8},{13,12},{17,16},{21,20},{25,24},{29,28}} | collective-permute-start | bytes 1966088 | tf_op jit(solution)/shard_map/ppermute | solution.py:26
  143.8 19.4 %collective-permute-start.31 = (bf16[128,4096]{1,0:T(8,128)(2,1)}, bf16[128,4096]{1,0:T(8,128)(2,1)S(1)}, u32[]{:S(2)}, u32[]{:S(2)}) collective-permute-start(bf16[128,4096]{1,0:T(8,128)(2,1)} %bitcast.202), channel_id=1, source_target_pairs={{0,24},{1,25},{2,26},{3,27},{4,28},{5,29},{6,30},{7,31},{8,0},{9,1... | collective-permute-start | bytes 3145736 | tf_op jit(solution)/shard_map/ppermute | solution.py:26
  153.1 22.0 %collective-permute-start.25 = (bf16[2,80,2048]{2,1,0:T(8,128)(2,1)S(1)}, bf16[2,80,2048]{2,1,0:T(8,128)(2,1)S(1)}, u32[]{:S(2)}, u32[]{:S(2)}) collective-permute-start(bf16[2,80,2048]{2,1,0:T(8,128)(2,1)S(1)} %add_convert_fusion), channel_id=1, source_target_pairs={{1,0},{2,1},{3,2},{5,4},{6,5},{7,6},{9,8},{10,9},{11,10},{13,12},{... | collective-permute-start | bytes 1966088 | tf_op jit(solution)/shard_map/ppermute | solution.py:26
  156.0 20.8 %collective-permute-start.24 = (bf16[2,80,2048]{2,1,0:T(8,128)(2,1)S(1)}, bf16[2,80,2048]{2,1,0:T(8,128)(2,1)S(1)}, u32[]{:S(2)}, u32[]{:S(2)}) collective-permute-start(bf16[2,80,2048]{2,1,0:T(8,128)(2,1)S(1)} %add_convert_fusion.1), channel_id=1, source_target_pairs={{0,1},{1,2},{2,3},{4,5},{5,6},{6,7},{8,9},{9,10},{10,11},{12,13},{... | collective-permute-start | bytes 1966088 | tf_op jit(solution)/shard_map/ppermute | solution.py:26
  168.6 16.1 %collective-permute-start.32 = (bf16[4,80,1024]{2,1,0:T(8,128)(2,1)S(1)}, bf16[4,80,1024]{2,1,0:T(8,128)(2,1)S(1)}, u32[]{:S(2)}, u32[]{:S(2)}) collective-permute-start(bf16[4,80,1024]{2,1,0:T(8,128)(2,1)S(1)} %dynamic-slice_bitcast_fusion.1), channel_id=1, source_target_pairs={{0,4},{1,5},{2,6},{3,7},{4,0},{5,1},{6,2},{7,3},{8,12},{9,13},{10,... | collective-permute-start | bytes 1966088 | tf_op jit(solution)/shard_map/ppermute | solution.py:26
  177.3 25.5 %collective-permute-start.27 = (bf16[2,80,1024]{2,1,0:T(8,128)(2,1)S(1)}, bf16[2,80,1024]{2,1,0:T(8,128)(2,1)S(1)}, u32[]{:S(2)}, u32[]{:S(2)}) collective-permute-start(bf16[2,80,1024]{2,1,0:T(8,128)(2,1)S(1)} %fusion.32), channel_id=1, source_target_pairs={{0,2},{1,3},{2,0},{3,1},{4,6},{5,7},{6,4},{7,5},{8,10},{9,11},{10,... | collective-permute-start | bytes 983048 | tf_op jit(solution)/shard_map/ppermute | solution.py:26
  181.0 21.8 %collective-permute-start.26 = (bf16[2,80,1024]{2,1,0:T(8,128)(2,1)S(1)}, bf16[2,80,1024]{2,1,0:T(8,128)(2,1)S(1)}, u32[]{:S(2)}, u32[]{:S(2)}) collective-permute-start(bf16[2,80,1024]{2,1,0:T(8,128)(2,1)S(1)} %fusion.32), channel_id=1, source_target_pairs={{0,3},{1,0},{2,1},{3,2},{4,7},{5,4},{6,5},{7,6},{8,11},{9,8},{10,9... | collective-permute-start | bytes 983048 | tf_op jit(solution)/shard_map/ppermute | solution.py:26
  182.2 20.6 %collective-permute-start.28 = (bf16[2,80,1024]{2,1,0:T(8,128)(2,1)S(1)}, bf16[2,80,1024]{2,1,0:T(8,128)(2,1)S(1)}, u32[]{:S(2)}, u32[]{:S(2)}) collective-permute-start(bf16[2,80,1024]{2,1,0:T(8,128)(2,1)S(1)} %fusion.32), channel_id=1, source_target_pairs={{0,1},{1,2},{2,3},{3,0},{4,5},{5,6},{6,7},{7,4},{8,9},{9,10},{10,1... | collective-permute-start | bytes 983048 | tf_op jit(solution)/shard_map/ppermute | solution.py:26
  206.1 20.2 %collective-permute-start.40 = (bf16[128,1024]{1,0:T(8,128)(2,1)S(1)}, bf16[128,1024]{1,0:T(8,128)(2,1)S(1)}, u32[]{:S(2)}, u32[]{:S(2)}) collective-permute-start(bf16[128,1024]{1,0:T(8,128)(2,1)S(1)} %get-tuple-element.129), channel_id=1, source_target_pairs={{0,27},{1,24},{2,25},{3,26},{4,31},{5,28},{6,29},{7,30},{8,3},{9,0... | collective-permute-start | bytes 786440 | tf_op jit(solution)/shard_map/ppermute | solution.py:26
  208.4 36.1 %collective-permute-start.39 = (bf16[128,1024]{1,0:T(8,128)(2,1)S(1)}, bf16[128,1024]{1,0:T(8,128)(2,1)S(1)}, u32[]{:S(2)}, u32[]{:S(2)}) collective-permute-start(bf16[128,1024]{1,0:T(8,128)(2,1)S(1)} %get-tuple-element.130), channel_id=1, source_target_pairs={{0,25},{1,26},{2,27},{3,24},{4,29},{5,30},{6,31},{7,28},{8,1},{9,2... | collective-permute-start | bytes 786440 | tf_op jit(solution)/shard_map/ppermute | solution.py:26
  212.3 35.9 %collective-permute-start.38 = (bf16[128,1024]{1,0:T(8,128)(2,1)S(1)}, bf16[128,1024]{1,0:T(8,128)(2,1)S(1)}, u32[]{:S(2)}, u32[]{:S(2)}) collective-permute-start(bf16[128,1024]{1,0:T(8,128)(2,1)S(1)} %get-tuple-element.131), channel_id=1, source_target_pairs={{0,26},{1,27},{2,24},{3,25},{4,30},{5,31},{6,28},{7,29},{8,2},{9,3... | collective-permute-start | bytes 786440 | tf_op jit(solution)/shard_map/ppermute | solution.py:26
  219.3 31.4 %collective-permute-start.37 = (bf16[128,1024]{1,0:T(8,128)(2,1)S(1)}, bf16[128,1024]{1,0:T(8,128)(2,1)S(1)}, u32[]{:S(2)}, u32[]{:S(2)}) collective-permute-start(bf16[128,1024]{1,0:T(8,128)(2,1)S(1)} %get-tuple-element.120), channel_id=1, source_target_pairs={{0,8},{1,9},{2,10},{3,11},{4,12},{5,13},{6,14},{7,15},{8,16},{9,17... | collective-permute-start | bytes 786440 | tf_op jit(solution)/shard_map/ppermute | solution.py:26
  219.4 33.1 %collective-permute-start.34 = (bf16[128,1024]{1,0:T(8,128)(2,1)S(1)}, bf16[128,1024]{1,0:T(8,128)(2,1)S(1)}, u32[]{:S(2)}, u32[]{:S(2)}) collective-permute-start(bf16[128,1024]{1,0:T(8,128)(2,1)S(1)} %get-tuple-element.121), channel_id=1, source_target_pairs={{0,10},{1,11},{2,8},{3,9},{4,14},{5,15},{6,12},{7,13},{8,18},{9,19... | collective-permute-start | bytes 786440 | tf_op jit(solution)/shard_map/ppermute | solution.py:26
  226.4 26.1 %collective-permute-start.35 = (bf16[128,1024]{1,0:T(8,128)(2,1)S(1)}, bf16[128,1024]{1,0:T(8,128)(2,1)S(1)}, u32[]{:S(2)}, u32[]{:S(2)}) collective-permute-start(bf16[128,1024]{1,0:T(8,128)(2,1)S(1)} %get-tuple-element.122), channel_id=1, source_target_pairs={{0,9},{1,10},{2,11},{3,8},{4,13},{5,14},{6,15},{7,12},{8,17},{9,18... | collective-permute-start | bytes 786440 | tf_op jit(solution)/shard_map/ppermute | solution.py:26
  (26 other events, 286.3 us)

commit v4 on v0

--- a/solution.py
+++ b/solution.py
@@ -323,8 +323,8 @@
     hidden = (jax.nn.silu(preact[..., :hidden_units]) * preact[..., hidden_units:]).astype(BF16)
     all_hidden = [move(hidden, by_local=-m) for m in (1, 2, 3)]
     merged_b = merge(own_b, got_b, node, tokens_here)
-    h1, h2, h3, merged_b = join(*all_hidden, merged_b)
-    all_hidden = jnp.stack([hidden, h1, h2, h3])
+    h2, merged_b = join(all_hidden[1], merged_b)
+    all_hidden = jnp.stack([hidden, all_hidden[0], h2, all_hidden[2]])
     home_b = send(homeward(merged_b, -1))
     done_a = jnp.dot(
         all_hidden.reshape(-1, hidden_units), w_dn, preferred_element_type=F32

time: 261 us -> 261 us (level)
  no operation moved by 1% of the time
where the time goes in v4:
time: 261 us; the launch traced here: 259 us
  starting transfers between devices  103 us (39%)
  waiting for transfers between devices  96.6 us (37%)
  other arithmetic  19.9 us (8%)
  matrix products  18.6 us (7%)
  local copies, waits for them, and re-layouts  9.71 us (4%)
  Pallas kernels  6.78 us (3%)
  between operations  4.28 us (2%)
    ppermute x42, starting transfers between devices, move(): return lax.ppermute(value, AXES, pairs)  103 us
    ppermute x42, waiting for transfers between devices, move(): return lax.ppermute(value, AXES, pairs)  96.6 us
    unnamed x48, local copies, waits for them, and re-layouts  7.49 us
    dot_general x4, matrix products, cut(): jnp.dot(placer, block, preferred_element_type=F32).astype(BF16)  6.86 us
    convert_element_type x3, other arithmetic, sums(): right, left = (right.astype(BF16), left.astype(BF16))  5.79 us
    pallas_call x2, Pallas kernels, finish(): pl.pallas_call(finish_kernel, out_shape=jax.ShapeDtypeStruct((1, tokens,...  5.68 us
  transfers between devices with their start and end apart: 42, of which 15 were waited for; matrix products, arithmetic and copies ran while one was open for 14% of the time, Pallas kernels for 1%

profile of v4, /device:TPU:0, one launch (start us, length us, event | category | flops | bytes accessed | tf_op | source)
XLA Modules:
  0.0 259.3 jit_solution(3004494539891435556)
XLA Ops:
  4.5 4.1 %collective-permute-start = (bf16[128,1024]{1,0:T(8,128)(2,1)S(1)}, bf16[128,1024]{1,0:T(8,128)(2,1)}, u32[]{:S(2)}, u32[]{:S(2)}) collective-permute-start(bf16[128,1024]{1,0:T(8,128)(2,1)S(1)} %get-tuple-element.54), channel_id=1, source_target_pairs={{0,2},{1,3},{2,0},{3,1},{4,6},{5,7},{6,4},{7,5},{8,10},{9,11},{10,... | collective-permute-start | bytes 786440 | tf_op jit(solution)/shard_map/ppermute | solution.py:26
  31.6 6.0 %collective-permute-start.9 = (bf16[128,1024]{1,0:T(8,128)(2,1)S(1)}, bf16[128,1024]{1,0:T(8,128)(2,1)S(1)}, u32[]{:S(2)}, u32[]{:S(2)}) collective-permute-start(bf16[128,1024]{1,0:T(8,128)(2,1)S(1)} %copy-done.19), channel_id=1, source_target_pairs={{0,2},{1,3},{2,0},{3,1},{4,6},{5,7},{6,4},{7,5},{8,10},{9,11},{10,... | collective-permute-start | bytes 786440 | tf_op jit(solution)/shard_map/ppermute | solution.py:26
  40.7 4.5 %collective-permute-done.5 = bf16[4,80,1024]{2,1,0:T(8,128)(2,1)S(1)} collective-permute-done((bf16[4,80,1024]{2,1,0:T(8,128)(2,1)S(1)}, bf16[4,80,1024]{2,1,0:T(8,128)(2,1)S(1)}, u32[]{:S(2)}, u32[]{:S(2)}) %collective-permute-start.5) | collective-permute-done | bytes 655392 | tf_op jit(solution)/shard_map/ppermute | solution.py:26
  47.2 3.2 %collective-permute-start.8 = (bf16[2,80,1024]{2,1,0:T(8,128)(2,1)S(1)}, bf16[2,80,1024]{2,1,0:T(8,128)(2,1)S(1)}, u32[]{:S(2)}, u32[]{:S(2)}) collective-permute-start(bf16[2,80,1024]{2,1,0:T(8,128)(2,1)S(1)} %bitcast.212), channel_id=1, source_target_pairs={{0,3},{1,0},{2,1},{3,2},{4,7},{5,4},{6,5},{7,6},{8,11},{9,8},{10,9... | collective-permute-start | bytes 983048 | tf_op jit(solution)/shard_map/ppermute | solution.py:26
  50.4 2.4 collective-permute-start.7
  52.8 4.0 %collective-permute-start.6 = (bf16[2,80,1024]{2,1,0:T(8,128)(2,1)S(1)}, bf16[2,80,1024]{2,1,0:T(8,128)(2,1)S(1)}, u32[]{:S(2)}, u32[]{:S(2)}) collective-permute-start(bf16[2,80,1024]{2,1,0:T(8,128)(2,1)S(1)} %bitcast.210), channel_id=1, source_target_pairs={{0,2},{1,3},{2,0},{3,1},{4,6},{5,7},{6,4},{7,5},{8,10},{9,11},{10,... | collective-permute-start | bytes 983048 | tf_op jit(solution)/shard_map/ppermute | solution.py:26
  58.3 10.5 %collective-permute-done.8 = bf16[2,80,1024]{2,1,0:T(8,128)(2,1)S(1)} collective-permute-done((bf16[2,80,1024]{2,1,0:T(8,128)(2,1)S(1)}, bf16[2,80,1024]{2,1,0:T(8,128)(2,1)S(1)}, u32[]{:S(2)}, u32[]{:S(2)}) %collective-permute-start.8) | collective-permute-done | bytes 327712 | tf_op jit(solution)/shard_map/ppermute | solution.py:26
  68.8 3.2 %collective-permute-done.7 = bf16[2,80,1024]{2,1,0:T(8,128)(2,1)S(1)} collective-permute-done((bf16[2,80,1024]{2,1,0:T(8,128)(2,1)S(1)}, bf16[2,80,1024]{2,1,0:T(8,128)(2,1)S(1)}, u32[]{:S(2)}, u32[]{:S(2)}) %collective-permute-start.7) | collective-permute-done | bytes 327712 | tf_op jit(solution)/shard_map/ppermute | solution.py:26
  72.0 16.8 %collective-permute-done.6 = bf16[2,80,1024]{2,1,0:T(8,128)(2,1)S(1)} collective-permute-done((bf16[2,80,1024]{2,1,0:T(8,128)(2,1)S(1)}, bf16[2,80,1024]{2,1,0:T(8,128)(2,1)S(1)}, u32[]{:S(2)}, u32[]{:S(2)}) %collective-permute-start.6) | collective-permute-done | bytes 327712 | tf_op jit(solution)/shard_map/ppermute | solution.py:26
  92.1 4.6 %collective-permute-start.12 = (bf16[2,80,2048]{2,1,0:T(8,128)(2,1)S(1)}, bf16[2,80,2048]{2,1,0:T(8,128)(2,1)S(1)}, u32[]{:S(2)}, u32[]{:S(2)}) collective-permute-start(bf16[2,80,2048]{2,1,0:T(8,128)(2,1)S(1)} %pad_maximum_fusion.6), channel_id=1, source_target_pairs={{0,1},{1,2},{2,3},{4,5},{5,6},{6,7},{8,9},{9,10},{10,11},{12,13},{... | collective-permute-start | bytes 1966088 | tf_op jit(solution)/shard_map/ppermute | solution.py:26
  97.2 8.5 %collective-permute-done.14 = bf16[4,80,1024]{2,1,0:T(8,128)(2,1)S(1)} collective-permute-done((bf16[4,80,1024]{2,1,0:T(8,128)(2,1)S(1)}, bf16[4,80,1024]{2,1,0:T(8,128)(2,1)S(1)}, u32[]{:S(2)}, u32[]{:S(2)}) %collective-permute-start.14) | collective-permute-done | bytes 655392 | tf_op jit(solution)/shard_map/ppermute | solution.py:26
  108.0 3.1 %fusion.4 = bf16[640,2048]{1,0:T(8,128)(2,1)S(1)} fusion(bf16[640,1024]{1,0:T(8,128)(2,1)S(1)} %bitcast.202, bf16[1,1,1024,2048]{3,2,1,0:T(8,128)(2,1)S(1)} %copy-done.21), kind=kOutput, calls=%fused_computation.4 | convolution fusion | flops 2685665280 | bytes 8126464 | tf_op jit(solution)/shard_map/dot_general | solution.py:302
  114.3 4.1 %collective-permute-start.20 = (bf16[2,80,2048]{2,1,0:T(8,128)(2,1)}, bf16[2,80,2048]{2,1,0:T(8,128)(2,1)}, u32[]{:S(2)}, u32[]{:S(2)}) collective-permute-start(bf16[2,80,2048]{2,1,0:T(8,128)(2,1)} %bitcast.50), channel_id=1, source_target_pairs={{0,1},{4,5},{8,9},{12,13},{16,17},{20,21},{24,25},{28,29}} | collective-permute-start | bytes 1966088 | tf_op jit(solution)/shard_map/ppermute | solution.py:26
  122.7 7.8 %collective-permute-done.20 = bf16[2,80,2048]{2,1,0:T(8,128)(2,1)} collective-permute-done((bf16[2,80,2048]{2,1,0:T(8,128)(2,1)}, bf16[2,80,2048]{2,1,0:T(8,128)(2,1)}, u32[]{:S(2)}, u32[]{:S(2)}) %collective-permute-start.20) | collective-permute-done | bytes 655392 | tf_op jit(solution)/shard_map/ppermute | solution.py:26
  130.5 3.0 %fusion.21 = (bf16[2,80,2048]{2,1,0:T(8,128)(2,1)}, bf16[2,80,2048]{2,1,0:T(8,128)(2,1)}) fusion(bf16[2,80,2048]{2,1,0:T(8,128)(2,1)} %bitcast.199, bf16[2,80,2048]{2,1,0:T(8,128)(2,1)} %collective-permute-done.21, bf16[2,80,2048]{2,1,0:T(8,128)(2,1)} %collective-permute-done.20), kind=kLoop, calls=%fused_computation.17 | loop fusion | flops 2293760 | bytes 3276800 | tf_op jit(solution)/shard_map/convert_element_type | solution.py:84
  135.0 5.0 %collective-permute-start.22 = (bf16[2,80,2048]{2,1,0:T(8,128)(2,1)}, bf16[2,80,2048]{2,1,0:T(8,128)(2,1)}, u32[]{:S(2)}, u32[]{:S(2)}) collective-permute-start(bf16[2,80,2048]{2,1,0:T(8,128)(2,1)} %get-tuple-element.131), channel_id=1, source_target_pairs={{0,1},{1,2},{4,5},{5,6},{8,9},{9,10},{12,13},{13,14},{16,17},{17,1... | collective-permute-start | bytes 1966088 | tf_op jit(solution)/shard_map/ppermute | solution.py:26
  145.1 6.1 %collective-permute-done.22 = bf16[2,80,2048]{2,1,0:T(8,128)(2,1)} collective-permute-done((bf16[2,80,2048]{2,1,0:T(8,128)(2,1)}, bf16[2,80,2048]{2,1,0:T(8,128)(2,1)}, u32[]{:S(2)}, u32[]{:S(2)}) %collective-permute-start.22) | collective-permute-done | bytes 655392 | tf_op jit(solution)/shard_map/ppermute | solution.py:26
  155.4 7.0 %collective-permute-start.24 = (bf16[2,80,2048]{2,1,0:T(8,128)(2,1)S(1)}, bf16[2,80,2048]{2,1,0:T(8,128)(2,1)S(1)}, u32[]{:S(2)}, u32[]{:S(2)}) collective-permute-start(bf16[2,80,2048]{2,1,0:T(8,128)(2,1)S(1)} %add_convert_fusion.1), channel_id=1, source_target_pairs={{0,1},{1,2},{2,3},{4,5},{5,6},{6,7},{8,9},{9,10},{10,11},{12,13},{... | collective-permute-start | bytes 1966088 | tf_op jit(solution)/shard_map/ppermute | solution.py:26
  164.9 2.9 %fusion.11 = bf16[640,1024]{1,0:T(8,128)(2,1)S(1)} fusion(bf16[640,2048]{1,0:T(8,128)(2,1)S(1)} %bitcast.195, bf16[1,1,1024,2048]{3,2,1,0:T(8,128)(2,1)S(1)} %copy-done.22), kind=kOutput, calls=%fused_computation.13 | convolution fusion | flops 2685009920 | bytes 8126464 | tf_op jit(solution)/shard_map/dot_general | solution.py:51
  169.0 5.5 %collective-permute-done.25 = bf16[2,80,2048]{2,1,0:T(8,128)(2,1)S(1)} collective-permute-done((bf16[2,80,2048]{2,1,0:T(8,128)(2,1)S(1)}, bf16[2,80,2048]{2,1,0:T(8,128)(2,1)S(1)}, u32[]{:S(2)}, u32[]{:S(2)}) %collective-permute-start.25) | collective-permute-done | bytes 655392 | tf_op jit(solution)/shard_map/ppermute | solution.py:26
  176.5 3.7 %collective-permute-start.27 = (bf16[2,80,1024]{2,1,0:T(8,128)(2,1)S(1)}, bf16[2,80,1024]{2,1,0:T(8,128)(2,1)S(1)}, u32[]{:S(2)}, u32[]{:S(2)}) collective-permute-start(bf16[2,80,1024]{2,1,0:T(8,128)(2,1)S(1)} %fusion.32), channel_id=1, source_target_pairs={{0,2},{1,3},{2,0},{3,1},{4,6},{5,7},{6,4},{7,5},{8,10},{9,11},{10,... | collective-permute-start | bytes 983048 | tf_op jit(solution)/shard_map/ppermute | solution.py:26
  184.1 17.8 %collective-permute-done.27 = bf16[2,80,1024]{2,1,0:T(8,128)(2,1)S(1)} collective-permute-done((bf16[2,80,1024]{2,1,0:T(8,128)(2,1)S(1)}, bf16[2,80,1024]{2,1,0:T(8,128)(2,1)S(1)}, u32[]{:S(2)}, u32[]{:S(2)}) %collective-permute-start.27) | collective-permute-done | bytes 327712 | tf_op jit(solution)/shard_map/ppermute | solution.py:26
  205.2 2.2 collective-permute-start.40
  207.4 3.9 %collective-permute-start.39 = (bf16[128,1024]{1,0:T(8,128)(2,1)S(1)}, bf16[128,1024]{1,0:T(8,128)(2,1)S(1)}, u32[]{:S(2)}, u32[]{:S(2)}) collective-permute-start(bf16[128,1024]{1,0:T(8,128)(2,1)S(1)} %get-tuple-element.126), channel_id=1, source_target_pairs={{0,25},{1,26},{2,27},{3,24},{4,29},{5,30},{6,31},{7,28},{8,1},{9,2... | collective-permute-start | bytes 786440 | tf_op jit(solution)/shard_map/ppermute | solution.py:26
  211.4 3.2 %collective-permute-start.38 = (bf16[128,1024]{1,0:T(8,128)(2,1)S(1)}, bf16[128,1024]{1,0:T(8,128)(2,1)S(1)}, u32[]{:S(2)}, u32[]{:S(2)}) collective-permute-start(bf16[128,1024]{1,0:T(8,128)(2,1)S(1)} %get-tuple-element.127), channel_id=1, source_target_pairs={{0,26},{1,27},{2,24},{3,25},{4,30},{5,31},{6,28},{7,29},{8,2},{9,3... | collective-permute-start | bytes 786440 | tf_op jit(solution)/shard_map/ppermute | solution.py:26
  214.6 3.5 %collective-permute-done.33 = bf16[4,80,1024]{2,1,0:T(8,128)(2,1)S(1)} collective-permute-done((bf16[4,80,1024]{2,1,0:T(8,128)(2,1)S(1)}, bf16[4,80,1024]{2,1,0:T(8,128)(2,1)S(1)}, u32[]{:S(2)}, u32[]{:S(2)}) %collective-permute-start.33) | collective-permute-done | bytes 655392 | tf_op jit(solution)/shard_map/ppermute | solution.py:26
  218.4 6.6 %collective-permute-start.34 = (bf16[128,1024]{1,0:T(8,128)(2,1)S(1)}, bf16[128,1024]{1,0:T(8,128)(2,1)S(1)}, u32[]{:S(2)}, u32[]{:S(2)}) collective-permute-start(bf16[128,1024]{1,0:T(8,128)(2,1)S(1)} %get-tuple-element.117), channel_id=1, source_target_pairs={{0,10},{1,11},{2,8},{3,9},{4,14},{5,15},{6,12},{7,13},{8,18},{9,19... | collective-permute-start | bytes 786440 | tf_op jit(solution)/shard_map/ppermute | solution.py:26
  225.0 18.7 %collective-permute-start.35 = (bf16[128,1024]{1,0:T(8,128)(2,1)S(1)}, bf16[128,1024]{1,0:T(8,128)(2,1)S(1)}, u32[]{:S(2)}, u32[]{:S(2)}) collective-permute-start(bf16[128,1024]{1,0:T(8,128)(2,1)S(1)} %get-tuple-element.118), channel_id=1, source_target_pairs={{0,9},{1,10},{2,11},{3,8},{4,13},{5,14},{6,15},{7,12},{8,17},{9,18... | collective-permute-start | bytes 786440 | tf_op jit(solution)/shard_map/ppermute | solution.py:26
  243.9 3.5 %collective-permute-done.38.refs_0_ = bf16[128,1024]{1,0:T(8,128)(2,1)S(1)} collective-permute-done((bf16[128,1024]{1,0:T(8,128)(2,1)S(1)}, bf16[128,1024]{1,0:T(8,128)(2,1)S(1)}, u32[]{:S(2)}, u32[]{:S(2)}) %collective-permute-start.38) | collective-permute-done | bytes 262176 | tf_op jit(solution)/shard_map/ppermute | solution.py:26
  247.4 2.5 finish.3
  251.4 4.5 %collective-permute-done.36.refs_2_ = bf16[128,1024]{1,0:T(8,128)(2,1)S(1)} collective-permute-done((bf16[128,1024]{1,0:T(8,128)(2,1)S(1)}, bf16[128,1024]{1,0:T(8,128)(2,1)S(1)}, u32[]{:S(2)}, u32[]{:S(2)}) %collective-permute-start.36) | collective-permute-done | bytes 262176 | tf_op jit(solution)/shard_map/ppermute | solution.py:26
  255.9 3.2 %finish.2 = bf16[1,128,4096]{2,1,0:T(8,128)(2,1)} custom-call(s32[4]{0:T(128)S(1)} %pad_add_fusion.2.at_ref, f32[1,128]{1,0:T(1,128)S(1)} %get-tuple-element.133.weight_ref, bf16[128,128]{1,0:T(8,128)(2,1)S(1)} %fusion.50.pick_ref, bf16[128,4096]{1,0:T(8,128)(2,1)} %collective-permute-done.19.residual_ref, ...), custom_call_target="tpu_custom_call" | custom-call | tf_op jit(solution)/shard_map/finish/pallas_call | solution.py:216
  (167 shorter events, 69.4 us)
Async XLA Ops:
  4.5 24.1 %collective-permute-start = (bf16[128,1024]{1,0:T(8,128)(2,1)S(1)}, bf16[128,1024]{1,0:T(8,128)(2,1)}, u32[]{:S(2)}, u32[]{:S(2)}) collective-permute-start(bf16[128,1024]{1,0:T(8,128)(2,1)S(1)} %get-tuple-element.54), channel_id=1, source_target_pairs={{0,2},{1,3},{2,0},{3,1},{4,6},{5,7},{6,4},{7,5},{8,10},{9,11},{10,... | collective-permute-start | bytes 786440 | tf_op jit(solution)/shard_map/ppermute | solution.py:26
  8.6 20.0 %collective-permute-start.1 = (bf16[128,1024]{1,0:T(8,128)(2,1)S(1)}, bf16[128,1024]{1,0:T(8,128)(2,1)}, u32[]{:S(2)}, u32[]{:S(2)}) collective-permute-start(bf16[128,1024]{1,0:T(8,128)(2,1)S(1)} %get-tuple-element.55), channel_id=1, source_target_pairs={{0,3},{1,0},{2,1},{3,2},{4,7},{5,4},{6,5},{7,6},{8,11},{9,8},{10,9... | collective-permute-start | bytes 786440 | tf_op jit(solution)/shard_map/ppermute | solution.py:26
  10.0 18.6 %collective-permute-start.2 = (bf16[128,1024]{1,0:T(8,128)(2,1)S(1)}, bf16[128,1024]{1,0:T(8,128)(2,1)}, u32[]{:S(2)}, u32[]{:S(2)}) collective-permute-start(bf16[128,1024]{1,0:T(8,128)(2,1)S(1)} %get-tuple-element.56), channel_id=1, source_target_pairs={{0,1},{1,2},{2,3},{3,0},{4,5},{5,6},{6,7},{7,4},{8,9},{9,10},{10,1... | collective-permute-start | bytes 786440 | tf_op jit(solution)/shard_map/ppermute | solution.py:26
  31.6 21.2 %collective-permute-start.9 = (bf16[128,1024]{1,0:T(8,128)(2,1)S(1)}, bf16[128,1024]{1,0:T(8,128)(2,1)S(1)}, u32[]{:S(2)}, u32[]{:S(2)}) collective-permute-start(bf16[128,1024]{1,0:T(8,128)(2,1)S(1)} %copy-done.19), channel_id=1, source_target_pairs={{0,2},{1,3},{2,0},{3,1},{4,6},{5,7},{6,4},{7,5},{8,10},{9,11},{10,... | collective-permute-start | bytes 786440 | tf_op jit(solution)/shard_map/ppermute | solution.py:26
  37.6 20.7 %collective-permute-start.10 = (bf16[128,1024]{1,0:T(8,128)(2,1)S(1)}, bf16[128,1024]{1,0:T(8,128)(2,1)S(1)}, u32[]{:S(2)}, u32[]{:S(2)}) collective-permute-start(bf16[128,1024]{1,0:T(8,128)(2,1)S(1)} %copy-done.18), channel_id=1, source_target_pairs={{0,3},{1,0},{2,1},{3,2},{4,7},{5,4},{6,5},{7,6},{8,11},{9,8},{10,9... | collective-permute-start | bytes 786440 | tf_op jit(solution)/shard_map/ppermute | solution.py:26
  38.0 20.3 %collective-permute-start.11 = (bf16[128,1024]{1,0:T(8,128)(2,1)S(1)}, bf16[128,1024]{1,0:T(8,128)(2,1)S(1)}, u32[]{:S(2)}, u32[]{:S(2)}) collective-permute-start(bf16[128,1024]{1,0:T(8,128)(2,1)S(1)} %copy-done.17), channel_id=1, source_target_pairs={{0,1},{1,2},{2,3},{3,0},{4,5},{5,6},{6,7},{7,4},{8,9},{9,10},{10,1... | collective-permute-start | bytes 786440 | tf_op jit(solution)/shard_map/ppermute | solution.py:26
  47.2 21.6 %collective-permute-start.8 = (bf16[2,80,1024]{2,1,0:T(8,128)(2,1)S(1)}, bf16[2,80,1024]{2,1,0:T(8,128)(2,1)S(1)}, u32[]{:S(2)}, u32[]{:S(2)}) collective-permute-start(bf16[2,80,1024]{2,1,0:T(8,128)(2,1)S(1)} %bitcast.212), channel_id=1, source_target_pairs={{0,3},{1,0},{2,1},{3,2},{4,7},{5,4},{6,5},{7,6},{8,11},{9,8},{10,9... | collective-permute-start | bytes 983048 | tf_op jit(solution)/shard_map/ppermute | solution.py:26
  50.4 21.6 %collective-permute-start.7 = (bf16[2,80,1024]{2,1,0:T(8,128)(2,1)S(1)}, bf16[2,80,1024]{2,1,0:T(8,128)(2,1)S(1)}, u32[]{:S(2)}, u32[]{:S(2)}) collective-permute-start(bf16[2,80,1024]{2,1,0:T(8,128)(2,1)S(1)} %bitcast.211), channel_id=1, source_target_pairs={{0,1},{1,2},{2,3},{3,0},{4,5},{5,6},{6,7},{7,4},{8,9},{9,10},{10,1... | collective-permute-start | bytes 983048 | tf_op jit(solution)/shard_map/ppermute | solution.py:26
  52.8 36.0 %collective-permute-start.6 = (bf16[2,80,1024]{2,1,0:T(8,128)(2,1)S(1)}, bf16[2,80,1024]{2,1,0:T(8,128)(2,1)S(1)}, u32[]{:S(2)}, u32[]{:S(2)}) collective-permute-start(bf16[2,80,1024]{2,1,0:T(8,128)(2,1)S(1)} %bitcast.210), channel_id=1, source_target_pairs={{0,2},{1,3},{2,0},{3,1},{4,6},{5,7},{6,4},{7,5},{8,10},{9,11},{10,... | collective-permute-start | bytes 983048 | tf_op jit(solution)/shard_map/ppermute | solution.py:26
  89.0 16.7 %collective-permute-start.14 = (bf16[4,80,1024]{2,1,0:T(8,128)(2,1)S(1)}, bf16[4,80,1024]{2,1,0:T(8,128)(2,1)S(1)}, u32[]{:S(2)}, u32[]{:S(2)}) collective-permute-start(bf16[4,80,1024]{2,1,0:T(8,128)(2,1)S(1)} %broadcast_select_fusion), channel_id=1, source_target_pairs={{0,4},{1,5},{2,6},{3,7},{4,0},{5,1},{6,2},{7,3},{8,12},{9,13},{10,... | collective-permute-start | bytes 1966088 | tf_op jit(solution)/shard_map/ppermute | solution.py:26
  90.8 20.4 %collective-permute-start.13 = (bf16[2,80,2048]{2,1,0:T(8,128)(2,1)S(1)}, bf16[2,80,2048]{2,1,0:T(8,128)(2,1)S(1)}, u32[]{:S(2)}, u32[]{:S(2)}) collective-permute-start(bf16[2,80,2048]{2,1,0:T(8,128)(2,1)S(1)} %pad_maximum_fusion.6), channel_id=1, source_target_pairs={{1,0},{2,1},{3,2},{5,4},{6,5},{7,6},{9,8},{10,9},{11,10},{13,12},{... | collective-permute-start | bytes 1966088 | tf_op jit(solution)/shard_map/ppermute | solution.py:26
  92.1 19.1 %collective-permute-start.12 = (bf16[2,80,2048]{2,1,0:T(8,128)(2,1)S(1)}, bf16[2,80,2048]{2,1,0:T(8,128)(2,1)S(1)}, u32[]{:S(2)}, u32[]{:S(2)}) collective-permute-start(bf16[2,80,2048]{2,1,0:T(8,128)(2,1)S(1)} %pad_maximum_fusion.6), channel_id=1, source_target_pairs={{0,1},{1,2},{2,3},{4,5},{5,6},{6,7},{8,9},{9,10},{10,11},{12,13},{... | collective-permute-start | bytes 1966088 | tf_op jit(solution)/shard_map/ppermute | solution.py:26
  114.3 16.1 %collective-permute-start.20 = (bf16[2,80,2048]{2,1,0:T(8,128)(2,1)}, bf16[2,80,2048]{2,1,0:T(8,128)(2,1)}, u32[]{:S(2)}, u32[]{:S(2)}) collective-permute-start(bf16[2,80,2048]{2,1,0:T(8,128)(2,1)} %bitcast.50), channel_id=1, source_target_pairs={{0,1},{4,5},{8,9},{12,13},{16,17},{20,21},{24,25},{28,29}} | collective-permute-start | bytes 1966088 | tf_op jit(solution)/shard_map/ppermute | solution.py:26
  118.4 23.0 %collective-permute-start.19 = (bf16[128,4096]{1,0:T(8,128)(2,1)}, bf16[128,4096]{1,0:T(8,128)(2,1)}, u32[]{:S(2)}, u32[]{:S(2)}) collective-permute-start(bf16[128,4096]{1,0:T(8,128)(2,1)} %bitcast.49), channel_id=1, source_target_pairs={{0,8},{1,9},{2,10},{3,11},{4,12},{5,13},{6,14},{7,15},{8,16},{9,17... | collective-permute-start | bytes 3145736 | tf_op jit(solution)/shard_map/ppermute | solution.py:26
  119.8 21.6 %collective-permute-start.17 = (bf16[2,80,2048]{2,1,0:T(8,128)(2,1)}, bf16[2,80,2048]{2,1,0:T(8,128)(2,1)}, u32[]{:S(2)}, u32[]{:S(2)}) collective-permute-start(bf16[2,80,2048]{2,1,0:T(8,128)(2,1)} %copy-done.15), channel_id=1, source_target_pairs={{1,2},{2,3},{5,6},{6,7},{9,10},{10,11},{13,14},{14,15},{17,18},{18... | collective-permute-start | bytes 1966088 | tf_op jit(solution)/shard_map/ppermute | solution.py:26
  121.4 20.0 %collective-permute-start.18 = (bf16[2,80,2048]{2,1,0:T(8,128)(2,1)}, bf16[2,80,2048]{2,1,0:T(8,128)(2,1)}, u32[]{:S(2)}, u32[]{:S(2)}) collective-permute-start(bf16[2,80,2048]{2,1,0:T(8,128)(2,1)} %copy-done.13), channel_id=1, source_target_pairs={{1,0},{2,1},{5,4},{6,5},{9,8},{10,9},{13,12},{14,13},{17,16},{18,1... | collective-permute-start | bytes 1966088 | tf_op jit(solution)/shard_map/ppermute | solution.py:26
  135.0 16.2 %collective-permute-start.22 = (bf16[2,80,2048]{2,1,0:T(8,128)(2,1)}, bf16[2,80,2048]{2,1,0:T(8,128)(2,1)}, u32[]{:S(2)}, u32[]{:S(2)}) collective-permute-start(bf16[2,80,2048]{2,1,0:T(8,128)(2,1)} %get-tuple-element.131), channel_id=1, source_target_pairs={{0,1},{1,2},{4,5},{5,6},{8,9},{9,10},{12,13},{13,14},{16,17},{17,1... | collective-permute-start | bytes 1966088 | tf_op jit(solution)/shard_map/ppermute | solution.py:26
  141.4 21.0 %collective-permute-start.28 = (bf16[2,80,2048]{2,1,0:T(8,128)(2,1)}, bf16[2,80,2048]{2,1,0:T(8,128)(2,1)S(1)}, u32[]{:S(2)}, u32[]{:S(2)}) collective-permute-start(bf16[2,80,2048]{2,1,0:T(8,128)(2,1)} %collective-permute-done.17), channel_id=1, source_target_pairs={{2,3},{6,7},{10,11},{14,15},{18,19},{22,23},{26,27},{30,31}} | collective-permute-start | bytes 1966088 | tf_op jit(solution)/shard_map/ppermute | solution.py:26
  142.1 20.3 %collective-permute-start.29 = (bf16[2,80,2048]{2,1,0:T(8,128)(2,1)}, bf16[2,80,2048]{2,1,0:T(8,128)(2,1)S(1)}, u32[]{:S(2)}, u32[]{:S(2)}) collective-permute-start(bf16[2,80,2048]{2,1,0:T(8,128)(2,1)} %collective-permute-done.18), channel_id=1, source_target_pairs={{1,0},{5,4},{9,8},{13,12},{17,16},{21,20},{25,24},{29,28}} | collective-permute-start | bytes 1966088 | tf_op jit(solution)/shard_map/ppermute | solution.py:26
  143.5 19.0 %collective-permute-start.30 = (bf16[128,4096]{1,0:T(8,128)(2,1)S(1)}, bf16[128,4096]{1,0:T(8,128)(2,1)S(1)}, u32[]{:S(2)}, u32[]{:S(2)}) collective-permute-start(bf16[128,4096]{1,0:T(8,128)(2,1)S(1)} %bitcast.189), channel_id=1, source_target_pairs={{0,24},{1,25},{2,26},{3,27},{4,28},{5,29},{6,30},{7,31},{8,0},{9,1... | collective-permute-start | bytes 3145736 | tf_op jit(solution)/shard_map/ppermute | solution.py:26
  152.7 21.8 %collective-permute-start.25 = (bf16[2,80,2048]{2,1,0:T(8,128)(2,1)S(1)}, bf16[2,80,2048]{2,1,0:T(8,128)(2,1)S(1)}, u32[]{:S(2)}, u32[]{:S(2)}) collective-permute-start(bf16[2,80,2048]{2,1,0:T(8,128)(2,1)S(1)} %add_convert_fusion), channel_id=1, source_target_pairs={{1,0},{2,1},{3,2},{5,4},{6,5},{7,6},{9,8},{10,9},{11,10},{13,12},{... | collective-permute-start | bytes 1966088 | tf_op jit(solution)/shard_map/ppermute | solution.py:26
  155.4 20.5 %collective-permute-start.24 = (bf16[2,80,2048]{2,1,0:T(8,128)(2,1)S(1)}, bf16[2,80,2048]{2,1,0:T(8,128)(2,1)S(1)}, u32[]{:S(2)}, u32[]{:S(2)}) collective-permute-start(bf16[2,80,2048]{2,1,0:T(8,128)(2,1)S(1)} %add_convert_fusion.1), channel_id=1, source_target_pairs={{0,1},{1,2},{2,3},{4,5},{5,6},{6,7},{8,9},{9,10},{10,11},{12,13},{... | collective-permute-start | bytes 1966088 | tf_op jit(solution)/shard_map/ppermute | solution.py:26
  167.8 16.0 %collective-permute-start.31 = (bf16[4,80,1024]{2,1,0:T(8,128)(2,1)S(1)}, bf16[4,80,1024]{2,1,0:T(8,128)(2,1)S(1)}, u32[]{:S(2)}, u32[]{:S(2)}) collective-permute-start(bf16[4,80,1024]{2,1,0:T(8,128)(2,1)S(1)} %dynamic-slice_bitcast_fusion.1), channel_id=1, source_target_pairs={{0,4},{1,5},{2,6},{3,7},{4,0},{5,1},{6,2},{7,3},{8,12},{9,13},{10,... | collective-permute-start | bytes 1966088 | tf_op jit(solution)/shard_map/ppermute | solution.py:26
  176.5 25.4 %collective-permute-start.27 = (bf16[2,80,1024]{2,1,0:T(8,128)(2,1)S(1)}, bf16[2,80,1024]{2,1,0:T(8,128)(2,1)S(1)}, u32[]{:S(2)}, u32[]{:S(2)}) collective-permute-start(bf16[2,80,1024]{2,1,0:T(8,128)(2,1)S(1)} %fusion.32), channel_id=1, source_target_pairs={{0,2},{1,3},{2,0},{3,1},{4,6},{5,7},{6,4},{7,5},{8,10},{9,11},{10,... | collective-permute-start | bytes 983048 | tf_op jit(solution)/shard_map/ppermute | solution.py:26
  180.2 21.7 %collective-permute-start.26 = (bf16[2,80,1024]{2,1,0:T(8,128)(2,1)S(1)}, bf16[2,80,1024]{2,1,0:T(8,128)(2,1)S(1)}, u32[]{:S(2)}, u32[]{:S(2)}) collective-permute-start(bf16[2,80,1024]{2,1,0:T(8,128)(2,1)S(1)} %fusion.32), channel_id=1, source_target_pairs={{0,3},{1,0},{2,1},{3,2},{4,7},{5,4},{6,5},{7,6},{8,11},{9,8},{10,9... | collective-permute-start | bytes 983048 | tf_op jit(solution)/shard_map/ppermute | solution.py:26
  181.4 20.5 %collective-permute-start.32 = (bf16[2,80,1024]{2,1,0:T(8,128)(2,1)S(1)}, bf16[2,80,1024]{2,1,0:T(8,128)(2,1)S(1)}, u32[]{:S(2)}, u32[]{:S(2)}) collective-permute-start(bf16[2,80,1024]{2,1,0:T(8,128)(2,1)S(1)} %fusion.32), channel_id=1, source_target_pairs={{0,1},{1,2},{2,3},{3,0},{4,5},{5,6},{6,7},{7,4},{8,9},{9,10},{10,1... | collective-permute-start | bytes 983048 | tf_op jit(solution)/shard_map/ppermute | solution.py:26
  205.2 19.7 %collective-permute-start.40 = (bf16[128,1024]{1,0:T(8,128)(2,1)S(1)}, bf16[128,1024]{1,0:T(8,128)(2,1)S(1)}, u32[]{:S(2)}, u32[]{:S(2)}) collective-permute-start(bf16[128,1024]{1,0:T(8,128)(2,1)S(1)} %get-tuple-element.125), channel_id=1, source_target_pairs={{0,27},{1,24},{2,25},{3,26},{4,31},{5,28},{6,29},{7,30},{8,3},{9,0... | collective-permute-start | bytes 786440 | tf_op jit(solution)/shard_map/ppermute | solution.py:26
  207.4 36.2 %collective-permute-start.39 = (bf16[128,1024]{1,0:T(8,128)(2,1)S(1)}, bf16[128,1024]{1,0:T(8,128)(2,1)S(1)}, u32[]{:S(2)}, u32[]{:S(2)}) collective-permute-start(bf16[128,1024]{1,0:T(8,128)(2,1)S(1)} %get-tuple-element.126), channel_id=1, source_target_pairs={{0,25},{1,26},{2,27},{3,24},{4,29},{5,30},{6,31},{7,28},{8,1},{9,2... | collective-permute-start | bytes 786440 | tf_op jit(solution)/shard_map/ppermute | solution.py:26
  211.4 36.0 %collective-permute-start.38 = (bf16[128,1024]{1,0:T(8,128)(2,1)S(1)}, bf16[128,1024]{1,0:T(8,128)(2,1)S(1)}, u32[]{:S(2)}, u32[]{:S(2)}) collective-permute-start(bf16[128,1024]{1,0:T(8,128)(2,1)S(1)} %get-tuple-element.127), channel_id=1, source_target_pairs={{0,26},{1,27},{2,24},{3,25},{4,30},{5,31},{6,28},{7,29},{8,2},{9,3... | collective-permute-start | bytes 786440 | tf_op jit(solution)/shard_map/ppermute | solution.py:26
  218.3 31.6 %collective-permute-start.37 = (bf16[128,1024]{1,0:T(8,128)(2,1)S(1)}, bf16[128,1024]{1,0:T(8,128)(2,1)S(1)}, u32[]{:S(2)}, u32[]{:S(2)}) collective-permute-start(bf16[128,1024]{1,0:T(8,128)(2,1)S(1)} %get-tuple-element.116), channel_id=1, source_target_pairs={{0,8},{1,9},{2,10},{3,11},{4,12},{5,13},{6,14},{7,15},{8,16},{9,17... | collective-permute-start | bytes 786440 | tf_op jit(solution)/shard_map/ppermute | solution.py:26
  218.4 33.0 %collective-permute-start.34 = (bf16[128,1024]{1,0:T(8,128)(2,1)S(1)}, bf16[128,1024]{1,0:T(8,128)(2,1)S(1)}, u32[]{:S(2)}, u32[]{:S(2)}) collective-permute-start(bf16[128,1024]{1,0:T(8,128)(2,1)S(1)} %get-tuple-element.117), channel_id=1, source_target_pairs={{0,10},{1,11},{2,8},{3,9},{4,14},{5,15},{6,12},{7,13},{8,18},{9,19... | collective-permute-start | bytes 786440 | tf_op jit(solution)/shard_map/ppermute | solution.py:26
  225.0 26.5 %collective-permute-start.35 = (bf16[128,1024]{1,0:T(8,128)(2,1)S(1)}, bf16[128,1024]{1,0:T(8,128)(2,1)S(1)}, u32[]{:S(2)}, u32[]{:S(2)}) collective-permute-start(bf16[128,1024]{1,0:T(8,128)(2,1)S(1)} %get-tuple-element.118), channel_id=1, source_target_pairs={{0,9},{1,10},{2,11},{3,8},{4,13},{5,14},{6,15},{7,12},{8,17},{9,18... | collective-permute-start | bytes 786440 | tf_op jit(solution)/shard_map/ppermute | solution.py:26
  (34 other events, 329.7 us)

commit v5 on v4

--- a/solution.py
+++ b/solution.py
@@ -265,7 +265,7 @@
     saved_got = move(saved_other, by_node=1)
     (zeros_wait,) = after([zeros], saved_other)
     zeros_got = move(zeros_wait, by_node=1)
-    cut_a = cut(act, sort_a, local)
+    cut_a = scaled_cut(act, jnp.ones((tokens_here,), F32), route_a, local)
     *got_b, saved_got, zeros_got, a0, a1, a2, a3 = join(*got_b, saved_got, zeros_got, *cut_a)
     cut_a = [a0, a1, a2, a3]
     zeros = by_node(zeros, zeros_got, 0)
@@ -323,8 +323,8 @@
     hidden = (jax.nn.silu(preact[..., :hidden_units]) * preact[..., hidden_units:]).astype(BF16)
     all_hidden = [move(hidden, by_local=-m) for m in (1, 2, 3)]
     merged_b = merge(own_b, got_b, node, tokens_here)
-    h2, merged_b = join(all_hidden[1], merged_b)
-    all_hidden = jnp.stack([hidden, all_hidden[0], h2, all_hidden[2]])
+    h1, merged_b = join(all_hidden[0], merged_b)
+    all_hidden = jnp.stack([hidden, h1, *all_hidden[1:]])
     home_b = send(homeward(merged_b, -1))
     done_a = jnp.dot(
         all_hidden.reshape(-1, hidden_units), w_dn, preferred_element_type=F32

time: 261 us -> 262 us (level)
  matrix products: 18.6 us -> 10.9 us
  waiting for transfers between devices: 96.6 us -> 102 us
  starting transfers between devices: 103 us -> 106 us
    dot_general x4 -> x0, matrix products: 6.86 us -> none  [cut(): jnp.dot(placer, block, preferred_element_type=F32).astype(BF16)]
    ppermute x42, waiting for transfers between devices: 96.6 us -> 102 us  [move(): return lax.ppermute(value, AXES, pairs)]
    unnamed x48 -> x42, local copies, waits for them, and re-layouts: 7.49 us -> 7.45 us
  transfers between devices with their start and end apart: 42 -> 42, of which waited for: 15 -> 18; matrix products, arithmetic and copies ran while one was open for 14% -> 11% of each run, Pallas kernels for 1% -> 1%
where the time goes in v5:
time: 262 us; the launch traced here: 261 us
  starting transfers between devices  106 us (40%)
  waiting for transfers between devices  102 us (39%)
  other arithmetic  19.5 us (7%)
  matrix products  10.9 us (4%)
  local copies, waits for them, and re-layouts  9.93 us (4%)
  Pallas kernels  8.65 us (3%)
  between operations  3.44 us (1%)
    ppermute x42, starting transfers between devices, move(): return lax.ppermute(value, AXES, pairs)  106 us
    ppermute x42, waiting for transfers between devices, move(): return lax.ppermute(value, AXES, pairs)  102 us
    unnamed x42, local copies, waits for them, and re-layouts  7.45 us
    convert_element_type x3, other arithmetic, sums(): right, left = (right.astype(BF16), left.astype(BF16))  5.89 us
    pallas_call x2, Pallas kernels, finish(): pl.pallas_call(finish_kernel, out_shape=jax.ShapeDtypeStruct((1, tokens,...  5.67 us
  transfers between devices with their start and end apart: 42, of which 18 were waited for; matrix products, arithmetic and copies ran while one was open for 11% of the time, Pallas kernels for 1%

profile of v5, /device:TPU:0, one launch (start us, length us, event | category | flops | bytes accessed | tf_op | source)
XLA Modules:
  0.0 260.5 jit_solution(8995615343644864543)
XLA Ops:
  5.3 4.0 %collective-permute-start = (bf16[128,1024]{1,0:T(8,128)(2,1)}, bf16[128,1024]{1,0:T(8,128)(2,1)}, u32[]{:S(2)}, u32[]{:S(2)}) collective-permute-start(bf16[128,1024]{1,0:T(8,128)(2,1)} %get-tuple-element.58), channel_id=1, source_target_pairs={{0,2},{1,3},{2,0},{3,1},{4,6},{5,7},{6,4},{7,5},{8,10},{9,11},{10,... | collective-permute-start | bytes 786440 | tf_op jit(solution)/shard_map/ppermute | solution.py:26
  21.5 3.1 %collective-permute-done.4 = f32[2]{0:T(128)S(1)} collective-permute-done((f32[2]{0:T(128)S(1)}, f32[2]{0:T(128)S(1)}, u32[]{:S(2)}, u32[]{:S(2)}) %collective-permute-start.4) | collective-permute-done | bytes 40 | tf_op jit(solution)/shard_map/ppermute | solution.py:26
  24.6 3.8 %collective-permute-done.2 = bf16[128,1024]{1,0:T(8,128)(2,1)} collective-permute-done((bf16[128,1024]{1,0:T(8,128)(2,1)}, bf16[128,1024]{1,0:T(8,128)(2,1)}, u32[]{:S(2)}, u32[]{:S(2)}) %collective-permute-start.2) | collective-permute-done | bytes 262176 | tf_op jit(solution)/shard_map/ppermute | solution.py:26
  31.4 7.1 %collective-permute-start.9 = (bf16[128,1024]{1,0:T(8,128)(2,1)S(1)}, bf16[128,1024]{1,0:T(8,128)(2,1)S(1)}, u32[]{:S(2)}, u32[]{:S(2)}) collective-permute-start(bf16[128,1024]{1,0:T(8,128)(2,1)S(1)} %get-tuple-element.72), channel_id=1, source_target_pairs={{0,2},{1,3},{2,0},{3,1},{4,6},{5,7},{6,4},{7,5},{8,10},{9,11},{10,... | collective-permute-start | bytes 786440 | tf_op jit(solution)/shard_map/ppermute | solution.py:26
  41.6 3.8 %collective-permute-done.5 = bf16[4,80,1024]{2,1,0:T(8,128)(2,1)S(1)} collective-permute-done((bf16[4,80,1024]{2,1,0:T(8,128)(2,1)S(1)}, bf16[4,80,1024]{2,1,0:T(8,128)(2,1)S(1)}, u32[]{:S(2)}, u32[]{:S(2)}) %collective-permute-start.5) | collective-permute-done | bytes 655392 | tf_op jit(solution)/shard_map/ppermute | solution.py:26
  47.5 3.5 %collective-permute-start.8 = (bf16[2,80,1024]{2,1,0:T(8,128)(2,1)S(1)}, bf16[2,80,1024]{2,1,0:T(8,128)(2,1)S(1)}, u32[]{:S(2)}, u32[]{:S(2)}) collective-permute-start(bf16[2,80,1024]{2,1,0:T(8,128)(2,1)S(1)} %bitcast.186), channel_id=1, source_target_pairs={{0,3},{1,0},{2,1},{3,2},{4,7},{5,4},{6,5},{7,6},{8,11},{9,8},{10,9... | collective-permute-start | bytes 983048 | tf_op jit(solution)/shard_map/ppermute | solution.py:26
  53.9 3.9 %collective-permute-start.6 = (bf16[2,80,1024]{2,1,0:T(8,128)(2,1)S(1)}, bf16[2,80,1024]{2,1,0:T(8,128)(2,1)S(1)}, u32[]{:S(2)}, u32[]{:S(2)}) collective-permute-start(bf16[2,80,1024]{2,1,0:T(8,128)(2,1)S(1)} %bitcast.184), channel_id=1, source_target_pairs={{0,2},{1,3},{2,0},{3,1},{4,6},{5,7},{6,4},{7,5},{8,10},{9,11},{10,... | collective-permute-start | bytes 983048 | tf_op jit(solution)/shard_map/ppermute | solution.py:26
  59.3 10.1 %collective-permute-done.8 = bf16[2,80,1024]{2,1,0:T(8,128)(2,1)S(1)} collective-permute-done((bf16[2,80,1024]{2,1,0:T(8,128)(2,1)S(1)}, bf16[2,80,1024]{2,1,0:T(8,128)(2,1)S(1)}, u32[]{:S(2)}, u32[]{:S(2)}) %collective-permute-start.8) | collective-permute-done | bytes 327712 | tf_op jit(solution)/shard_map/ppermute | solution.py:26
  69.4 3.5 %collective-permute-done.7 = bf16[2,80,1024]{2,1,0:T(8,128)(2,1)S(1)} collective-permute-done((bf16[2,80,1024]{2,1,0:T(8,128)(2,1)S(1)}, bf16[2,80,1024]{2,1,0:T(8,128)(2,1)S(1)}, u32[]{:S(2)}, u32[]{:S(2)}) %collective-permute-start.7) | collective-permute-done | bytes 327712 | tf_op jit(solution)/shard_map/ppermute | solution.py:26
  72.9 16.8 %collective-permute-done.6 = bf16[2,80,1024]{2,1,0:T(8,128)(2,1)S(1)} collective-permute-done((bf16[2,80,1024]{2,1,0:T(8,128)(2,1)S(1)}, bf16[2,80,1024]{2,1,0:T(8,128)(2,1)S(1)}, u32[]{:S(2)}, u32[]{:S(2)}) %collective-permute-start.6) | collective-permute-done | bytes 327712 | tf_op jit(solution)/shard_map/ppermute | solution.py:26
  92.7 4.6 %collective-permute-start.12 = (bf16[2,80,2048]{2,1,0:T(8,128)(2,1)S(1)}, bf16[2,80,2048]{2,1,0:T(8,128)(2,1)S(1)}, u32[]{:S(2)}, u32[]{:S(2)}) collective-permute-start(bf16[2,80,2048]{2,1,0:T(8,128)(2,1)S(1)} %pad_maximum_fusion.6), channel_id=1, source_target_pairs={{0,1},{1,2},{2,3},{4,5},{5,6},{6,7},{8,9},{9,10},{10,11},{12,13},{... | collective-permute-start | bytes 1966088 | tf_op jit(solution)/shard_map/ppermute | solution.py:26
  97.9 8.6 %collective-permute-done.14 = bf16[4,80,1024]{2,1,0:T(8,128)(2,1)S(1)} collective-permute-done((bf16[4,80,1024]{2,1,0:T(8,128)(2,1)S(1)}, bf16[4,80,1024]{2,1,0:T(8,128)(2,1)S(1)}, u32[]{:S(2)}, u32[]{:S(2)}) %collective-permute-start.14) | collective-permute-done | bytes 655392 | tf_op jit(solution)/shard_map/ppermute | solution.py:26
  108.8 3.1 %fusion.4 = bf16[640,2048]{1,0:T(8,128)(2,1)S(1)} fusion(bf16[640,1024]{1,0:T(8,128)(2,1)S(1)} %bitcast.177, bf16[1,1,1024,2048]{3,2,1,0:T(8,128)(2,1)S(1)} %copy-done.19), kind=kOutput, calls=%fused_computation.4 | convolution fusion | flops 2685665280 | bytes 8126464 | tf_op jit(solution)/shard_map/dot_general | solution.py:302
  115.4 3.8 %collective-permute-start.20 = (bf16[2,80,2048]{2,1,0:T(8,128)(2,1)}, bf16[2,80,2048]{2,1,0:T(8,128)(2,1)}, u32[]{:S(2)}, u32[]{:S(2)}) collective-permute-start(bf16[2,80,2048]{2,1,0:T(8,128)(2,1)} %bitcast.42), channel_id=1, source_target_pairs={{0,1},{4,5},{8,9},{12,13},{16,17},{20,21},{24,25},{28,29}} | collective-permute-start | bytes 1966088 | tf_op jit(solution)/shard_map/ppermute | solution.py:26
  123.3 7.8 %collective-permute-done.20 = bf16[2,80,2048]{2,1,0:T(8,128)(2,1)} collective-permute-done((bf16[2,80,2048]{2,1,0:T(8,128)(2,1)}, bf16[2,80,2048]{2,1,0:T(8,128)(2,1)}, u32[]{:S(2)}, u32[]{:S(2)}) %collective-permute-start.20) | collective-permute-done | bytes 655392 | tf_op jit(solution)/shard_map/ppermute | solution.py:26
  131.1 2.9 %fusion.21 = (bf16[2,80,2048]{2,1,0:T(8,128)(2,1)}, bf16[2,80,2048]{2,1,0:T(8,128)(2,1)}) fusion(bf16[2,80,2048]{2,1,0:T(8,128)(2,1)} %bitcast.174, bf16[2,80,2048]{2,1,0:T(8,128)(2,1)} %collective-permute-done.21, bf16[2,80,2048]{2,1,0:T(8,128)(2,1)} %collective-permute-done.20), kind=kLoop, calls=%fused_computation.17 | loop fusion | flops 2293760 | bytes 3276800 | tf_op jit(solution)/shard_map/convert_element_type | solution.py:84
  135.6 5.0 %collective-permute-start.22 = (bf16[2,80,2048]{2,1,0:T(8,128)(2,1)}, bf16[2,80,2048]{2,1,0:T(8,128)(2,1)}, u32[]{:S(2)}, u32[]{:S(2)}) collective-permute-start(bf16[2,80,2048]{2,1,0:T(8,128)(2,1)} %get-tuple-element.139), channel_id=1, source_target_pairs={{0,1},{1,2},{4,5},{5,6},{8,9},{9,10},{12,13},{13,14},{16,17},{17,1... | collective-permute-start | bytes 1966088 | tf_op jit(solution)/shard_map/ppermute | solution.py:26
  145.7 6.0 %collective-permute-done.22 = bf16[2,80,2048]{2,1,0:T(8,128)(2,1)} collective-permute-done((bf16[2,80,2048]{2,1,0:T(8,128)(2,1)}, bf16[2,80,2048]{2,1,0:T(8,128)(2,1)}, u32[]{:S(2)}, u32[]{:S(2)}) %collective-permute-start.22) | collective-permute-done | bytes 655392 | tf_op jit(solution)/shard_map/ppermute | solution.py:26
  156.1 7.2 %collective-permute-start.24 = (bf16[2,80,2048]{2,1,0:T(8,128)(2,1)S(1)}, bf16[2,80,2048]{2,1,0:T(8,128)(2,1)S(1)}, u32[]{:S(2)}, u32[]{:S(2)}) collective-permute-start(bf16[2,80,2048]{2,1,0:T(8,128)(2,1)S(1)} %add_convert_fusion.1), channel_id=1, source_target_pairs={{0,1},{1,2},{2,3},{4,5},{5,6},{6,7},{8,9},{9,10},{10,11},{12,13},{... | collective-permute-start | bytes 1966088 | tf_op jit(solution)/shard_map/ppermute | solution.py:26
  165.7 2.9 %fusion.11 = bf16[640,1024]{1,0:T(8,128)(2,1)S(1)} fusion(bf16[640,2048]{1,0:T(8,128)(2,1)S(1)} %bitcast.172, bf16[1,1,1024,2048]{3,2,1,0:T(8,128)(2,1)S(1)} %copy-done.20), kind=kOutput, calls=%fused_computation.13 | convolution fusion | flops 2685009920 | bytes 8126464 | tf_op jit(solution)/shard_map/dot_general | solution.py:51
  170.1 5.0 %collective-permute-done.25 = bf16[2,80,2048]{2,1,0:T(8,128)(2,1)S(1)} collective-permute-done((bf16[2,80,2048]{2,1,0:T(8,128)(2,1)S(1)}, bf16[2,80,2048]{2,1,0:T(8,128)(2,1)S(1)}, u32[]{:S(2)}, u32[]{:S(2)}) %collective-permute-start.25) | collective-permute-done | bytes 655392 | tf_op jit(solution)/shard_map/ppermute | solution.py:26
  177.4 3.7 %collective-permute-start.31 = (bf16[2,80,1024]{2,1,0:T(8,128)(2,1)S(1)}, bf16[2,80,1024]{2,1,0:T(8,128)(2,1)S(1)}, u32[]{:S(2)}, u32[]{:S(2)}) collective-permute-start(bf16[2,80,1024]{2,1,0:T(8,128)(2,1)S(1)} %fusion.32), channel_id=1, source_target_pairs={{0,2},{1,3},{2,0},{3,1},{4,6},{5,7},{6,4},{7,5},{8,10},{9,11},{10,... | collective-permute-start | bytes 983048 | tf_op jit(solution)/shard_map/ppermute | solution.py:26
  185.0 11.3 %collective-permute-done.26 = bf16[2,80,1024]{2,1,0:T(8,128)(2,1)S(1)} collective-permute-done((bf16[2,80,1024]{2,1,0:T(8,128)(2,1)S(1)}, bf16[2,80,1024]{2,1,0:T(8,128)(2,1)S(1)}, u32[]{:S(2)}, u32[]{:S(2)}) %collective-permute-start.26) | collective-permute-done | bytes 327712 | tf_op jit(solution)/shard_map/ppermute | solution.py:26
  196.3 6.6 %collective-permute-done.31 = bf16[2,80,1024]{2,1,0:T(8,128)(2,1)S(1)} collective-permute-done((bf16[2,80,1024]{2,1,0:T(8,128)(2,1)S(1)}, bf16[2,80,1024]{2,1,0:T(8,128)(2,1)S(1)}, u32[]{:S(2)}, u32[]{:S(2)}) %collective-permute-start.31) | collective-permute-done | bytes 327712 | tf_op jit(solution)/shard_map/ppermute | solution.py:26
  208.7 3.9 %collective-permute-start.39 = (bf16[128,1024]{1,0:T(8,128)(2,1)S(1)}, bf16[128,1024]{1,0:T(8,128)(2,1)S(1)}, u32[]{:S(2)}, u32[]{:S(2)}) collective-permute-start(bf16[128,1024]{1,0:T(8,128)(2,1)S(1)} %get-tuple-element.134), channel_id=1, source_target_pairs={{0,25},{1,26},{2,27},{3,24},{4,29},{5,30},{6,31},{7,28},{8,1},{9,2... | collective-permute-start | bytes 786440 | tf_op jit(solution)/shard_map/ppermute | solution.py:26
  212.6 3.4 %collective-permute-start.38 = (bf16[128,1024]{1,0:T(8,128)(2,1)S(1)}, bf16[128,1024]{1,0:T(8,128)(2,1)S(1)}, u32[]{:S(2)}, u32[]{:S(2)}) collective-permute-start(bf16[128,1024]{1,0:T(8,128)(2,1)S(1)} %get-tuple-element.135), channel_id=1, source_target_pairs={{0,26},{1,27},{2,24},{3,25},{4,30},{5,31},{6,28},{7,29},{8,2},{9,3... | collective-permute-start | bytes 786440 | tf_op jit(solution)/shard_map/ppermute | solution.py:26
  216.0 3.1 %collective-permute-done.33 = bf16[4,80,1024]{2,1,0:T(8,128)(2,1)S(1)} collective-permute-done((bf16[4,80,1024]{2,1,0:T(8,128)(2,1)S(1)}, bf16[4,80,1024]{2,1,0:T(8,128)(2,1)S(1)}, u32[]{:S(2)}, u32[]{:S(2)}) %collective-permute-start.33) | collective-permute-done | bytes 655392 | tf_op jit(solution)/shard_map/ppermute | solution.py:26
  219.5 6.9 %collective-permute-start.34 = (bf16[128,1024]{1,0:T(8,128)(2,1)S(1)}, bf16[128,1024]{1,0:T(8,128)(2,1)S(1)}, u32[]{:S(2)}, u32[]{:S(2)}) collective-permute-start(bf16[128,1024]{1,0:T(8,128)(2,1)S(1)} %get-tuple-element.125), channel_id=1, source_target_pairs={{0,10},{1,11},{2,8},{3,9},{4,14},{5,15},{6,12},{7,13},{8,18},{9,19... | collective-permute-start | bytes 786440 | tf_op jit(solution)/shard_map/ppermute | solution.py:26
  226.3 18.5 %collective-permute-start.35 = (bf16[128,1024]{1,0:T(8,128)(2,1)S(1)}, bf16[128,1024]{1,0:T(8,128)(2,1)S(1)}, u32[]{:S(2)}, u32[]{:S(2)}) collective-permute-start(bf16[128,1024]{1,0:T(8,128)(2,1)S(1)} %get-tuple-element.126), channel_id=1, source_target_pairs={{0,9},{1,10},{2,11},{3,8},{4,13},{5,14},{6,15},{7,12},{8,17},{9,18... | collective-permute-start | bytes 786440 | tf_op jit(solution)/shard_map/ppermute | solution.py:26
  245.1 3.5 %collective-permute-done.38.refs_0_ = bf16[128,1024]{1,0:T(8,128)(2,1)S(1)} collective-permute-done((bf16[128,1024]{1,0:T(8,128)(2,1)S(1)}, bf16[128,1024]{1,0:T(8,128)(2,1)S(1)}, u32[]{:S(2)}, u32[]{:S(2)}) %collective-permute-start.38) | collective-permute-done | bytes 262176 | tf_op jit(solution)/shard_map/ppermute | solution.py:26
  252.7 4.5 %collective-permute-done.36.refs_2_ = bf16[128,1024]{1,0:T(8,128)(2,1)S(1)} collective-permute-done((bf16[128,1024]{1,0:T(8,128)(2,1)S(1)}, bf16[128,1024]{1,0:T(8,128)(2,1)S(1)}, u32[]{:S(2)}, u32[]{:S(2)}) %collective-permute-start.36) | collective-permute-done | bytes 262176 | tf_op jit(solution)/shard_map/ppermute | solution.py:26
  257.2 3.2 %finish.2 = bf16[1,128,4096]{2,1,0:T(8,128)(2,1)} custom-call(s32[4]{0:T(128)S(1)} %pad_add_fusion.2.at_ref, f32[1,128]{1,0:T(1,128)S(1)} %get-tuple-element.141.weight_ref, bf16[128,128]{1,0:T(8,128)(2,1)S(1)} %fusion.42.pick_ref, bf16[128,4096]{1,0:T(8,128)(2,1)} %collective-permute-done.19.residual_ref, ...), custom_call_target="tpu_custom_call" | custom-call | tf_op jit(solution)/shard_map/finish/pallas_call | solution.py:216
  (156 shorter events, 71.8 us)
Async XLA Ops:
  5.3 19.3 %collective-permute-start = (bf16[128,1024]{1,0:T(8,128)(2,1)}, bf16[128,1024]{1,0:T(8,128)(2,1)}, u32[]{:S(2)}, u32[]{:S(2)}) collective-permute-start(bf16[128,1024]{1,0:T(8,128)(2,1)} %get-tuple-element.58), channel_id=1, source_target_pairs={{0,2},{1,3},{2,0},{3,1},{4,6},{5,7},{6,4},{7,5},{8,10},{9,11},{10,... | collective-permute-start | bytes 786440 | tf_op jit(solution)/shard_map/ppermute | solution.py:26
  9.4 15.3 %collective-permute-start.1 = (bf16[128,1024]{1,0:T(8,128)(2,1)}, bf16[128,1024]{1,0:T(8,128)(2,1)}, u32[]{:S(2)}, u32[]{:S(2)}) collective-permute-start(bf16[128,1024]{1,0:T(8,128)(2,1)} %get-tuple-element.59), channel_id=1, source_target_pairs={{0,3},{1,0},{2,1},{3,2},{4,7},{5,4},{6,5},{7,6},{8,11},{9,8},{10,9... | collective-permute-start | bytes 786440 | tf_op jit(solution)/shard_map/ppermute | solution.py:26
  10.7 17.7 %collective-permute-start.2 = (bf16[128,1024]{1,0:T(8,128)(2,1)}, bf16[128,1024]{1,0:T(8,128)(2,1)}, u32[]{:S(2)}, u32[]{:S(2)}) collective-permute-start(bf16[128,1024]{1,0:T(8,128)(2,1)} %get-tuple-element.60), channel_id=1, source_target_pairs={{0,1},{1,2},{2,3},{3,0},{4,5},{5,6},{6,7},{7,4},{8,9},{9,10},{10,1... | collective-permute-start | bytes 786440 | tf_op jit(solution)/shard_map/ppermute | solution.py:26
  29.8 15.6 %collective-permute-start.5 = (bf16[4,80,1024]{2,1,0:T(8,128)(2,1)S(1)}, bf16[4,80,1024]{2,1,0:T(8,128)(2,1)S(1)}, u32[]{:S(2)}, u32[]{:S(2)}) collective-permute-start(bf16[4,80,1024]{2,1,0:T(8,128)(2,1)S(1)} %broadcast_select_fusion.2), channel_id=1, source_target_pairs={{0,4},{1,5},{2,6},{3,7},{4,0},{5,1},{6,2},{7,3},{8,12},{9,13},{10,... | collective-permute-start | bytes 1966088 | tf_op jit(solution)/shard_map/ppermute | solution.py:26
  31.4 22.5 %collective-permute-start.9 = (bf16[128,1024]{1,0:T(8,128)(2,1)S(1)}, bf16[128,1024]{1,0:T(8,128)(2,1)S(1)}, u32[]{:S(2)}, u32[]{:S(2)}) collective-permute-start(bf16[128,1024]{1,0:T(8,128)(2,1)S(1)} %get-tuple-element.72), channel_id=1, source_target_pairs={{0,2},{1,3},{2,0},{3,1},{4,6},{5,7},{6,4},{7,5},{8,10},{9,11},{10,... | collective-permute-start | bytes 786440 | tf_op jit(solution)/shard_map/ppermute | solution.py:26
  38.5 20.8 %collective-permute-start.10 = (bf16[128,1024]{1,0:T(8,128)(2,1)S(1)}, bf16[128,1024]{1,0:T(8,128)(2,1)S(1)}, u32[]{:S(2)}, u32[]{:S(2)}) collective-permute-start(bf16[128,1024]{1,0:T(8,128)(2,1)S(1)} %get-tuple-element.73), channel_id=1, source_target_pairs={{0,3},{1,0},{2,1},{3,2},{4,7},{5,4},{6,5},{7,6},{8,11},{9,8},{10,9... | collective-permute-start | bytes 786440 | tf_op jit(solution)/shard_map/ppermute | solution.py:26
  39.0 20.3 %collective-permute-start.11 = (bf16[128,1024]{1,0:T(8,128)(2,1)S(1)}, bf16[128,1024]{1,0:T(8,128)(2,1)S(1)}, u32[]{:S(2)}, u32[]{:S(2)}) collective-permute-start(bf16[128,1024]{1,0:T(8,128)(2,1)S(1)} %get-tuple-element.74), channel_id=1, source_target_pairs={{0,1},{1,2},{2,3},{3,0},{4,5},{5,6},{6,7},{7,4},{8,9},{9,10},{10,1... | collective-permute-start | bytes 786440 | tf_op jit(solution)/shard_map/ppermute | solution.py:26
  47.5 21.9 %collective-permute-start.8 = (bf16[2,80,1024]{2,1,0:T(8,128)(2,1)S(1)}, bf16[2,80,1024]{2,1,0:T(8,128)(2,1)S(1)}, u32[]{:S(2)}, u32[]{:S(2)}) collective-permute-start(bf16[2,80,1024]{2,1,0:T(8,128)(2,1)S(1)} %bitcast.186), channel_id=1, source_target_pairs={{0,3},{1,0},{2,1},{3,2},{4,7},{5,4},{6,5},{7,6},{8,11},{9,8},{10,9... | collective-permute-start | bytes 983048 | tf_op jit(solution)/shard_map/ppermute | solution.py:26
  51.0 21.9 %collective-permute-start.7 = (bf16[2,80,1024]{2,1,0:T(8,128)(2,1)S(1)}, bf16[2,80,1024]{2,1,0:T(8,128)(2,1)S(1)}, u32[]{:S(2)}, u32[]{:S(2)}) collective-permute-start(bf16[2,80,1024]{2,1,0:T(8,128)(2,1)S(1)} %bitcast.185), channel_id=1, source_target_pairs={{0,1},{1,2},{2,3},{3,0},{4,5},{5,6},{6,7},{7,4},{8,9},{9,10},{10,1... | collective-permute-start | bytes 983048 | tf_op jit(solution)/shard_map/ppermute | solution.py:26
  53.9 35.8 %collective-permute-start.6 = (bf16[2,80,1024]{2,1,0:T(8,128)(2,1)S(1)}, bf16[2,80,1024]{2,1,0:T(8,128)(2,1)S(1)}, u32[]{:S(2)}, u32[]{:S(2)}) collective-permute-start(bf16[2,80,1024]{2,1,0:T(8,128)(2,1)S(1)} %bitcast.184), channel_id=1, source_target_pairs={{0,2},{1,3},{2,0},{3,1},{4,6},{5,7},{6,4},{7,5},{8,10},{9,11},{10,... | collective-permute-start | bytes 983048 | tf_op jit(solution)/shard_map/ppermute | solution.py:26
  89.9 16.6 %collective-permute-start.14 = (bf16[4,80,1024]{2,1,0:T(8,128)(2,1)S(1)}, bf16[4,80,1024]{2,1,0:T(8,128)(2,1)S(1)}, u32[]{:S(2)}, u32[]{:S(2)}) collective-permute-start(bf16[4,80,1024]{2,1,0:T(8,128)(2,1)S(1)} %broadcast_select_fusion), channel_id=1, source_target_pairs={{0,4},{1,5},{2,6},{3,7},{4,0},{5,1},{6,2},{7,3},{8,12},{9,13},{10,... | collective-permute-start | bytes 1966088 | tf_op jit(solution)/shard_map/ppermute | solution.py:26
  91.4 20.5 %collective-permute-start.13 = (bf16[2,80,2048]{2,1,0:T(8,128)(2,1)S(1)}, bf16[2,80,2048]{2,1,0:T(8,128)(2,1)S(1)}, u32[]{:S(2)}, u32[]{:S(2)}) collective-permute-start(bf16[2,80,2048]{2,1,0:T(8,128)(2,1)S(1)} %pad_maximum_fusion.6), channel_id=1, source_target_pairs={{1,0},{2,1},{3,2},{5,4},{6,5},{7,6},{9,8},{10,9},{11,10},{13,12},{... | collective-permute-start | bytes 1966088 | tf_op jit(solution)/shard_map/ppermute | solution.py:26
  92.7 19.3 %collective-permute-start.12 = (bf16[2,80,2048]{2,1,0:T(8,128)(2,1)S(1)}, bf16[2,80,2048]{2,1,0:T(8,128)(2,1)S(1)}, u32[]{:S(2)}, u32[]{:S(2)}) collective-permute-start(bf16[2,80,2048]{2,1,0:T(8,128)(2,1)S(1)} %pad_maximum_fusion.6), channel_id=1, source_target_pairs={{0,1},{1,2},{2,3},{4,5},{5,6},{6,7},{8,9},{9,10},{10,11},{12,13},{... | collective-permute-start | bytes 1966088 | tf_op jit(solution)/shard_map/ppermute | solution.py:26
  115.4 15.7 %collective-permute-start.20 = (bf16[2,80,2048]{2,1,0:T(8,128)(2,1)}, bf16[2,80,2048]{2,1,0:T(8,128)(2,1)}, u32[]{:S(2)}, u32[]{:S(2)}) collective-permute-start(bf16[2,80,2048]{2,1,0:T(8,128)(2,1)} %bitcast.42), channel_id=1, source_target_pairs={{0,1},{4,5},{8,9},{12,13},{16,17},{20,21},{24,25},{28,29}} | collective-permute-start | bytes 1966088 | tf_op jit(solution)/shard_map/ppermute | solution.py:26
  119.2 22.7 %collective-permute-start.19 = (bf16[128,4096]{1,0:T(8,128)(2,1)S(1)}, bf16[128,4096]{1,0:T(8,128)(2,1)}, u32[]{:S(2)}, u32[]{:S(2)}) collective-permute-start(bf16[128,4096]{1,0:T(8,128)(2,1)S(1)} %bitcast.162), channel_id=1, source_target_pairs={{0,8},{1,9},{2,10},{3,11},{4,12},{5,13},{6,14},{7,15},{8,16},{9,17... | collective-permute-start | bytes 3145736 | tf_op jit(solution)/shard_map/ppermute | solution.py:26
  120.5 21.4 %collective-permute-start.17 = (bf16[2,80,2048]{2,1,0:T(8,128)(2,1)}, bf16[2,80,2048]{2,1,0:T(8,128)(2,1)}, u32[]{:S(2)}, u32[]{:S(2)}) collective-permute-start(bf16[2,80,2048]{2,1,0:T(8,128)(2,1)} %copy-done.16), channel_id=1, source_target_pairs={{1,2},{2,3},{5,6},{6,7},{9,10},{10,11},{13,14},{14,15},{17,18},{18... | collective-permute-start | bytes 1966088 | tf_op jit(solution)/shard_map/ppermute | solution.py:26
  122.0 19.9 %collective-permute-start.18 = (bf16[2,80,2048]{2,1,0:T(8,128)(2,1)}, bf16[2,80,2048]{2,1,0:T(8,128)(2,1)}, u32[]{:S(2)}, u32[]{:S(2)}) collective-permute-start(bf16[2,80,2048]{2,1,0:T(8,128)(2,1)} %copy-done.14), channel_id=1, source_target_pairs={{1,0},{2,1},{5,4},{6,5},{9,8},{10,9},{13,12},{14,13},{17,16},{18,1... | collective-permute-start | bytes 1966088 | tf_op jit(solution)/shard_map/ppermute | solution.py:26
  135.6 16.1 %collective-permute-start.22 = (bf16[2,80,2048]{2,1,0:T(8,128)(2,1)}, bf16[2,80,2048]{2,1,0:T(8,128)(2,1)}, u32[]{:S(2)}, u32[]{:S(2)}) collective-permute-start(bf16[2,80,2048]{2,1,0:T(8,128)(2,1)} %get-tuple-element.139), channel_id=1, source_target_pairs={{0,1},{1,2},{4,5},{5,6},{8,9},{9,10},{12,13},{13,14},{16,17},{17,1... | collective-permute-start | bytes 1966088 | tf_op jit(solution)/shard_map/ppermute | solution.py:26
  141.9 21.4 %collective-permute-start.27 = (bf16[2,80,2048]{2,1,0:T(8,128)(2,1)}, bf16[2,80,2048]{2,1,0:T(8,128)(2,1)S(1)}, u32[]{:S(2)}, u32[]{:S(2)}) collective-permute-start(bf16[2,80,2048]{2,1,0:T(8,128)(2,1)} %collective-permute-done.17), channel_id=1, source_target_pairs={{2,3},{6,7},{10,11},{14,15},{18,19},{22,23},{26,27},{30,31}} | collective-permute-start | bytes 1966088 | tf_op jit(solution)/shard_map/ppermute | solution.py:26
  142.6 20.7 %collective-permute-start.28 = (bf16[2,80,2048]{2,1,0:T(8,128)(2,1)}, bf16[2,80,2048]{2,1,0:T(8,128)(2,1)S(1)}, u32[]{:S(2)}, u32[]{:S(2)}) collective-permute-start(bf16[2,80,2048]{2,1,0:T(8,128)(2,1)} %collective-permute-done.18), channel_id=1, source_target_pairs={{1,0},{5,4},{9,8},{13,12},{17,16},{21,20},{25,24},{29,28}} | collective-permute-start | bytes 1966088 | tf_op jit(solution)/shard_map/ppermute | solution.py:26
  143.9 19.4 %collective-permute-start.29 = (bf16[128,4096]{1,0:T(8,128)(2,1)}, bf16[128,4096]{1,0:T(8,128)(2,1)S(1)}, u32[]{:S(2)}, u32[]{:S(2)}) collective-permute-start(bf16[128,4096]{1,0:T(8,128)(2,1)} %bitcast.163), channel_id=1, source_target_pairs={{0,24},{1,25},{2,26},{3,27},{4,28},{5,29},{6,30},{7,31},{8,0},{9,1... | collective-permute-start | bytes 3145736 | tf_op jit(solution)/shard_map/ppermute | solution.py:26
  153.1 22.0 %collective-permute-start.25 = (bf16[2,80,2048]{2,1,0:T(8,128)(2,1)S(1)}, bf16[2,80,2048]{2,1,0:T(8,128)(2,1)S(1)}, u32[]{:S(2)}, u32[]{:S(2)}) collective-permute-start(bf16[2,80,2048]{2,1,0:T(8,128)(2,1)S(1)} %add_convert_fusion), channel_id=1, source_target_pairs={{1,0},{2,1},{3,2},{5,4},{6,5},{7,6},{9,8},{10,9},{11,10},{13,12},{... | collective-permute-start | bytes 1966088 | tf_op jit(solution)/shard_map/ppermute | solution.py:26
  156.1 20.8 %collective-permute-start.24 = (bf16[2,80,2048]{2,1,0:T(8,128)(2,1)S(1)}, bf16[2,80,2048]{2,1,0:T(8,128)(2,1)S(1)}, u32[]{:S(2)}, u32[]{:S(2)}) collective-permute-start(bf16[2,80,2048]{2,1,0:T(8,128)(2,1)S(1)} %add_convert_fusion.1), channel_id=1, source_target_pairs={{0,1},{1,2},{2,3},{4,5},{5,6},{6,7},{8,9},{9,10},{10,11},{12,13},{... | collective-permute-start | bytes 1966088 | tf_op jit(solution)/shard_map/ppermute | solution.py:26
  168.7 16.1 %collective-permute-start.30 = (bf16[4,80,1024]{2,1,0:T(8,128)(2,1)S(1)}, bf16[4,80,1024]{2,1,0:T(8,128)(2,1)S(1)}, u32[]{:S(2)}, u32[]{:S(2)}) collective-permute-start(bf16[4,80,1024]{2,1,0:T(8,128)(2,1)S(1)} %dynamic-slice_bitcast_fusion.1), channel_id=1, source_target_pairs={{0,4},{1,5},{2,6},{3,7},{4,0},{5,1},{6,2},{7,3},{8,12},{9,13},{10,... | collective-permute-start | bytes 1966088 | tf_op jit(solution)/shard_map/ppermute | solution.py:26
  177.4 25.5 %collective-permute-start.31 = (bf16[2,80,1024]{2,1,0:T(8,128)(2,1)S(1)}, bf16[2,80,1024]{2,1,0:T(8,128)(2,1)S(1)}, u32[]{:S(2)}, u32[]{:S(2)}) collective-permute-start(bf16[2,80,1024]{2,1,0:T(8,128)(2,1)S(1)} %fusion.32), channel_id=1, source_target_pairs={{0,2},{1,3},{2,0},{3,1},{4,6},{5,7},{6,4},{7,5},{8,10},{9,11},{10,... | collective-permute-start | bytes 983048 | tf_op jit(solution)/shard_map/ppermute | solution.py:26
  182.3 20.6 %collective-permute-start.32 = (bf16[2,80,1024]{2,1,0:T(8,128)(2,1)S(1)}, bf16[2,80,1024]{2,1,0:T(8,128)(2,1)S(1)}, u32[]{:S(2)}, u32[]{:S(2)}) collective-permute-start(bf16[2,80,1024]{2,1,0:T(8,128)(2,1)S(1)} %fusion.32), channel_id=1, source_target_pairs={{0,1},{1,2},{2,3},{3,0},{4,5},{5,6},{6,7},{7,4},{8,9},{9,10},{10,1... | collective-permute-start | bytes 983048 | tf_op jit(solution)/shard_map/ppermute | solution.py:26
  206.5 19.9 %collective-permute-start.40 = (bf16[128,1024]{1,0:T(8,128)(2,1)S(1)}, bf16[128,1024]{1,0:T(8,128)(2,1)S(1)}, u32[]{:S(2)}, u32[]{:S(2)}) collective-permute-start(bf16[128,1024]{1,0:T(8,128)(2,1)S(1)} %get-tuple-element.133), channel_id=1, source_target_pairs={{0,27},{1,24},{2,25},{3,26},{4,31},{5,28},{6,29},{7,30},{8,3},{9,0... | collective-permute-start | bytes 786440 | tf_op jit(solution)/shard_map/ppermute | solution.py:26
  208.7 36.2 %collective-permute-start.39 = (bf16[128,1024]{1,0:T(8,128)(2,1)S(1)}, bf16[128,1024]{1,0:T(8,128)(2,1)S(1)}, u32[]{:S(2)}, u32[]{:S(2)}) collective-permute-start(bf16[128,1024]{1,0:T(8,128)(2,1)S(1)} %get-tuple-element.134), channel_id=1, source_target_pairs={{0,25},{1,26},{2,27},{3,24},{4,29},{5,30},{6,31},{7,28},{8,1},{9,2... | collective-permute-start | bytes 786440 | tf_op jit(solution)/shard_map/ppermute | solution.py:26
  212.6 36.0 %collective-permute-start.38 = (bf16[128,1024]{1,0:T(8,128)(2,1)S(1)}, bf16[128,1024]{1,0:T(8,128)(2,1)S(1)}, u32[]{:S(2)}, u32[]{:S(2)}) collective-permute-start(bf16[128,1024]{1,0:T(8,128)(2,1)S(1)} %get-tuple-element.135), channel_id=1, source_target_pairs={{0,26},{1,27},{2,24},{3,25},{4,30},{5,31},{6,28},{7,29},{8,2},{9,3... | collective-permute-start | bytes 786440 | tf_op jit(solution)/shard_map/ppermute | solution.py:26
  219.4 31.7 %collective-permute-start.37 = (bf16[128,1024]{1,0:T(8,128)(2,1)S(1)}, bf16[128,1024]{1,0:T(8,128)(2,1)S(1)}, u32[]{:S(2)}, u32[]{:S(2)}) collective-permute-start(bf16[128,1024]{1,0:T(8,128)(2,1)S(1)} %get-tuple-element.124), channel_id=1, source_target_pairs={{0,8},{1,9},{2,10},{3,11},{4,12},{5,13},{6,14},{7,15},{8,16},{9,17... | collective-permute-start | bytes 786440 | tf_op jit(solution)/shard_map/ppermute | solution.py:26
  219.5 33.2 %collective-permute-start.34 = (bf16[128,1024]{1,0:T(8,128)(2,1)S(1)}, bf16[128,1024]{1,0:T(8,128)(2,1)S(1)}, u32[]{:S(2)}, u32[]{:S(2)}) collective-permute-start(bf16[128,1024]{1,0:T(8,128)(2,1)S(1)} %get-tuple-element.125), channel_id=1, source_target_pairs={{0,10},{1,11},{2,8},{3,9},{4,14},{5,15},{6,12},{7,13},{8,18},{9,19... | collective-permute-start | bytes 786440 | tf_op jit(solution)/shard_map/ppermute | solution.py:26
  226.3 26.4 %collective-permute-start.35 = (bf16[128,1024]{1,0:T(8,128)(2,1)S(1)}, bf16[128,1024]{1,0:T(8,128)(2,1)S(1)}, u32[]{:S(2)}, u32[]{:S(2)}) collective-permute-start(bf16[128,1024]{1,0:T(8,128)(2,1)S(1)} %get-tuple-element.126), channel_id=1, source_target_pairs={{0,9},{1,10},{2,11},{3,8},{4,13},{5,14},{6,15},{7,12},{8,17},{9,18... | collective-permute-start | bytes 786440 | tf_op jit(solution)/shard_map/ppermute | solution.py:26
  (31 other events, 303.1 us)
